TPU v7x, 32 devices: a whole 2x2x4 slice. The times are simulated.
32 devices in a mesh: dp: 2 (over core), seq: 16 (over z, y, x).
Axes of the slice: x: 2, y: 2, z: 4, core: 2. Of those that a mesh axis runs over, the one named last changes fastest.
Arguments:
- long_tokens: bfloat16 [2, 2, 1024, 256], P(None, 'dp', 'seq'), may hold values from -6 to 6
- short_tokens: bfloat16 [2, 32, 128, 256], P(None, ('dp', 'seq')), may hold values from -6 to 6
- long_cotangent: bfloat16 [2, 2, 1024, 256], P(None, 'dp', 'seq'), may hold values from -6 to 6
- short_cotangent: bfloat16 [2, 32, 128, 256], P(None, ('dp', 'seq')), may hold values from -6 to 6
- long_mask: int32 [2, 2, 1024], P(None, 'dp', 'seq'), may hold values 0 or 1
- short_mask: int32 [2, 32, 128], P(None, ('dp', 'seq')), may hold values 0 or 1
- complement: int32 [256], replicated, may hold values from 0 to 255, as said below
- norm_gain: float32 [256], P(('dp', 'seq')), may hold values from 0.5 to 1.5
- in_weight: bfloat16 [256, 1024], P(None, ('dp', 'seq')), may hold values from -0.375 to 0.375
- conv_weight: float32 [4, 512], P(None, ('dp', 'seq')), may hold values from -3 to 3
- conv_bias: float32 [512], P(('dp', 'seq')), may hold values from -0.5 to 0.5
- x_weight: bfloat16 [512, 48], P(('dp', 'seq')), may hold values from -0.25 to 0.25
- dt_weight: bfloat16 [16, 512], P(None, ('dp', 'seq')), may hold values from -1.5 to 1.5
- dt_bias: float32 [512], P(('dp', 'seq')), may hold values from -6 to -2
- a_log: float32 [512, 16], P(('dp', 'seq')), may hold values from -9 to 0.5
- d_skip: float32 [512], P(('dp', 'seq')), may hold values from 0.5 to 1.5
- out_weight: bfloat16 [512, 256], P(('dp', 'seq')), may hold values from -0.75 to 0.75
Outputs:
- long_out: bfloat16 [2, 2, 1024, 256], P(None, 'dp', 'seq')
- short_out: bfloat16 [2, 32, 128, 256], P(None, ('dp', 'seq'))
- long_input_grad: float32 [2, 2, 1024, 256], P(None, 'dp', 'seq')
- short_input_grad: float32 [2, 32, 128, 256], P(None, ('dp', 'seq'))
- grad_gain: float32 [256], P(('dp', 'seq'))
- grad_in: float32 [256, 1024], P(None, ('dp', 'seq'))
- grad_conv_w: float32 [4, 512], P(None, ('dp', 'seq'))
- grad_conv_b: float32 [512], P(('dp', 'seq'))
- grad_x: float32 [512, 48], P(('dp', 'seq'))
- grad_dt: float32 [16, 512], P(None, ('dp', 'seq'))
- grad_dt_b: float32 [512], P(('dp', 'seq'))
- grad_a_log: float32 [512, 16], P(('dp', 'seq'))
- grad_skip: float32 [512], P(('dp', 'seq'))
- grad_out: float32 [512, 256], P(('dp', 'seq'))
Inputs may be any that keep to these rules, and one draw needn't show every extreme that they name: complement pairs the channels: complement[complement[c]] = c and complement[c] != c.
All inputs are finite; a program needn't handle non-finite values. No bound on the sum of `long_mask` or of `short_mask` on one device may be relied on, other than what follows from the above.
Results may differ from a plain program's by a relative error of at most 0.0077.
Values may be sent and summed in bfloat16 or wider, within the bound.
No kernel may reach another device: no remote copies, remote signals or barrier semaphores. Data moves between devices by JAX's collectives and lax.ppermute only.
A program may use at most 384 MiB of HBM per device.

v0:
```python
import functools
import types

import jax
import jax.numpy as jnp
from jax import lax
from jax.experimental import pallas as pl
from jax.experimental.pallas import tpu as pltpu
from jax.sharding import PartitionSpec as P

EPS = 1e-05
D, E, N, MB, HALO = 256, 512, 16, 2, 16
LT = 128
NP = N // 2
LOG2E = 1.4426950408889634
LN2 = 0.6931471805599453
F32, BF = jnp.float32, jnp.bfloat16
NT = (((1,), (1,)), ((), ()))
TN = (((0,), (0,)), ((), ()))
BOTH = ("dp", "seq")
IN_ROWS, OUT_ROWS, CH_ROWS = 32, 16, 16
PACK = 2 * IN_ROWS + 2 * OUT_ROWS + CH_ROWS
AT_DT, AT_A, AT_SMALL = 48, 64, 96


def mm(a, b, dims=None):
    if dims is None:
        return jnp.dot(a, b, preferred_element_type=F32)
    return lax.dot_general(a, b, dims, preferred_element_type=F32)


def iota(shape, axis):
    return lax.broadcasted_iota(jnp.int32, shape, axis)


def onehot(cond):
    return jnp.where(cond, 1.0, 0.0).astype(BF)


def eye(n):
    return onehot(iota((n, n), 0) == iota((n, n), 1))


def split(x):
    hi = x.astype(BF)
    return hi, (x - hi.astype(F32)).astype(BF)


def sigmoid(x):
    return 1.0 / (1.0 + jnp.exp(-x))


def loop(count, body):
    lax.fori_loop(0, count, lambda i, c: (body(i), c)[1], 0)


def run(name, body, ins, outs, scratch=None, flops=0, far=()):
    scratch = scratch or {}
    in_names, out_names, scratch_names = list(ins), list(outs), list(scratch)

    def kernel(*refs):
        body(types.SimpleNamespace(**dict(zip(in_names + out_names + scratch_names, refs))))

    def spec(key):
        if key == "place":
            return pl.BlockSpec(memory_space=pltpu.SMEM)
        return pl.BlockSpec(memory_space=pl.ANY if key in far else pltpu.VMEM)

    result = pl.pallas_call(
        kernel,
        out_shape=tuple(jax.ShapeDtypeStruct(*outs[k]) for k in out_names),
        in_specs=[spec(k) for k in in_names],
        out_specs=tuple(pl.BlockSpec(memory_space=pltpu.VMEM) for _ in out_names),
        scratch_shapes=[
            pltpu.VMEM(*scratch[k]) if isinstance(scratch[k], tuple) else scratch[k]
            for k in scratch_names
        ],
        compiler_params=pltpu.CompilerParams(vmem_limit_bytes=60 * 1024 * 1024),
        cost_estimate=pl.CostEstimate(flops=flops, bytes_accessed=1 << 20, transcendentals=0),
        name=name,
    )(*[ins[k] for k in in_names])
    return dict(zip(out_names, result))


def pack_body(r):
    r.rows[...] = jnp.zeros((8, CH_ROWS), F32)
    r.rows[0:4, :] = r.conv_w[...]
    r.rows[4:5, :] = r.conv_b[...]
    r.rows[5:6, :] = r.dt_b[...]
    r.rows[6:7, :] = r.skip[...]
    r.rows[7:8, 0 : r.gain.shape[1]] = r.gain[...]
    in_t = mm(eye(IN_ROWS), r.in_w[...], NT).astype(BF)
    small = jnp.concatenate(split(r.rows[...]), 0)
    id16 = eye(CH_ROWS)

    def place(a, at):
        n = a.shape[1]
        return mm(a.astype(BF), onehot(iota((n, LT), 0) + at == iota((n, LT), 1)))

    a_hi, a_lo = split(r.a_log[...])
    chan = (
        place(r.x_w[...], 0)
        + place(mm(id16, r.dt_w[...], NT), AT_DT)
        + place(a_hi, AT_A)
        + place(a_lo, AT_A + N)
        + place(mm(id16, small, NT), AT_SMALL)
    ).astype(BF)
    out_w = r.out_w[...]
    for j in range(r.buf.shape[0] // PACK):
        at = j * PACK
        for half in range(2):
            lanes = slice(half * LT, (half + 1) * LT)
            r.buf[at + half * IN_ROWS : at + (half + 1) * IN_ROWS, :] = in_t[:, lanes]
            low = at + 2 * IN_ROWS + half * OUT_ROWS
            r.buf[low : low + OUT_ROWS, :] = out_w[:, lanes]
        r.buf[at + PACK - CH_ROWS : at + PACK, :] = chan


def unpack(r):
    count = r.mine.shape[0] // PACK
    mine_at = r.place[0]
    for src, d in ((r.mine, mine_at), (r.other, 1 - mine_at)):
        for j in range(count):
            at = j * PACK
            in_at = pl.multiple_of(d * (count * IN_ROWS) + j * IN_ROWS, IN_ROWS)
            out_at = pl.multiple_of(d * (count * OUT_ROWS) + j * OUT_ROWS, OUT_ROWS)
            for half in range(2):
                lanes = slice(half * LT, (half + 1) * LT)
                r.inT[pl.ds(in_at, IN_ROWS), lanes] = src[
                    at + half * IN_ROWS : at + (half + 1) * IN_ROWS, :
                ]
                low = at + 2 * IN_ROWS + half * OUT_ROWS
                r.outw[pl.ds(out_at, OUT_ROWS), lanes] = src[low : low + OUT_ROWS, :]
            r.pe[pl.ds(out_at, CH_ROWS), :] = src[at + PACK - CH_ROWS : at + PACK, :]


def derive(r):
    peT = mm(eye(LT), r.pe[...], NT)
    small = peT[AT_SMALL : AT_SMALL + 8] + peT[AT_SMALL + 8 : AT_SMALL + 16]
    r.rowp[...] = small
    rate = -jnp.exp(peT[AT_A : AT_A + N] + peT[AT_A + N : AT_A + 2 * N])
    r.rate[...] = rate
    for n in range(N):
        r.r2[4 * n : 4 * n + 4, :] = jnp.broadcast_to(rate[n : n + 1] * LOG2E, (4, E))
    dt = peT[AT_DT : AT_DT + N]
    r.dtw2[...] = jnp.concatenate([dt, dt, jnp.zeros((LT - 2 * N, E), F32)], 0).astype(BF)
    r.xwT[...] = jnp.where(iota((LT, E), 0) < 3 * N, peT, 0.0).astype(BF)


def gain_of(r):
    per = E // (D // 8)
    low = mm(eye(LT), r.pe[...], NT)[AT_SMALL : AT_SMALL + 16].astype(BF)
    lane, col = iota((E, D), 0), iota((E, D), 1)
    pick = onehot(((lane // per) == (col // 8)) & ((lane % per) == (col % 8)))
    g = mm(low, pick)
    return g[0:8] + g[8:16]


def placing(T, transposed):
    shape = (2 * MB * T, 2 * MB * T)
    row, col = iota(shape, 1 if transposed else 0), iota(shape, 0 if transposed else 1)
    t, scan = row >> 2, row & 3
    turn = T.bit_length() - 1
    pos, src = col & (T - 1), col >> turn
    want = jnp.where(scan >= 2, T - 1 - t, t)
    return (src == scan) & (pos == want)


def normalise(tok, gain):
    source = tok.astype(F32)
    scale = lax.rsqrt(jnp.mean(source * source, 1, keepdims=True) + EPS)
    return source, scale, source * scale


def swap_of(r):
    return onehot(iota((D, D), 0) == jnp.broadcast_to(r.comp[...], (D, D)))


def prep(r, T, halo):
    R = 4 * T
    gain = r.gain[0:1, :] if r.gain.shape[0] == 1 else r.gain[7:8, :]
    swap = swap_of(r)
    _, _, unit = normalise(r.tok[...], gain)
    normed = (unit * gain).astype(BF)
    put = placing(T, False)
    r.V[HALO:, :] = mm(
        onehot(put), jnp.concatenate([normed, mm(normed, swap).astype(BF)], 0)
    ).astype(BF)
    mrow = jnp.concatenate([r.mask[0:1, :], r.mask[1:2, :]], 1)
    mrow = jnp.concatenate([mrow, mrow], 1)
    cot = r.cot[...]
    r.GR[...] = mm(
        onehot(put & (mrow != 0)), jnp.concatenate([cot, mm(cot, swap).astype(BF)], 0)
    ).astype(BF)
    if halo:
        hn = (normalise(r.edge[...], gain)[2] * gain).astype(BF)
        r.V[0:HALO, :] = (
            mm(onehot(edge_place(False)), hn)
            + mm(onehot(edge_place(True)), mm(hn, swap).astype(BF))
        ).astype(BF)
        r.ip[0:HALO, :] = mm(r.V[0:HALO, :], r.inT[0:E, :], NT)
    else:
        r.V[0:HALO, :] = jnp.zeros((HALO, D), BF)
        r.ip[0:HALO, :] = jnp.zeros((HALO, E), F32)
    for c in range(0, E, 256):
        r.ip[HALO:, c : c + 256] = mm(r.V[HALO:, :], r.inT[c : c + 256, :], NT)
        r.gate[:, c : c + 256] = mm(r.V[HALO:, :], r.inT[E + c : E + c + 256, :], NT)
        r.gm[:, c : c + 256] = mm(r.GR[...], r.outw[c : c + 256, :], NT)
    w = [r.rowp[k : k + 1, :] for k in range(4)]
    conv_b, dt_b = r.rowp[4:5, :], r.rowp[5:6, :]
    B = 32

    def first(i):
        r0 = pl.multiple_of(i * B, B)
        x = r.ip[pl.ds(r0, B + HALO), :]
        total = conv_b
        for k in range(4):
            total = total + w[k] * x[4 + 4 * k : 4 + 4 * k + B]
        r.co[pl.ds(r0, B), :] = total
        inner = total * sigmoid(total)
        r.si[pl.ds(r0, B), :] = inner
        r.il[pl.ds(r0, B), :] = inner.astype(BF)
        g = r.gate[pl.ds(r0, B), :]
        r.gm[pl.ds(r0, B), :] = r.gm[pl.ds(r0, B), :] * (g * sigmoid(g))

    loop(R // B, first)
    sel = mm(r.il[...], r.pe[...])
    r.sel[...] = sel
    lane = iota((R, LT), 1)
    low = jnp.where(lane < N, sel, 0.0)
    hi = low.astype(BF).astype(F32)
    both = (hi + pltpu.roll(low - hi, N, 1)).astype(BF)
    for c in range(0, E, 256):
        r.st[:, c : c + 256] = mm(both, r.dtw2[:, c : c + 256])

    def second(i):
        r0 = pl.multiple_of(i * B, B)
        z = r.st[pl.ds(r0, B), :] + dt_b
        u = jnp.exp(-jnp.abs(z))
        inv = 1.0 / (1.0 + u)
        near = u * (1.0 - u * (0.5 - u * (1.0 / 3.0)))
        st = jnp.maximum(z, 0.0) + jnp.where(u < 0.01, near, jnp.log(1.0 + u))
        r.sz[pl.ds(r0, B), :] = jnp.where(z >= 0, inv, u * inv)
        r.st[pl.ds(r0, B), :] = st
        r.si[pl.ds(r0, B), :] = r.si[pl.ds(r0, B), :] * st

    loop(R // B, second)


def edge_place(rev):
    row, col = iota((HALO, HALO), 0), iota((HALO, HALO), 1)
    j, scan = row >> 2, row & 3
    if rev:
        return (scan >= 2) & (col == 8 + (scan - 2) * 4 + (3 - j))
    return (scan < 2) & (col == scan * 4 + j)


def maps(r, T):
    R = 4 * T
    sel = r.sel[...]
    lane = iota((R, LT), 1)
    kept = jnp.where((lane >= N) & (lane < 3 * N), sel, 0.0)
    hi = kept.astype(BF).astype(F32)
    both = (hi + pltpu.roll(kept - hi, 64, 1)).astype(BF)
    G = 128
    r8, r4 = iota((2 * G, G), 0), iota((2 * G, G), 1)
    twice = onehot(((r8 >> 3) * 4 + (r8 & 3)) == r4)
    own = (iota((2 * G, LT), 1) & 1) == ((iota((2 * G, LT), 0) >> 2) & 1)
    l, c = iota((LT, NP * LT), 0), iota((LT, NP * LT), 1)
    l = l & 63
    spread_in = onehot((l >= N) & (l < 2 * N) & (((l - N) >> 1) == (c >> 7)))
    spread_out = onehot((l >= 2 * N) & (l < 3 * N) & (((l - 2 * N) >> 1) == (c >> 7)))
    for g in range(R // G):
        left = jnp.where(own, mm(twice, both[g * G : (g + 1) * G]), 0.0).astype(BF)
        r.imb[g * 2 * G : (g + 1) * 2 * G, :] = mm(left, spread_in)
        r.omb[g * 2 * G : (g + 1) * 2 * G, :] = mm(left, spread_out)


def dup(x, low):
    turned = pltpu.roll(x, 4, 0)
    return jnp.where(low, x, turned), jnp.where(low, turned, x)


def lanes_of(e):
    return slice(e * LT, (e + 1) * LT)


def scan_forward(r, T, start, full, U=8):
    low = iota((8, LT), 0) < 4
    for e in range(E // LT):
        es = lanes_of(e)
        if start is None:
            first = tuple(jnp.zeros((8, LT), F32) for _ in range(NP))
        else:
            first = tuple(start[8 * k : 8 * k + 8, es] for k in range(NP))
        if full:
            for k in range(NP):
                r.states[0, 8 * k : 8 * k + 8, es] = first[k]

        def body(i, state):
            state = list(state)
            for u in range(U // 2):
                pair = i * (U // 2) + u
                row = pl.multiple_of(pair * 8, 8)
                st = dup(r.st[pl.ds(row, 8), es], low)
                si = dup(r.si[pl.ds(row, 8), es], low)
                ys = []
                for h in range(2):
                    t = pair * 2 + h
                    r8 = pl.multiple_of(t * 8, 8)
                    acc = None
                    for k in range(NP):
                        decay = jnp.exp2(st[h] * r.r2[8 * k : 8 * k + 8, es])
                        state[k] = decay * state[k] + si[h] * r.imb[pl.ds(r8, 8), lanes_of(k)]
                        if full:
                            r.states[t + 1, 8 * k : 8 * k + 8, es] = state[k]
                            y = state[k] * r.omb[pl.ds(r8, 8), lanes_of(k)]
                            acc = y if acc is None else acc + y
                    if full:
                        ys.append(acc + pltpu.roll(acc, 4, 0))
                if full:
                    r.mix[pl.ds(row, 8), es] = jnp.where(low, ys[0], ys[1])
            return tuple(state)

        last = lax.fori_loop(0, T // U, body, first)
        if not full:
            for k in range(NP):
                r.ends[8 * k : 8 * k + 8, es] = last[k]


def scan_adjoint_local(r, T, U=8):
    low = iota((8, LT), 0) < 4
    for e in range(E // LT):
        es = lanes_of(e)

        def body(i, b):
            b = list(b)
            for u in range(U // 2):
                pair = T // 2 - 1 - (i * (U // 2) + u)
                row = pl.multiple_of(pair * 8, 8)
                st = dup(r.st[pl.ds(row, 8), es], low)
                gm = dup(r.gm[pl.ds(row, 8), es], low)
                for h in (1, 0):
                    r8 = pl.multiple_of((pair * 2 + h) * 8, 8)
                    for k in range(NP):
                        a = gm[h] * r.omb[pl.ds(r8, 8), lanes_of(k)] + b[k]
                        b[k] = jnp.exp2(st[h] * r.r2[8 * k : 8 * k + 8, es]) * a
            return tuple(b)

        last = lax.fori_loop(0, T // U, body, tuple(jnp.zeros((8, LT), F32) for _ in range(NP)))
        for k in range(NP):
            r.ends[64 + 8 * k : 64 + 8 * k + 8, es] = last[k]


def scan_backward(r, T, start, U=8):
    low = iota((8, LT), 0) < 4
    rl, rc = iota((NP * LT, LT), 0), iota((NP * LT, LT), 1)
    r.red[...] = onehot((rl >> 7) == (rc >> 1))
    for e in range(E // LT):
        es = lanes_of(e)
        if start is None:
            first = tuple(jnp.zeros((8, LT), F32) for _ in range(NP))
        else:
            first = tuple(start[64 + 8 * k : 64 + 8 * k + 8, es] for k in range(NP))

        def body(i, carry):
            b, acc = list(carry[0]), list(carry[1])
            base = T // U - 1 - i
            xi = [[None] * U for _ in range(NP)]
            xo = [[None] * U for _ in range(NP)]
            for u in range(U // 2 - 1, -1, -1):
                pair = base * (U // 2) + u
                row = pl.multiple_of(pair * 8, 8)
                st = dup(r.st[pl.ds(row, 8), es], low)
                si = dup(r.si[pl.ds(row, 8), es], low)
                gm = dup(r.gm[pl.ds(row, 8), es], low)
                qs, ps = [None, None], [None, None]
                for h in (1, 0):
                    t = pair * 2 + h
                    r8 = pl.multiple_of(t * 8, 8)
                    q = p = None
                    for k in range(NP):
                        rk = r.r2[8 * k : 8 * k + 8, es]
                        a = gm[h] * r.omb[pl.ds(r8, 8), lanes_of(k)] + b[k]
                        b[k] = jnp.exp2(st[h] * rk) * a
                        w = b[k] * r.states[t, 8 * k : 8 * k + 8, es]
                        q = w * rk if q is None else q + w * rk
                        acc[k] = acc[k] + w * st[h]
                        ai = a * r.imb[pl.ds(r8, 8), lanes_of(k)]
                        p = ai if p is None else p + ai
                        xi[k][2 * u + h] = a * si[h]
                        xo[k][2 * u + h] = r.states[t + 1, 8 * k : 8 * k + 8, es] * gm[h]
                    qs[h] = q + pltpu.roll(q, 4, 0)
                    ps[h] = p + pltpu.roll(p, 4, 0)
                r.q[pl.ds(row, 8), es] = jnp.where(low, qs[0], qs[1])
                r.p[pl.ds(row, 8), es] = jnp.where(low, ps[0], ps[1])
            y = None
            for k in range(0, NP, 2):
                left = jnp.concatenate(
                    [jnp.concatenate(xi[j] + xo[j], 0).astype(BF) for j in (k, k + 1)], 1
                )
                part = mm(left, r.red[k * LT : (k + 2) * LT, :])
                y = part if y is None else y + part
            at = pl.multiple_of(base * U * 8, U * 8)
            if e == 0:
                r.yi[pl.ds(at, U * 8), :] = y[: U * 8]
                r.yo[pl.ds(at, U * 8), :] = y[U * 8 :]
            else:
                r.yi[pl.ds(at, U * 8), :] += y[: U * 8]
                r.yo[pl.ds(at, U * 8), :] += y[U * 8 :]
            return tuple(b), tuple(acc)

        zero = tuple(jnp.zeros((8, LT), F32) for _ in range(NP))
        _, acc = lax.fori_loop(0, T // U, body, (first, zero))
        for k in range(NP):
            r.alog[8 * k : 8 * k + 8, es] = acc[k]
    G = 256
    own = (iota((G, LT), 1) & 1) == ((iota((G, LT), 0) >> 2) & 1)
    valid = own & (iota((G, LT), 1) < N)
    r8, r4 = iota((G // 2, G), 1), iota((G // 2, G), 0)
    fold = onehot(((r8 >> 3) * 4 + (r8 & 3)) == r4)
    for g in range(8 * T // G):
        at = slice(g * G, (g + 1) * G)
        y = pltpu.roll(jnp.where(valid, r.yi[at, :], 0.0), N, 1) + pltpu.roll(
            jnp.where(valid, r.yo[at, :], 0.0), 2 * N, 1
        )
        hi, lo = split(y)
        r.gsel[g * G // 2 : (g + 1) * G // 2, :] = mm(fold, hi) + mm(fold, lo)


def scan_scratch(T):
    return dict(
        states=((T + 1, 8 * NP, E), F32),
        imb=((8 * T, NP * LT), F32),
        omb=((8 * T, NP * LT), F32),
        red=((NP * LT, LT), BF),
        yi=((8 * T, LT), F32),
        yo=((8 * T, LT), F32),
        mix=((4 * T, E), F32),
        q=((4 * T, E), F32),
        p=((4 * T, E), F32),
        alog=((8 * NP, E), F32),
        gsel=((4 * T, LT), F32),
    )


def post(r, T, halo):
    R = 4 * T
    B = 32
    w = [r.rowp[k : k + 1, :] for k in range(4)]
    skip = r.rowp[6:7, :]
    gain = r.gain[0:1, :] if r.gain.shape[0] == 1 else r.gain[7:8, :]
    r.acc[...] = jnp.zeros((64, E), F32)
    for c in range(0, E, 256):
        r.gg[:, c : c + 256] = mm(r.GR[...], r.outw[c : c + 256, :], NT)

    def fold8(x):
        total = x[0:8]
        for j in range(8, x.shape[0], 8):
            total = total + x[j : j + 8]
        return total

    def first(i):
        r0 = pl.multiple_of(i * B, B)
        at = pl.ds(r0, B)
        co, gate, st, gm, p = r.co[at, :], r.gate[at, :], r.st[at, :], r.gm[at, :], r.p[at, :]
        sg = sigmoid(co)
        inner = co * sg
        r.il[at, :] = inner.astype(BF)
        mixed = r.mix[at, :] + skip * inner
        gs = sigmoid(gate)
        silu_gate = gate * gs
        r.gated[at, :] = (mixed * silu_gate).astype(BF)
        r.gp[pl.ds(HALO + r0, B), E:] = (r.gg[at, :] * mixed * (gs + silu_gate * (1.0 - gs))).astype(
            BF
        )
        gz = (r.q[at, :] * LN2 + inner * p) * r.sz[at, :]
        r.gz[at, :] = gz.astype(BF)
        r.acc[40:48, :] += fold8(gz)
        r.acc[48:56, :] += fold8(gm * inner)
        r.gg[at, :] = st * p + gm * skip
        r.slope[at, :] = sg + inner * (1.0 - sg)

    loop(R // B, first)
    lane = iota((R, LT), 1)
    gs_low = jnp.where(lane < N, mm(r.gz[...], r.dtw2[...], NT), r.gsel[...])
    gs_low = jnp.where(lane < 3 * N, gs_low, 0.0)
    r.z[...] = (
        gs_low
        + jnp.where((lane >= AT_DT) & (lane < AT_DT + N), pltpu.roll(r.sel[...], AT_DT, 1), 0.0)
    ).astype(BF)
    gsb = gs_low.astype(BF)
    for c in range(0, E, 256):
        r.mix[:, c : c + 256] = mm(gsb, r.xwT[:, c : c + 256])
    r.gco[0:HALO, :] = jnp.zeros((HALO, E), F32)
    r.gco[HALO + R :, :] = jnp.zeros((HALO, E), F32)

    def second(i):
        r0 = pl.multiple_of(i * B, B)
        at = pl.ds(r0, B)
        gco = (r.gg[at, :] + r.mix[at, :]) * r.slope[at, :]
        r.gco[pl.ds(HALO + r0, B), :] = gco
        x = r.ip[pl.ds(r0, B + HALO), :]
        for k in range(4):
            r.acc[8 * k : 8 * k + 8, :] += fold8(gco * x[4 + 4 * k : 4 + 4 * k + B])
        r.acc[32:40, :] += fold8(gco)

    loop(R // B, second)

    def third(i):
        r0 = pl.multiple_of(i * 16, 16)
        x = r.gco[pl.ds(r0, 32), :]
        total = w[3] * x[0:16]
        for k in range(3):
            total = total + w[k] * x[4 * (3 - k) : 4 * (3 - k) + 16]
        r.gp[pl.ds(r0, 16), :E] = total.astype(BF)

    loop((HALO + R) // 16, third)
    r.gp[0:HALO, E:] = jnp.zeros((HALO, E), BF)
    if not halo:
        r.gp[0:HALO, :E] = jnp.zeros((HALO, E), BF)

    zT = mm(eye(LT), r.z[...], NT).astype(BF)
    row = iota((LT, E), 0)
    peT = jnp.where(row < AT_DT, mm(zT, r.il[...]), 0.0)
    peT = peT + jnp.where((row >= AT_DT) & (row < AT_A), mm(zT, r.gz[...]), 0.0)
    rr, cc = iota((LT, 64), 0), iota((LT, 64), 1)
    hi, lo = split(r.alog[...])
    fold = onehot((rr >= AT_A) & (rr - AT_A == (cc >> 2)))
    rate = jnp.concatenate(
        [jnp.zeros((AT_A, E), F32), r.rate[...], jnp.zeros((LT - AT_A - N, E), F32)], 0
    )
    peT = peT + (mm(fold, hi) + mm(fold, lo)) * rate
    rr, cc = iota((LT, 64), 0), iota((LT, 64), 1)
    hi, lo = split(r.acc[...])
    fold = onehot((rr >= AT_SMALL) & (rr - AT_SMALL == (cc >> 3)))
    peT = peT + mm(fold, hi) + mm(fold, lo)
    r.g_out[...] = mm(r.gated[...], r.GR[...], TN)
    for c in range(0, 2 * E, 256):
        r.g_inT[c : c + 256, :] = mm(r.gp[:, c : c + 256], r.V[...], TN)

    swap = swap_of(r)
    back = onehot(placing(T, True))
    half = MB * T
    gated = mm(back, r.gated[...]).astype(BF)
    source, scale, unit = normalise(r.tok[...], gain)
    outs = mm(r.outw[...], swap).astype(BF)
    result = source + mm(gated[:half], r.outw[...]) + mm(gated[half:], outs)
    r.out[...] = result.astype(BF)
    grad = jnp.zeros((half, D), F32)
    for c in range(0, 2 * E, 256):
        g = mm(back, r.gp[HALO:, c : c + 256]).astype(BF)
        win = r.inT[c : c + 256, :]
        grad = grad + mm(g[:half], win) + mm(g[half:], mm(win, swap).astype(BF))
    gain_term = jnp.sum(grad * unit, 0, keepdims=True)
    g = grad * gain
    mrow = jnp.concatenate([r.mask[0:1, :], r.mask[1:2, :]], 1)
    keep = onehot((iota((half, half), 0) == iota((half, half), 1)) & (mrow != 0))
    r.ing[...] = scale * (g - unit * jnp.mean(g * unit, 1, keepdims=True)) + mm(keep, r.cot[...])
    if halo:
        rows = mm(r.gp[0:HALO, :E], r.inT[0:E, :])
        hi, lo = split(rows)
        rows = jnp.where(
            (iota((HALO, D), 0) & 3) < 2, rows, mm(hi, swap) + mm(lo, swap)
        )
        put = onehot(edge_place(False) | edge_place(True))
        tok = mm(put, r.edge[...])
        _, scale, unit = normalise(tok, gain)
        gain_term = gain_term + jnp.sum(rows * unit, 0, keepdims=True)
        g = rows * gain
        r.delta[...] = scale * (g - unit * jnp.mean(g * unit, 1, keepdims=True))
    r.g_gain[...] = jnp.broadcast_to(gain_term, (8, D))
    r.g_peT[...] = peT


def post_scratch(T):
    R = 4 * T
    return dict(
        acc=((64, E), F32),
        gg=((R, E), F32),
        slope=((R, E), F32),
        gco=((R + 2 * HALO, E), F32),
        il=((R, E), BF),
        gated=((R, E), BF),
        gz=((R, E), BF),
        z=((R, LT), BF),
        gp=((R + HALO, 2 * E), BF),
    )


def post_outs(T):
    return dict(
        out=((MB * T, D), BF),
        ing=((MB * T, D), F32),
        g_inT=((2 * E, D), F32),
        g_out=((E, D), F32),
        g_peT=((LT, E), F32),
        g_gain=((8, D), F32),
    )


def combine_body(r, radix, stride, first, last):
    digit = (r.place[1] // stride) % radix
    for m in range(radix):
        src = r.own if m == 0 else getattr(r, f"recv{m}")
        r.mem[m, 0:128, :] = src[0:128, :].astype(F32)
        both = src[128:144, :].astype(F32)
        r.mem[m, 128:136, :] = both[0:8] + both[8:16]
    fwd = (iota((8, LT), 0) & 3) < 2
    for half in range(2):
        asc = fwd if half == 0 else jnp.logical_not(fwd)
        place = jnp.where(asc, digit, radix - 1 - digit)
        for e in range(E // LT):
            es = lanes_of(e)
            sums = []
            for f in range(radix):
                sums.append(
                    jnp.where(
                        asc,
                        r.mem[f ^ digit, 128:136, es],
                        r.mem[(radix - 1 - f) ^ digit, 128:136, es],
                    )
                )
            before = jnp.zeros((8, LT), F32)
            for f in range(radix):
                before = before + jnp.where(f < place, sums[f], 0.0)
            old = None if first else r.spre[8 * half : 8 * half + 8, es]
            if not last:
                r.spre_new[8 * half : 8 * half + 8, es] = before if first else old + before
            for k in range(NP):
                at = slice(64 * half + 8 * k, 64 * half + 8 * k + 8)
                rk = r.r2[8 * k : 8 * k + 8, es]
                total = prefix = jnp.zeros((8, LT), F32)
                for f in range(radix):
                    part = jnp.where(
                        asc, r.mem[f ^ digit, at, es], r.mem[(radix - 1 - f) ^ digit, at, es]
                    )
                    prefix = jnp.where(place == f, total, prefix)
                    total = jnp.exp2(rk * sums[f]) * total + part
                if not first:
                    prefix = jnp.exp2(rk * old) * prefix + r.prefix[at, es]
                r.prefix_new[at, es] = prefix
                if not last:
                    r.tot[at, es] = total
            if not last and half == 0:
                whole = sums[0]
                for f in range(1, radix):
                    whole = whole + sums[f]
                r.tot[128:136, es] = whole
    if not last:
        write_element(r.element, r.tot)


def write_element(out, f32):
    out[0:128, :] = f32[0:128, :].astype(BF)
    hi, lo = split(f32[128:136, :])
    out[128:144, :] = jnp.concatenate([hi.astype(F32), lo.astype(F32)], 0).astype(BF)


def stages(count):
    stride, result = 1, []
    while stride < count:
        radix = 4 if (count // stride) % 4 == 0 else 2
        result.append((stride, radix))
        stride *= radix
    return result


ELEMENT = ((144, E), BF)


def carry_send(element, count, stage):
    stride, radix = stage
    return [
        lax.ppermute(element, "seq", [(i, i ^ (m * stride)) for i in range(count)])
        for m in range(1, radix)
    ]


def combine(place, element, received, r2, before, stage, first, last):
    stride, radix = stage
    ins = dict(place=place, own=element, r2=r2)
    for m in range(1, radix):
        ins[f"recv{m}"] = received[m - 1]
    if not first:
        ins.update(prefix=before["prefix_new"], spre=before["spre_new"])
    outs = dict(prefix_new=((128, E), F32))
    if not last:
        outs.update(spre_new=((16, E), F32), element=ELEMENT)
    scratch = dict(mem=((radix, 136, E), F32))
    if not last:
        scratch["tot"] = ((136, E), F32)
    return run(
        f"combine{stride}",
        functools.partial(
            combine_body, radix=radix, stride=stride, first=first, last=last
        ),
        ins,
        outs,
        scratch,
    )


def long_start_body(r, T, packed):
    if packed:
        unpack(r)
        r.gain[...] = gain_of(r)
    derive(r)
    prep(r, T, True)
    maps(r, T)
    scan_forward(r, T, None, False)
    scan_adjoint_local(r, T)

    def add(i, total):
        return total + r.st[pl.ds(pl.multiple_of(i * 8, 8), 8), :]

    total = lax.fori_loop(0, T // 2, add, jnp.zeros((8, E), F32))
    r.ends[128:136, :] = total + pltpu.roll(total, 4, 0)
    write_element(r.element, r.ends)


def short_start_body(r, T):
    prep(r, T, False)


def fetch_start(r, names):
    copies = []
    for i, name in enumerate(names):
        copy = pltpu.make_async_copy(getattr(r, name + "_far"), getattr(r, name), r.sems.at[i])
        copy.start()
        copies.append(copy)
    return copies


LATE = ("ip", "gate", "co", "sz", "V", "GR", "tok", "cot", "inT", "outw", "xwT", "dtw2")


def windows_body(r, T, halo, names):
    copies = fetch_start(r, names)
    maps(r, T)
    start = r.carry if halo else None
    scan_forward(r, T, start, True)
    scan_backward(r, T, start)
    for copy in copies:
        copy.wait()
    post(r, T, halo)
    if halo:
        finish_grads(r)


def finish_grads(r):
    g_inT, g_out = r.g_inT, r.g_out
    g_inT[...] += r.s_inT[...]
    g_out[...] += r.s_out[...]
    r.g_peT[...] += r.s_peT[...]
    r.g_gain[...] += r.s_gain[...]
    if not hasattr(r, "keep"):
        return
    lane, col = iota((D, E), 1), iota((D, E), 0)
    pick = onehot(((lane // 16) == (col // 8)) & ((lane % 16) == (col % 8)))
    peT = r.g_peT[...] + jnp.where(
        iota((LT, E), 0) == AT_SMALL + 7, mm(r.g_gain[0:1, :].astype(BF), pick), 0.0
    )
    r.pe_out[...] = peT.T.astype(BF)
    count = r.keep.shape[0] // PACK
    mine = r.place[0]
    for dst, d in ((r.keep, mine), (r.give, 1 - mine)):
        for j in range(count):
            at = j * PACK
            in_at = pl.multiple_of(d * (count * IN_ROWS) + j * IN_ROWS, IN_ROWS)
            out_at = pl.multiple_of(d * (count * OUT_ROWS) + j * OUT_ROWS, OUT_ROWS)
            for half in range(2):
                lanes = slice(half * LT, (half + 1) * LT)
                dst[at + half * IN_ROWS : at + (half + 1) * IN_ROWS, :] = g_inT[
                    pl.ds(in_at, IN_ROWS), lanes
                ].astype(BF)
                low = at + 2 * IN_ROWS + half * OUT_ROWS
                dst[low : low + OUT_ROWS, :] = g_out[pl.ds(out_at, OUT_ROWS), lanes].astype(BF)
            dst[at + PACK - CH_ROWS : at + PACK, :] = r.pe_out[pl.ds(out_at, CH_ROWS), :]


def final_body(r, packed):
    r.grad[...] = r.ing[...]
    T = r.grad.shape[0] // MB
    for mb in range(MB):
        for j in range(4):
            row = mb * T + T - 4 + j
            r.grad[row : row + 1, :] += r.from_next[4 * j + mb : 4 * j + mb + 1, :]
            row = mb * T + 3 - j
            r.grad[row : row + 1, :] += r.from_prev[4 * j + 2 + mb : 4 * j + 3 + mb, :]
    if not packed:
        return
    count = r.parts.shape[0] // PACK
    total = r.parts[0:PACK, :].astype(F32)
    for j in range(1, count):
        total = total + r.parts[j * PACK : (j + 1) * PACK, :].astype(F32)
    for half in range(2):
        lanes = slice(half * LT, (half + 1) * LT)
        hi, lo = split(total[half * IN_ROWS : (half + 1) * IN_ROWS])
        r.in_w[lanes, :] = mm(eye(LT), hi, NT) + mm(eye(LT), lo, NT)
        low = 2 * IN_ROWS + half * OUT_ROWS
        r.out_w[:, lanes] = total[low : low + OUT_ROWS]
    pe = total[PACK - CH_ROWS :]
    hi, lo = split(pe)
    peT = mm(eye(LT), hi, NT) + mm(eye(LT), lo, NT)
    r.x_w[...] = pe[:, : 3 * N]
    r.a_log[...] = pe[:, AT_A : AT_A + N]
    r.dt_w[...] = peT[AT_DT : AT_DT + N]
    small = peT[AT_SMALL : AT_SMALL + 8]
    r.conv_w[...] = small[0:4]
    r.conv_b[...] = small[4:5]
    r.dt_b[...] = small[5:6]
    r.skip[...] = small[6:7]
    r.gain[...] = small[7:8, 0 : r.gain.shape[1]]


PREP_OUTS = ("V", "GR", "ip", "gate", "co", "st", "sz", "si", "gm", "sel")


def prep_outs(T):
    R = 4 * T
    wide = ((R, E), F32)
    return dict(
        V=((R + HALO, D), BF),
        GR=((R, D), BF),
        ip=((R + HALO, E), F32),
        gate=wide,
        co=wide,
        st=wide,
        sz=wide,
        si=wide,
        gm=wide,
        sel=((R, LT), F32),
    )


def local(
    long_tokens,
    short_tokens,
    long_cotangent,
    short_cotangent,
    long_mask,
    short_mask,
    complement,
    norm_gain,
    in_weight,
    conv_weight,
    conv_bias,
    x_weight,
    dt_weight,
    dt_bias,
    a_log,
    d_skip,
    out_weight,
):
    count = lax.axis_size("seq")
    span, short = long_tokens.shape[2], short_tokens.shape[2]
    packed = out_weight.shape[0] == OUT_ROWS and in_weight.shape[1] == IN_ROWS
    place = jnp.stack([lax.axis_index("dp"), lax.axis_index("seq")]).astype(jnp.int32)
    comp = complement.reshape(1, D)
    up = [(i, i + 1) for i in range(count - 1)]
    down = [(i + 1, i) for i in range(count - 1)]

    tail = lax.ppermute(long_tokens[:, 0, span - 4 :, :].reshape(8, D), "seq", up)
    head = lax.ppermute(long_tokens[:, 0, :4, :].reshape(8, D), "seq", down)
    edge = jnp.concatenate([tail, head], 0)
    if packed:
        buf = run(
            "pack",
            pack_body,
            dict(
                gain=norm_gain.reshape(1, -1),
                in_w=in_weight,
                conv_w=conv_weight,
                conv_b=conv_bias.reshape(1, -1),
                x_w=x_weight,
                dt_w=dt_weight,
                dt_b=dt_bias.reshape(1, -1),
                a_log=a_log,
                skip=d_skip.reshape(1, -1),
                out_w=out_weight,
            ),
            dict(buf=((count * PACK, LT), BF)),
            dict(rows=((8, CH_ROWS), F32)),
        )["buf"]
        mine = lax.all_to_all(buf, "seq", 0, 0, tiled=True)
        other = lax.ppermute(mine, "dp", [(0, 1), (1, 0)])
        weights_in = dict(mine=mine, other=other)
    else:

        def whole(a, axis):
            return lax.all_gather(a, BOTH, axis=axis, tiled=True)

        small = jnp.stack([*conv_weight, conv_bias, dt_bias, d_skip, jnp.zeros_like(d_skip)])
        columns = jnp.concatenate([a_log, small.T], 1)
        hi = columns.astype(BF)
        lo = (columns - hi.astype(F32)).astype(BF)
        zero = jnp.zeros((columns.shape[0], LT - AT_SMALL - 16), BF)
        chan = jnp.concatenate(
            [x_weight, dt_weight.T, hi[:, :N], lo[:, :N], hi[:, N:], lo[:, N:], zero], 1
        )
        weights_in = dict(
            inT=whole(in_weight.T, 0),
            outw=whole(out_weight, 0),
            pe=whole(chan, 0),
            gain=whole(norm_gain, 0).reshape(1, D),
        )

    def tokens_of(tok, cot, mask):
        T = tok.shape[2]
        return dict(
            tok=tok.reshape(MB * T, D), cot=cot.reshape(MB * T, D), mask=mask.reshape(MB, T)
        )

    long_in = tokens_of(long_tokens, long_cotangent, long_mask)
    short_in = tokens_of(short_tokens, short_cotangent, short_mask)

    derived = dict(
        r2=((8 * NP, E), F32),
        rowp=((8, E), F32),
        rate=((N, E), F32),
        dtw2=((LT, E), BF),
        xwT=((LT, E), BF),
    )
    unpacked = dict(inT=((2 * E, D), BF), outw=((E, D), BF), pe=((E, LT), BF), gain=((8, D), F32))
    started = run(
        "long_start",
        functools.partial(long_start_body, T=span, packed=packed),
        dict(place=place, comp=comp, edge=edge, **long_in, **weights_in),
        dict(
            element=ELEMENT, **prep_outs(span), **derived, **(unpacked if packed else {})
        ),
        dict(
            il=((4 * span, E), BF),
            imb=((8 * span, NP * LT), F32),
            omb=((8 * span, NP * LT), F32),
            ends=((136, E), F32),
        ),
        flops=1 << 33,
    )
    weights = {k: started[k] for k in derived}
    for k in unpacked:
        weights[k] = started[k] if packed else weights_in[k]

    plan = stages(count)
    element, before = started["element"], None
    received = carry_send(element, count, plan[0])
    prepared = run(
        "short_start",
        functools.partial(short_start_body, T=short),
        dict(comp=comp, **short_in, **{k: weights[k] for k in ("inT", "outw", "pe", "gain", "dtw2", "rowp")}),
        prep_outs(short),
        dict(il=((4 * short, E), BF)),
        flops=1 << 33,
    )

    def windows(name, T, halo, prep_out, inputs, extra, outs_more):
        ins = dict(
            comp=comp,
            mask=inputs["mask"],
            **{k: weights[k] for k in ("r2", "rowp", "rate", "gain")},
            **{k: prep_out[k] for k in ("st", "si", "gm", "sel")},
            **extra,
        )
        late = dict(
            {k: prep_out[k] for k in ("ip", "gate", "co", "sz", "V", "GR")},
            tok=inputs["tok"],
            cot=inputs["cot"],
            **{k: weights[k] for k in ("inT", "outw", "xwT", "dtw2")},
        )
        for k in ("s_inT", "s_out", "s_peT", "s_gain"):
            if k in ins:
                late[k] = ins.pop(k)
        ins.update({k + "_far": v for k, v in late.items()})
        names = tuple(late)
        return run(
            name,
            functools.partial(windows_body, T=T, halo=halo, names=names),
            ins,
            dict(post_outs(T), **outs_more),
            dict(
                scan_scratch(T),
                **post_scratch(T),
                **{k: (v.shape, v.dtype) for k, v in late.items()},
                sems=pltpu.SemaphoreType.DMA((len(names),)),
                **(dict(pe_out=((E, LT), BF)) if halo and packed else {}),
            ),
            flops=1 << 35,
            far=tuple(k + "_far" for k in names),
        )

    for at, stage in enumerate(plan[:-1]):
        before = combine(place, element, received, weights["r2"], before, stage, at == 0, False)
        element = before["element"]
        received = carry_send(element, count, plan[at + 1])
    shorts = windows("short_windows", short, False, prepared, short_in, {}, {})
    last = len(plan) - 1
    carry = combine(
        place, element, received, weights["r2"], before, plan[last], last == 0, True
    )["prefix_new"]
    more = dict(delta=((HALO, D), F32))
    if packed:
        more.update(keep=((count * PACK, LT), BF), give=((count * PACK, LT), BF))
    longs = windows(
        "long_windows",
        span,
        True,
        started,
        long_in,
        dict(
            place=place,
            carry=carry,
            edge=edge,
            s_inT=shorts["g_inT"],
            s_out=shorts["g_out"],
            s_peT=shorts["g_peT"],
            s_gain=shorts["g_gain"],
        ),
        more,
    )
    from_next = lax.ppermute(longs["delta"], "seq", down)
    from_prev = lax.ppermute(longs["delta"], "seq", up)
    ins = dict(ing=longs["ing"], from_next=from_next, from_prev=from_prev)
    outs = dict(grad=((MB * span, D), F32))
    if packed:
        got = lax.ppermute(longs["give"], "dp", [(0, 1), (1, 0)])
        ins["parts"] = lax.all_to_all(longs["keep"] + got, "seq", 0, 0, tiled=True)
        outs.update(
            gain=((1, D // (2 * count)), F32),
            in_w=((D, IN_ROWS), F32),
            conv_w=((4, CH_ROWS), F32),
            conv_b=((1, CH_ROWS), F32),
            x_w=((CH_ROWS, 3 * N), F32),
            dt_w=((N, CH_ROWS), F32),
            dt_b=((1, CH_ROWS), F32),
            a_log=((CH_ROWS, N), F32),
            skip=((1, CH_ROWS), F32),
            out_w=((OUT_ROWS, D), F32),
        )
    done = run("final", functools.partial(final_body, packed=packed), ins, outs)
    if packed:
        grads = {k: done[k] for k in outs if k != "grad"}
        for k in ("gain", "conv_b", "dt_b", "skip"):
            grads[k] = grads[k].reshape(-1)
    else:

        def own(a, axis=0):
            return lax.psum_scatter(a, BOTH, scatter_dimension=axis, tiled=True)

        pe = own(longs["g_peT"].T)
        grads = dict(
            gain=own(longs["g_gain"][0]),
            in_w=own(longs["g_inT"]).T,
            conv_w=pe[:, AT_SMALL : AT_SMALL + 4].T,
            conv_b=pe[:, AT_SMALL + 4],
            x_w=pe[:, : 3 * N],
            dt_w=pe[:, AT_DT : AT_DT + N].T,
            dt_b=pe[:, AT_SMALL + 5],
            a_log=pe[:, AT_A : AT_A + N],
            skip=pe[:, AT_SMALL + 6],
            out_w=own(longs["g_out"]),
        )
    order = ("gain", "in_w", "conv_w", "conv_b", "x_w", "dt_w", "dt_b", "a_log", "skip", "out_w")
    return (
        longs["out"].reshape(long_tokens.shape),
        shorts["out"].reshape(short_tokens.shape),
        done["grad"].reshape(long_tokens.shape),
        shorts["ing"].reshape(short_tokens.shape),
    ) + tuple(grads[k] for k in order)


def solution(mesh):
    long_spec, short_spec = P(None, "dp", "seq", None), P(None, BOTH, None, None)
    rows, columns, vector = P(BOTH, None), P(None, BOTH), P(BOTH)
    params = (vector, columns, columns, vector, rows, columns, vector, rows, vector, rows)
    return jax.shard_map(
        local,
        mesh=mesh,
        in_specs=(
            long_spec,
            short_spec,
            long_spec,
            short_spec,
            P(None, "dp", "seq"),
            P(None, BOTH, None),
            P(),
        )
        + params,
        out_specs=(long_spec, short_spec, long_spec, short_spec) + params,
        check_vma=False,
    )
```

profile of v0, /device:TPU:0, one launch (start us, length us, event | category | flops | bytes accessed | tf_op | source)
XLA Modules:
  0.0 157.5 jit_solution(18054403519373809929)
XLA Ops:
  0.6 1.5 copy.31.refs_1_
  2.1 2.0 %pack.1 = bf16[1792,128]{1,0:T(8,128)(2,1)} custom-call(f32[1,8]{1,0:T(1,128)} %bitcast.39, bf16[256,32]{1,0:T(8,128)(2,1)} %copy.31.refs_1_, f32[4,16]{1,0:T(4,128)} %refs_2_.1, f32[1,16]{1,0:T(1,128)} %bitcast.40, bf16[16,48]{1,0:T(8,128)(2,1)} %refs_4_.1, bf16[16,16]{1,0:T(8,128)(2,1)} %refs_5_.1, f32[1,16]{1,0:T(1,128)} %bitcast.41, f32[16,16]{1,0:T(8,128)} %refs_7_.1, ...), custom_call_target="tpu_custom_call" | custom-call | bytes 1048576 | tf_op jit(solution)/shard_map/pack/pallas_call | solution.py:69
  4.1 22.2 %all_to_all.22 = bf16[16,112,128]{2,1,0:T(8,128)(2,1)S(1)} all-to-all(bf16[16,112,128]{2,1,0:T(8,128)(2,1)} %bitcast.34), channel_id=1, replica_groups=mesh['dp'=2,'seq'=16] {'seq'}, dimensions={0} | all-to-all | bytes 917504 | tf_op jit(solution)/shard_map/all_to_all | solution.py:886
  26.3 0.0 copy-start.1
  26.3 0.0 collective-permute-start.2
  26.3 0.8 fusion
  27.1 2.5 %collective-permute-start = (bf16[8,256]{1,0:T(8,128)(2,1)S(1)}, bf16[8,256]{1,0:T(8,128)(2,1)S(1)}, u32[]{:S(2)}, u32[]{:S(2)}) collective-permute-start(bf16[8,256]{1,0:T(8,128)(2,1)S(1)} %reshape_squeeze.6), channel_id=1, source_target_pairs={{0,1},{1,2},{2,3},{3,4},{4,5},{5,6},{6,7},{7,8},{8,9},{9,10},{10,1... | collective-permute-start | bytes 12296 | tf_op jit(solution)/shard_map/ppermute | solution.py:864
  29.5 1.3 collective-permute-start.1
  30.8 0.6 pad_add_fusion.refs_0_.refs_10_
  31.4 0.0 collective-permute-done
  31.4 3.6 %collective-permute-done.1 = bf16[8,256]{1,0:T(8,128)(2,1)S(1)} collective-permute-done((bf16[8,256]{1,0:T(8,128)(2,1)S(1)}, bf16[8,256]{1,0:T(8,128)(2,1)S(1)}, u32[]{:S(2)}, u32[]{:S(2)}) %collective-permute-start.1) | collective-permute-done | bytes 4128 | tf_op jit(solution)/shard_map/ppermute | solution.py:865
  35.0 0.0 copy-start.10
  35.0 0.0 collective-permute-done.2.refs_7_
  35.0 0.0 copy-start.11
  35.1 0.0 copy-done.1
  35.1 0.6 copy-done.10
  35.6 0.2 copy-done.11
  35.8 11.3 %long_start.1 = (bf16[144,512]{1,0:T(8,128)(2,1)}, bf16[272,256]{1,0:T(8,128)(2,1)}, bf16[256,256]{1,0:T(8,128)(2,1)}, f32[272,512]{1,0:T(8,128)}, f32[256,512]{...) custom-call(s32[2]{0:T(128)} %pad_add_fusion.refs_0_.refs_10_, ...), custom_call_target="tpu_custom_call" | custom-call | flops 8589934592 | bytes 1048576 | tf_op jit(solution)/shard_map/long_start/pallas_call | solution.py:69
  47.2 2.7 %collective-permute-start.3 = (bf16[144,512]{1,0:T(8,128)(2,1)}, bf16[144,512]{1,0:T(8,128)(2,1)S(1)}, u32[]{:S(2)}, u32[]{:S(2)}) collective-permute-start(bf16[144,512]{1,0:T(8,128)(2,1)} %get-tuple-element.77.refs_1_), channel_id=1, source_target_pairs={{0,1},{1,0},{2,3},{3,2},{4,5},{5,4},{6,7},{7,6},{8,9},{9,8},{10,11... | collective-permute-start | bytes 442376 | tf_op jit(solution)/shard_map/ppermute | solution.py:675
  49.9 2.7 %collective-permute-start.4 = (bf16[144,512]{1,0:T(8,128)(2,1)}, bf16[144,512]{1,0:T(8,128)(2,1)S(1)}, u32[]{:S(2)}, u32[]{:S(2)}) collective-permute-start(bf16[144,512]{1,0:T(8,128)(2,1)} %get-tuple-element.77.refs_1_), channel_id=1, source_target_pairs={{0,2},{1,3},{2,0},{3,1},{4,6},{5,7},{6,4},{7,5},{8,10},{9,11},{10,... | collective-permute-start | bytes 442376 | tf_op jit(solution)/shard_map/ppermute | solution.py:675
  52.6 0.0 collective-permute-start.5
  52.6 8.8 %short_start.1 = (bf16[528,256]{1,0:T(8,128)(2,1)}, bf16[512,256]{1,0:T(8,128)(2,1)}, f32[528,512]{1,0:T(8,128)}, f32[512,512]{1,0:T(8,128)}, f32[512,512]{1,0:T...) custom-call(s32[1,256]{1,0:T(1,128)} %bitcast.53, ...), custom_call_target="tpu_custom_call" | custom-call | flops 8589934592 | bytes 1048576 | tf_op jit(solution)/shard_map/short_start/pallas_call | solution.py:69
  61.4 0.0 collective-permute-done.3.refs_3_
  61.4 0.0 copy-start.5
  61.4 0.0 collective-permute-done.4.refs_4_
  61.4 0.0 copy-start.6
  61.4 0.0 collective-permute-done.5.refs_5_
  61.4 0.0 copy-start.7
  61.4 0.6 copy-done.5
  62.0 0.1 copy-done.6
  62.1 0.1 copy-done.7
  62.2 2.2 %combine1.1 = (f32[128,512]{1,0:T(8,128)}, f32[16,512]{1,0:T(8,128)}, bf16[144,512]{1,0:T(8,128)(2,1)}) custom-call(s32[2]{0:T(128)} %pad_add_fusion.refs_0_.refs_10_, bf16[144,512]{1,0:T(8,128)(2,1)} %get-tuple-element.77.refs_1_, f32[64,512]{1,0:T(8,128)} %get-tuple-element.69.refs_2_, bf16[144,512]{1,0:T(8,128)(2,1)} %copy-done.5, ...), custom_call_target="tpu_custom_call" | custom-call | bytes 1048576 | tf_op jit(solution)/shard_map/combine1/pallas_call | solution.py:69
  64.4 0.3 collective-permute-start.6
  64.7 1.2 collective-permute-start.7
  65.9 2.9 %collective-permute-start.8 = (bf16[144,512]{1,0:T(8,128)(2,1)}, bf16[144,512]{1,0:T(8,128)(2,1)S(1)}, u32[]{:S(2)}, u32[]{:S(2)}) collective-permute-start(bf16[144,512]{1,0:T(8,128)(2,1)} %get-tuple-element.78.refs_1_), channel_id=1, source_target_pairs={{0,12},{1,13},{2,14},{3,15},{4,8},{5,9},{6,10},{7,11},{8,4},{9,5},... | collective-permute-start | bytes 442376 | tf_op jit(solution)/shard_map/ppermute | solution.py:675
  68.8 37.6 %short_windows.1 = (bf16[256,256]{1,0:T(8,128)(2,1)}, f32[256,256]{1,0:T(8,128)}, f32[1024,256]{1,0:T(8,128)}, f32[512,256]{1,0:T(8,128)}, f32[128,512]{1,0:T(8,128)}, /*index=5*/f32[8,256]{1,0:T(8,128)}) custom-call(s32[1,256]{1,0:T(1,128)} %bitcast.54, s32[2,128]{1,0:T(2,128)} %bitcast.51, f32[64,512]{1,0:T(8,128)} %get-tuple-element.69.refs_2_, ...), custom_call_target="tpu_custom_call" | custom-call | flops 34359738368 | bytes 1048576 | tf_op jit(solution)/shard_map/short_windows/pallas_call | solution.py:69
  106.4 0.0 collective-permute-done.6.refs_3_
  106.4 0.0 copy-start.2
  106.4 0.0 collective-permute-done.7.refs_4_
  106.4 0.0 copy-start.3
  106.4 0.0 collective-permute-done.8.refs_5_
  106.4 0.0 copy-start.4
  106.4 0.6 copy-done.2
  107.1 0.1 copy-done.3
  107.1 0.1 copy-done.4
  107.2 2.2 %combine4.1.refs_11_ = f32[128,512]{1,0:T(8,128)} custom-call(s32[2]{0:T(128)} %pad_add_fusion.refs_0_.refs_10_, bf16[144,512]{1,0:T(8,128)(2,1)} %get-tuple-element.78.refs_1_, f32[64,512]{1,0:T(8,128)} %get-tuple-element.69.refs_2_, bf16[144,512]{1,0:T(8,128)(2,1)} %copy-done.2, bf16[144,512]{1,0:T(8,128)(2,1)} %copy-done.3, bf16[144,512]{1,0:T(8,128)(2,1)} %copy-done.4, ...), custom_call_target="tpu_custom_call" | custom-call | bytes 1048576 | tf_op jit(solution)/shard_map/combine4/pallas_call | solution.py:69
  109.4 21.2 %long_windows.1 = (bf16[128,256]{1,0:T(8,128)(2,1)}, f32[128,256]{1,0:T(8,128)}, f32[1024,256]{1,0:T(8,128)}, f32[512,256]{1,0:T(8,128)}, f32[128,512]{1,0:T(8,1...) custom-call(s32[1,256]{1,0:T(1,128)} %bitcast.55, ...), custom_call_target="tpu_custom_call" | custom-call | flops 34359738368 | bytes 1048576 | tf_op jit(solution)/shard_map/long_windows/pallas_call | solution.py:69
  130.6 0.1 collective-permute-start.11
  130.7 2.0 %collective-permute-done.11 = bf16[1792,128]{1,0:T(8,128)(2,1)S(1)} collective-permute-done((bf16[1792,128]{1,0:T(8,128)(2,1)}, bf16[1792,128]{1,0:T(8,128)(2,1)S(1)}, u32[]{:S(2)}, u32[]{:S(2)}) %collective-permute-start.11) | collective-permute-done | bytes 458784 | tf_op jit(solution)/shard_map/ppermute | solution.py:1026
  132.7 0.0 copy-start.12
  132.7 1.9 %add.3 = bf16[1792,128]{1,0:T(8,128)(2,1)} add(bf16[1792,128]{1,0:T(8,128)(2,1)} %get-tuple-element.110, bf16[1792,128]{1,0:T(8,128)(2,1)S(1)} %collective-permute-done.11) | non-fusion elementwise | flops 229376 | bytes 1376256 | tf_op jit(solution)/shard_map/add | solution.py:1027
  134.6 4.3 %all-to-all-start.1 = ((bf16[16,112,128]{2,1,0:T(8,128)(2,1)}), bf16[16,112,128]{2,1,0:T(8,128)(2,1)S(1)}, u32[]{:S(2)}, u32[]{:S(2)}) async-start(bf16[16,112,128]{2,1,0:T(8,128)(2,1)} %bitcast.19), calls=%async_computation.1 | async-start | bytes 917504 | tf_op jit(solution)/shard_map/all_to_all | solution.py:1027
  138.9 0.0 copy-done.12
  138.9 3.8 %collective-permute-start.10 = (f32[16,256]{1,0:T(8,128)S(1)}, f32[16,256]{1,0:T(8,128)S(1)}, u32[]{:S(2)}, u32[]{:S(2)}) collective-permute-start(f32[16,256]{1,0:T(8,128)S(1)} %copy-done.12), channel_id=1, source_target_pairs={{0,1},{1,2},{2,3},{3,4},{4,5},{5,6},{6,7},{7,8},{8,9},{9,10},{10,1... | collective-permute-start | bytes 49160 | tf_op jit(solution)/shard_map/ppermute | solution.py:1022
  142.7 1.3 collective-permute-start.9
  144.0 0.1 collective-permute-done.10.refs_2_
  144.2 0.0 copy-start.8
  144.2 4.3 %collective-permute-done.9.refs_1_ = f32[16,256]{1,0:T(8,128)S(1)} collective-permute-done((f32[16,256]{1,0:T(8,128)S(1)}, f32[16,256]{1,0:T(8,128)S(1)}, u32[]{:S(2)}, u32[]{:S(2)}) %collective-permute-start.9) | collective-permute-done | bytes 16416 | tf_op jit(solution)/shard_map/ppermute | solution.py:1021
  148.4 4.6 %all-to-all-done.1 = bf16[16,112,128]{2,1,0:T(8,128)(2,1)S(1)} async-done(((bf16[16,112,128]{2,1,0:T(8,128)(2,1)}), bf16[16,112,128]{2,1,0:T(8,128)(2,1)S(1)}, u32[]{:S(2)}, u32[]{:S(2)}) %all-to-all-start.1) | async-done | bytes 458784 | tf_op jit(solution)/shard_map/all_to_all | solution.py:1027
  153.1 0.0 copy-done.8
  153.1 0.0 copy-done.9
  153.1 0.8 copy-done
  153.8 2.0 %final.1 = (f32[128,256]{1,0:T(8,128)}, f32[1,8]{1,0:T(1,128)}, f32[256,32]{1,0:T(8,128)}, f32[4,16]{1,0:T(4,128)}, f32[1,16]{1,0:T(1,128)}, /*index=5*/f32[16,4...) custom-call(f32[128,256]{1,0:T(8,128)} %get-tuple-element.108.refs_0, ...), custom_call_target="tpu_custom_call" | custom-call | bytes 1048576 | tf_op jit(solution)/shard_map/final/pallas_call | solution.py:69
  155.9 1.6 %copy.36 = f32[256,32]{0,1:T(8,128)} copy(f32[256,32]{1,0:T(8,128)} %get-tuple-element.129) | data formatting | bytes 65536
  (6 shorter events, 0.0 us)
Async XLA Ops:
  26.3 8.8 %copy-start.1 = (bf16[16,112,128]{2,1,0:T(8,128)(2,1)}, bf16[16,112,128]{2,1,0:T(8,128)(2,1)S(1)}, u32[]{:S(2)}) copy-start(bf16[16,112,128]{2,1,0:T(8,128)(2,1)S(1)} %all_to_all.22) | copy-start | bytes 1376260
  26.3 8.8 %collective-permute-start.2 = (bf16[1792,128]{1,0:T(8,128)(2,1)S(1)}, bf16[1792,128]{1,0:T(8,128)(2,1)S(1)}, u32[]{:S(2)}, u32[]{:S(2)}) collective-permute-start(bf16[1792,128]{1,0:T(8,128)(2,1)S(1)} %bitcast.35), channel_id=1, source_target_pairs={{0,16},{16,0},{1,17},{17,1},{2,18},{18,2},{3,19},{19,3},{4,20},{20... | collective-permute-start | bytes 1376264 | tf_op jit(solution)/shard_map/ppermute | solution.py:887
  27.1 4.4 %collective-permute-start = (bf16[8,256]{1,0:T(8,128)(2,1)S(1)}, bf16[8,256]{1,0:T(8,128)(2,1)S(1)}, u32[]{:S(2)}, u32[]{:S(2)}) collective-permute-start(bf16[8,256]{1,0:T(8,128)(2,1)S(1)} %reshape_squeeze.6), channel_id=1, source_target_pairs={{0,1},{1,2},{2,3},{3,4},{4,5},{5,6},{6,7},{7,8},{8,9},{9,10},{10,1... | collective-permute-start | bytes 12296 | tf_op jit(solution)/shard_map/ppermute | solution.py:864
  29.5 5.5 %collective-permute-start.1 = (bf16[8,256]{1,0:T(8,128)(2,1)S(1)}, bf16[8,256]{1,0:T(8,128)(2,1)S(1)}, u32[]{:S(2)}, u32[]{:S(2)}) collective-permute-start(bf16[8,256]{1,0:T(8,128)(2,1)S(1)} %reshape_squeeze.7), channel_id=1, source_target_pairs={{1,0},{2,1},{3,2},{4,3},{5,4},{6,5},{7,6},{8,7},{9,8},{10,9},{11,1... | collective-permute-start | bytes 12296 | tf_op jit(solution)/shard_map/ppermute | solution.py:865
  35.0 0.6 copy-start.10
  35.0 0.8 copy-start.11
  47.2 14.2 %collective-permute-start.3 = (bf16[144,512]{1,0:T(8,128)(2,1)}, bf16[144,512]{1,0:T(8,128)(2,1)S(1)}, u32[]{:S(2)}, u32[]{:S(2)}) collective-permute-start(bf16[144,512]{1,0:T(8,128)(2,1)} %get-tuple-element.77.refs_1_), channel_id=1, source_target_pairs={{0,1},{1,0},{2,3},{3,2},{4,5},{5,4},{6,7},{7,6},{8,9},{9,8},{10,11... | collective-permute-start | bytes 442376 | tf_op jit(solution)/shard_map/ppermute | solution.py:675
  49.9 11.5 %collective-permute-start.4 = (bf16[144,512]{1,0:T(8,128)(2,1)}, bf16[144,512]{1,0:T(8,128)(2,1)S(1)}, u32[]{:S(2)}, u32[]{:S(2)}) collective-permute-start(bf16[144,512]{1,0:T(8,128)(2,1)} %get-tuple-element.77.refs_1_), channel_id=1, source_target_pairs={{0,2},{1,3},{2,0},{3,1},{4,6},{5,7},{6,4},{7,5},{8,10},{9,11},{10,... | collective-permute-start | bytes 442376 | tf_op jit(solution)/shard_map/ppermute | solution.py:675
  52.6 8.8 %collective-permute-start.5 = (bf16[144,512]{1,0:T(8,128)(2,1)}, bf16[144,512]{1,0:T(8,128)(2,1)S(1)}, u32[]{:S(2)}, u32[]{:S(2)}) collective-permute-start(bf16[144,512]{1,0:T(8,128)(2,1)} %get-tuple-element.77.refs_1_), channel_id=1, source_target_pairs={{0,3},{1,2},{2,1},{3,0},{4,7},{5,6},{6,5},{7,4},{8,11},{9,10},{10,... | collective-permute-start | bytes 442376 | tf_op jit(solution)/shard_map/ppermute | solution.py:675
  61.4 0.7 copy-start.5
  61.4 0.7 copy-start.6
  61.4 0.8 copy-start.7
  64.4 42.0 %collective-permute-start.6 = (bf16[144,512]{1,0:T(8,128)(2,1)}, bf16[144,512]{1,0:T(8,128)(2,1)S(1)}, u32[]{:S(2)}, u32[]{:S(2)}) collective-permute-start(bf16[144,512]{1,0:T(8,128)(2,1)} %get-tuple-element.78.refs_1_), channel_id=1, source_target_pairs={{0,4},{1,5},{2,6},{3,7},{4,0},{5,1},{6,2},{7,3},{8,12},{9,13},{10,... | collective-permute-start | bytes 442376 | tf_op jit(solution)/shard_map/ppermute | solution.py:675
  64.7 41.7 %collective-permute-start.7 = (bf16[144,512]{1,0:T(8,128)(2,1)}, bf16[144,512]{1,0:T(8,128)(2,1)S(1)}, u32[]{:S(2)}, u32[]{:S(2)}) collective-permute-start(bf16[144,512]{1,0:T(8,128)(2,1)} %get-tuple-element.78.refs_1_), channel_id=1, source_target_pairs={{0,8},{1,9},{2,10},{3,11},{4,12},{5,13},{6,14},{7,15},{8,0},{9,1},... | collective-permute-start | bytes 442376 | tf_op jit(solution)/shard_map/ppermute | solution.py:675
  65.9 40.5 %collective-permute-start.8 = (bf16[144,512]{1,0:T(8,128)(2,1)}, bf16[144,512]{1,0:T(8,128)(2,1)S(1)}, u32[]{:S(2)}, u32[]{:S(2)}) collective-permute-start(bf16[144,512]{1,0:T(8,128)(2,1)} %get-tuple-element.78.refs_1_), channel_id=1, source_target_pairs={{0,12},{1,13},{2,14},{3,15},{4,8},{5,9},{6,10},{7,11},{8,4},{9,5},... | collective-permute-start | bytes 442376 | tf_op jit(solution)/shard_map/ppermute | solution.py:675
  106.4 0.7 copy-start.2
  106.4 0.7 copy-start.3
  106.4 0.8 copy-start.4
  130.6 2.1 %collective-permute-start.11 = (bf16[1792,128]{1,0:T(8,128)(2,1)}, bf16[1792,128]{1,0:T(8,128)(2,1)S(1)}, u32[]{:S(2)}, u32[]{:S(2)}) collective-permute-start(bf16[1792,128]{1,0:T(8,128)(2,1)} %get-tuple-element.111), channel_id=1, source_target_pairs={{0,16},{16,0},{1,17},{17,1},{2,18},{18,2},{3,19},{19,3},{4,20},{20... | collective-permute-start | bytes 1376264 | tf_op jit(solution)/shard_map/ppermute | solution.py:1026
  132.7 6.2 %copy-start.12 = (f32[16,256]{1,0:T(8,128)S(1)}, f32[16,256]{1,0:T(8,128)}, u32[]{:S(2)}) copy-start(f32[16,256]{1,0:T(8,128)} %get-tuple-element.109) | copy-start | bytes 49156
  134.6 18.4 %all-to-all-start.1 = ((bf16[16,112,128]{2,1,0:T(8,128)(2,1)}), bf16[16,112,128]{2,1,0:T(8,128)(2,1)S(1)}, u32[]{:S(2)}, u32[]{:S(2)}) async-start(bf16[16,112,128]{2,1,0:T(8,128)(2,1)} %bitcast.19), calls=%async_computation.1 | async-start | bytes 917504 | tf_op jit(solution)/shard_map/all_to_all | solution.py:1027
  138.9 5.3 %collective-permute-start.10 = (f32[16,256]{1,0:T(8,128)S(1)}, f32[16,256]{1,0:T(8,128)S(1)}, u32[]{:S(2)}, u32[]{:S(2)}) collective-permute-start(f32[16,256]{1,0:T(8,128)S(1)} %copy-done.12), channel_id=1, source_target_pairs={{0,1},{1,2},{2,3},{3,4},{4,5},{5,6},{6,7},{7,8},{8,9},{9,10},{10,1... | collective-permute-start | bytes 49160 | tf_op jit(solution)/shard_map/ppermute | solution.py:1022
  142.7 5.7 %collective-permute-start.9 = (f32[16,256]{1,0:T(8,128)S(1)}, f32[16,256]{1,0:T(8,128)S(1)}, u32[]{:S(2)}, u32[]{:S(2)}) collective-permute-start(f32[16,256]{1,0:T(8,128)S(1)} %copy-done.12), channel_id=1, source_target_pairs={{1,0},{2,1},{3,2},{4,3},{5,4},{6,5},{7,6},{8,7},{9,8},{10,9},{11,1... | collective-permute-start | bytes 49160 | tf_op jit(solution)/shard_map/ppermute | solution.py:1021
  144.2 8.9 %copy-start.8 = (f32[16,256]{1,0:T(8,128)}, f32[16,256]{1,0:T(8,128)S(1)}, u32[]{:S(2)}) copy-start(f32[16,256]{1,0:T(8,128)S(1)} %collective-permute-done.10.refs_2_) | copy-start | bytes 49156
  148.4 4.6 %copy-start.9 = (f32[16,256]{1,0:T(8,128)}, f32[16,256]{1,0:T(8,128)S(1)}, u32[]{:S(2)}) copy-start(f32[16,256]{1,0:T(8,128)S(1)} %collective-permute-done.9.refs_1_) | copy-start | bytes 49156
  153.1 0.8 copy-start
where the time goes:
time: 158 us; the launch traced here: 157 us
  Pallas kernels  87.4 us (55%)
  starting transfers between devices  23 us (15%)
  blocking collectives  22.2 us (14%)
  waiting for transfers between devices  14.7 us (9%)
  local copies, waits for them, and re-layouts  6.89 us (4%)
  other arithmetic  2.51 us (2%)
    pallas_call x8, Pallas kernels, run(): pl.pallas_call(kernel, out_shape=tuple((jax.ShapeDtypeStruct(*outs[k]) fo...  87.4 us
    all_to_all x1, blocking collectives, local(): mine = lax.all_to_all(buf, 'seq', 0, 0, tiled=True)  22.2 us
    ppermute x6, starting transfers between devices, carry_send(): lax.ppermute(element, 'seq', [(i, i ^ m * stride) for i in range(count)])  9.79 us
    unnamed x29, local copies, waits for them, and re-layouts  6.1 us
    all_to_all x1, waiting for transfers between devices, local(): ins['parts'] = lax.all_to_all(longs['keep'] + got, 'seq', 0, 0, tiled=True)  4.63 us
    all_to_all x1, starting transfers between devices, local(): ins['parts'] = lax.all_to_all(longs['keep'] + got, 'seq', 0, 0, tiled=True)  4.27 us
    ppermute x1, waiting for transfers between devices, local(): from_next = lax.ppermute(longs['delta'], 'seq', down)  4.26 us
    ppermute x1, starting transfers between devices, local(): from_prev = lax.ppermute(longs['delta'], 'seq', up)  3.83 us
  transfers between devices with their start and end apart: 13, of which 5 were waited for; matrix products, arithmetic and copies ran while one was open for 1% of the time, Pallas kernels for 29%

commit v1 on v0

--- a/solution.py
+++ b/solution.py
@@ -20,6 +20,8 @@
 BOTH = ("dp", "seq")
 IN_ROWS, OUT_ROWS, CH_ROWS = 32, 16, 16
 PACK = 2 * IN_ROWS + 2 * OUT_ROWS + CH_ROWS
+EDGE = 16
+BLOCK = PACK + EDGE
 AT_DT, AT_A, AT_SMALL = 48, 64, 96
 
 
@@ -47,39 +49,54 @@
 
 
 def sigmoid(x):
-    return 1.0 / (1.0 + jnp.exp(-x))
+    return 0.5 * jnp.tanh(0.5 * x) + 0.5
 
 
 def loop(count, body):
     lax.fori_loop(0, count, lambda i, c: (body(i), c)[1], 0)
 
 
-def run(name, body, ins, outs, scratch=None, flops=0, far=()):
-    scratch = scratch or {}
-    in_names, out_names, scratch_names = list(ins), list(outs), list(scratch)
+def run(name, body, ins, outs, scratch=None, flops=0, far=(), early=(), vmem=60):
+    scratch = dict(scratch or {}, **{k: outs[k] for k in early})
+    if early:
+        scratch["out_sems"] = pltpu.SemaphoreType.DMA((len(early),))
+    in_names, scratch_names = list(ins), list(scratch)
+    out_names = [k + "_out" if k in early else k for k in outs]
 
     def kernel(*refs):
-        body(types.SimpleNamespace(**dict(zip(in_names + out_names + scratch_names, refs))))
+        r = types.SimpleNamespace(**dict(zip(in_names + out_names + scratch_names, refs)))
+        r.early = tuple(early)
+        body(r)
 
     def spec(key):
-        if key == "place":
-            return pl.BlockSpec(memory_space=pltpu.SMEM)
         return pl.BlockSpec(memory_space=pl.ANY if key in far else pltpu.VMEM)
 
     result = pl.pallas_call(
         kernel,
-        out_shape=tuple(jax.ShapeDtypeStruct(*outs[k]) for k in out_names),
+        out_shape=tuple(jax.ShapeDtypeStruct(*v) for v in outs.values()),
         in_specs=[spec(k) for k in in_names],
-        out_specs=tuple(pl.BlockSpec(memory_space=pltpu.VMEM) for _ in out_names),
+        out_specs=tuple(
+            pl.BlockSpec(memory_space=pl.ANY if k in early else pltpu.VMEM) for k in outs
+        ),
         scratch_shapes=[
             pltpu.VMEM(*scratch[k]) if isinstance(scratch[k], tuple) else scratch[k]
             for k in scratch_names
         ],
-        compiler_params=pltpu.CompilerParams(vmem_limit_bytes=60 * 1024 * 1024),
+        compiler_params=pltpu.CompilerParams(vmem_limit_bytes=vmem << 20),
         cost_estimate=pl.CostEstimate(flops=flops, bytes_accessed=1 << 20, transcendentals=0),
         name=name,
     )(*[ins[k] for k in in_names])
-    return dict(zip(out_names, result))
+    return dict(zip(outs, result))
+
+
+def send(r, names):
+    copies = []
+    for name in names:
+        at = r.early.index(name)
+        copy = pltpu.make_async_copy(getattr(r, name), getattr(r, name + "_out"), r.out_sems.at[at])
+        copy.start()
+        copies.append(copy)
+    return copies
 
 
 def pack_body(r):
@@ -89,7 +106,7 @@
     r.rows[5:6, :] = r.dt_b[...]
     r.rows[6:7, :] = r.skip[...]
     r.rows[7:8, 0 : r.gain.shape[1]] = r.gain[...]
-    in_t = mm(eye(IN_ROWS), r.in_w[...], NT).astype(BF)
+    in_t = r.in_wT[...]
     small = jnp.concatenate(split(r.rows[...]), 0)
     id16 = eye(CH_ROWS)
 
@@ -106,22 +123,60 @@
         + place(mm(id16, small, NT), AT_SMALL)
     ).astype(BF)
     out_w = r.out_w[...]
-    for j in range(r.buf.shape[0] // PACK):
-        at = j * PACK
+    count = r.buf.shape[0] // BLOCK
+    for j in range(count):
+        at = j * BLOCK
         for half in range(2):
             lanes = slice(half * LT, (half + 1) * LT)
             r.buf[at + half * IN_ROWS : at + (half + 1) * IN_ROWS, :] = in_t[:, lanes]
             low = at + 2 * IN_ROWS + half * OUT_ROWS
             r.buf[low : low + OUT_ROWS, :] = out_w[:, lanes]
         r.buf[at + PACK - CH_ROWS : at + PACK, :] = chan
+        r.buf[at + PACK : at + BLOCK, :] = jnp.zeros((EDGE, LT), BF)
+    T = r.tok.shape[0] // MB
+
+    def edge(first):
+        rows = [r.tok[mb * T + first : mb * T + first + 16, :].astype(F32) for mb in range(MB)]
+        at = 12 if first else 0
+        return jnp.concatenate([x[at : at + 4] for x in rows], 0)
+
+    put_edges(r.buf, edge(T - 16), edge(0))
+
+
+def put_edges(buf, to_next, to_prev):
+    seq = lax.axis_index("seq")
+    count = buf.shape[0] // BLOCK
+
+    def halves(x):
+        return jnp.concatenate([x[:, :LT], x[:, LT:]], 0).astype(BF)
+
+    @pl.when(seq < count - 1)
+    def _():
+        buf[pl.ds(pl.multiple_of((seq + 1) * BLOCK + PACK, 16), EDGE), :] = halves(to_next)
+
+    @pl.when(seq > 0)
+    def _():
+        buf[pl.ds(pl.multiple_of((seq - 1) * BLOCK + PACK, 16), EDGE), :] = halves(to_prev)
+
+
+def get_edges(buf):
+    seq = lax.axis_index("seq")
+    count = buf.shape[0] // BLOCK
+    result = []
+    for j, there in ((jnp.maximum(seq - 1, 0), seq > 0), (jnp.minimum(seq + 1, count - 1), seq < count - 1)):
+        x = buf[pl.ds(pl.multiple_of(j * BLOCK + PACK, 16), EDGE), :].astype(F32)
+        x = jnp.concatenate([x[:8], x[8:]], 1)
+        result.append(jnp.where(there, x, 0.0))
+    return result
 
 
 def unpack(r):
-    count = r.mine.shape[0] // PACK
-    mine_at = r.place[0]
+    count = r.mine.shape[0] // BLOCK
+    mine_at = lax.axis_index("dp")
+    r.edge[...] = jnp.concatenate(get_edges(r.mine), 0).astype(BF)
     for src, d in ((r.mine, mine_at), (r.other, 1 - mine_at)):
         for j in range(count):
-            at = j * PACK
+            at = j * BLOCK
             in_at = pl.multiple_of(d * (count * IN_ROWS) + j * IN_ROWS, IN_ROWS)
             out_at = pl.multiple_of(d * (count * OUT_ROWS) + j * OUT_ROWS, OUT_ROWS)
             for half in range(2):
@@ -166,7 +221,11 @@
     return (src == scan) & (pos == want)
 
 
-def normalise(tok, gain):
+def gain_row(r):
+    return r.gain[0:1, :] if r.gain.shape[0] == 1 else r.gain[7:8, :]
+
+
+def normalise(tok):
     source = tok.astype(F32)
     scale = lax.rsqrt(jnp.mean(source * source, 1, keepdims=True) + EPS)
     return source, scale, source * scale
@@ -178,9 +237,9 @@
 
 def prep(r, T, halo):
     R = 4 * T
-    gain = r.gain[0:1, :] if r.gain.shape[0] == 1 else r.gain[7:8, :]
+    gain = gain_row(r)
     swap = swap_of(r)
-    _, _, unit = normalise(r.tok[...], gain)
+    _, _, unit = normalise(r.tok[...])
     normed = (unit * gain).astype(BF)
     put = placing(T, False)
     r.V[HALO:, :] = mm(
@@ -193,7 +252,7 @@
         onehot(put & (mrow != 0)), jnp.concatenate([cot, mm(cot, swap).astype(BF)], 0)
     ).astype(BF)
     if halo:
-        hn = (normalise(r.edge[...], gain)[2] * gain).astype(BF)
+        hn = (normalise(r.edge[...])[2] * gain).astype(BF)
         r.V[0:HALO, :] = (
             mm(onehot(edge_place(False)), hn)
             + mm(onehot(edge_place(True)), mm(hn, swap).astype(BF))
@@ -285,7 +344,7 @@
     return slice(e * LT, (e + 1) * LT)
 
 
-def scan_forward(r, T, start, full, U=8):
+def scan_forward(r, T, start, full, U=16):
     low = iota((8, LT), 0) < 4
     for e in range(E // LT):
         es = lanes_of(e)
@@ -352,68 +411,62 @@
             r.ends[64 + 8 * k : 64 + 8 * k + 8, es] = last[k]
 
 
-def scan_backward(r, T, start, U=8):
+def scan_backward(r, T, start, group=2, unroll=4):
     low = iota((8, LT), 0) < 4
+    r.alog[...] = jnp.zeros((8 * NP, E), F32)
+    r.b[...] = jnp.zeros((8 * NP, E), F32) if start is None else start[64:128, :]
+    groups = E // LT // group
+    for g in range(groups):
+        tiles = [lanes_of(g * group + e) for e in range(group)]
+
+        def body(i, g=g, tiles=tiles):
+            for u in range(unroll):
+                pair = T // 2 - 1 - (i * unroll + u)
+                row = pl.multiple_of(pair * 8, 8)
+                r16 = pl.multiple_of(pair * 16, 16)
+                st = [dup(r.st[pl.ds(row, 8), es], low) for es in tiles]
+                si = [dup(r.si[pl.ds(row, 8), es], low) for es in tiles]
+                gm = [dup(r.gm[pl.ds(row, 8), es], low) for es in tiles]
+                q = [[0.0, 0.0] for _ in tiles]
+                p = [[0.0, 0.0] for _ in tiles]
+                for k in range(NP):
+                    ks = slice(8 * k, 8 * k + 8)
+                    im = [r.imb[pl.ds(r16 + 8 * h, 8), lanes_of(k)] for h in range(2)]
+                    om = [r.omb[pl.ds(r16 + 8 * h, 8), lanes_of(k)] for h in range(2)]
+                    xi, xo = [0.0, 0.0], [0.0, 0.0]
+                    for e, es in enumerate(tiles):
+                        rk = r.r2[ks, es]
+                        b = r.b[ks, es]
+                        states = [r.states[2 * pair + h, ks, es] for h in range(3)]
+                        rates = 0.0
+                        for h in (1, 0):
+                            a = gm[e][h] * om[h] + b
+                            b = jnp.exp2(st[e][h] * rk) * a
+                            w = b * states[h]
+                            q[e][h] = w * rk + q[e][h]
+                            rates = w * st[e][h] + rates
+                            p[e][h] = a * im[h] + p[e][h]
+                            xi[h] = a * si[e][h] + xi[h]
+                            xo[h] = states[h + 1] * gm[e][h] + xo[h]
+                        r.b[ks, es] = b
+                        r.alog[ks, es] += rates
+                    cs = lanes_of(g * NP + k)
+                    r.xi[pl.ds(r16, 16), cs] = jnp.concatenate(xi, 0).astype(BF)
+                    r.xo[pl.ds(r16, 16), cs] = jnp.concatenate(xo, 0).astype(BF)
+                for e, es in enumerate(tiles):
+                    for out, v in ((r.q, q[e]), (r.p, p[e])):
+                        v = [x + pltpu.roll(x, 4, 0) for x in v]
+                        out[pl.ds(row, 8), es] = jnp.where(low, v[0], v[1])
+
+        loop(T // 2 // unroll, body)
     rl, rc = iota((NP * LT, LT), 0), iota((NP * LT, LT), 1)
-    r.red[...] = onehot((rl >> 7) == (rc >> 1))
-    for e in range(E // LT):
-        es = lanes_of(e)
-        if start is None:
-            first = tuple(jnp.zeros((8, LT), F32) for _ in range(NP))
-        else:
-            first = tuple(start[64 + 8 * k : 64 + 8 * k + 8, es] for k in range(NP))
-
-        def body(i, carry):
-            b, acc = list(carry[0]), list(carry[1])
-            base = T // U - 1 - i
-            xi = [[None] * U for _ in range(NP)]
-            xo = [[None] * U for _ in range(NP)]
-            for u in range(U // 2 - 1, -1, -1):
-                pair = base * (U // 2) + u
-                row = pl.multiple_of(pair * 8, 8)
-                st = dup(r.st[pl.ds(row, 8), es], low)
-                si = dup(r.si[pl.ds(row, 8), es], low)
-                gm = dup(r.gm[pl.ds(row, 8), es], low)
-                qs, ps = [None, None], [None, None]
-                for h in (1, 0):
-                    t = pair * 2 + h
-                    r8 = pl.multiple_of(t * 8, 8)
-                    q = p = None
-                    for k in range(NP):
-                        rk = r.r2[8 * k : 8 * k + 8, es]
-                        a = gm[h] * r.omb[pl.ds(r8, 8), lanes_of(k)] + b[k]
-                        b[k] = jnp.exp2(st[h] * rk) * a
-                        w = b[k] * r.states[t, 8 * k : 8 * k + 8, es]
-                        q = w * rk if q is None else q + w * rk
-                        acc[k] = acc[k] + w * st[h]
-                        ai = a * r.imb[pl.ds(r8, 8), lanes_of(k)]
-                        p = ai if p is None else p + ai
-                        xi[k][2 * u + h] = a * si[h]
-                        xo[k][2 * u + h] = r.states[t + 1, 8 * k : 8 * k + 8, es] * gm[h]
-                    qs[h] = q + pltpu.roll(q, 4, 0)
-                    ps[h] = p + pltpu.roll(p, 4, 0)
-                r.q[pl.ds(row, 8), es] = jnp.where(low, qs[0], qs[1])
-                r.p[pl.ds(row, 8), es] = jnp.where(low, ps[0], ps[1])
-            y = None
-            for k in range(0, NP, 2):
-                left = jnp.concatenate(
-                    [jnp.concatenate(xi[j] + xo[j], 0).astype(BF) for j in (k, k + 1)], 1
-                )
-                part = mm(left, r.red[k * LT : (k + 2) * LT, :])
-                y = part if y is None else y + part
-            at = pl.multiple_of(base * U * 8, U * 8)
-            if e == 0:
-                r.yi[pl.ds(at, U * 8), :] = y[: U * 8]
-                r.yo[pl.ds(at, U * 8), :] = y[U * 8 :]
-            else:
-                r.yi[pl.ds(at, U * 8), :] += y[: U * 8]
-                r.yo[pl.ds(at, U * 8), :] += y[U * 8 :]
-            return tuple(b), tuple(acc)
-
-        zero = tuple(jnp.zeros((8, LT), F32) for _ in range(NP))
-        _, acc = lax.fori_loop(0, T // U, body, (first, zero))
-        for k in range(NP):
-            r.alog[8 * k : 8 * k + 8, es] = acc[k]
+    red = onehot((rl >> 7) == (rc >> 1))
+    W = NP * LT
+    for out, x in ((r.yi, r.xi), (r.yo, r.xo)):
+        total = x[:, :W]
+        for g in range(1, groups):
+            total = total + x[:, g * W : (g + 1) * W]
+        out[...] = mm(total, red)
     G = 256
     own = (iota((G, LT), 1) & 1) == ((iota((G, LT), 0) >> 2) & 1)
     valid = own & (iota((G, LT), 1) < N)
@@ -433,7 +486,9 @@
         states=((T + 1, 8 * NP, E), F32),
         imb=((8 * T, NP * LT), F32),
         omb=((8 * T, NP * LT), F32),
-        red=((NP * LT, LT), BF),
+        xi=((8 * T, 2 * NP * LT), BF),
+        xo=((8 * T, 2 * NP * LT), BF),
+        b=((8 * NP, E), F32),
         yi=((8 * T, LT), F32),
         yo=((8 * T, LT), F32),
         mix=((4 * T, E), F32),
@@ -449,7 +504,6 @@
     B = 32
     w = [r.rowp[k : k + 1, :] for k in range(4)]
     skip = r.rowp[6:7, :]
-    gain = r.gain[0:1, :] if r.gain.shape[0] == 1 else r.gain[7:8, :]
     r.acc[...] = jnp.zeros((64, E), F32)
     for c in range(0, E, 256):
         r.gg[:, c : c + 256] = mm(r.GR[...], r.outw[c : c + 256, :], NT)
@@ -520,6 +574,8 @@
     if not halo:
         r.gp[0:HALO, :E] = jnp.zeros((HALO, E), BF)
 
+
+def param_grads(r):
     zT = mm(eye(LT), r.z[...], NT).astype(BF)
     row = iota((LT, E), 0)
     peT = jnp.where(row < AT_DT, mm(zT, r.il[...]), 0.0)
@@ -531,46 +587,61 @@
         [jnp.zeros((AT_A, E), F32), r.rate[...], jnp.zeros((LT - AT_A - N, E), F32)], 0
     )
     peT = peT + (mm(fold, hi) + mm(fold, lo)) * rate
-    rr, cc = iota((LT, 64), 0), iota((LT, 64), 1)
     hi, lo = split(r.acc[...])
     fold = onehot((rr >= AT_SMALL) & (rr - AT_SMALL == (cc >> 3)))
-    peT = peT + mm(fold, hi) + mm(fold, lo)
+    r.g_peT[...] = peT + mm(fold, hi) + mm(fold, lo)
     r.g_out[...] = mm(r.gated[...], r.GR[...], TN)
     for c in range(0, 2 * E, 256):
         r.g_inT[c : c + 256, :] = mm(r.gp[:, c : c + 256], r.V[...], TN)
-
+    rows = mm(r.gp[...], r.inT[...])
+    r.rows[...] = rows
+    term = rows * r.V[...].astype(F32)
+    first = (iota(term.shape, 0) & 3) < 2
+    fwd = jnp.sum(jnp.where(first, term, 0.0), 0, keepdims=True)
+    rev = jnp.sum(jnp.where(first, 0.0, term), 0, keepdims=True)
+    both = jnp.concatenate([fwd, rev, jnp.zeros((6, D), F32)], 0)
+    hi, lo = split(both)
+    swap = swap_of(r)
+    r.g_gain[...] = both + pltpu.roll(mm(hi, swap) + mm(lo, swap), 7, 0)
+
+
+def edge_delta(r):
+    swap = swap_of(r)
+    hi, lo = split(r.rows[0:HALO, :])
+    grad = jnp.where(
+        (iota((HALO, D), 0) & 3) < 2, r.rows[0:HALO, :], mm(hi, swap) + mm(lo, swap)
+    )
+    _, scale, unit = normalise(mm(onehot(edge_place(False) | edge_place(True)), r.edge[...]))
+    g = grad * gain_row(r)
+    return scale * (g - unit * jnp.mean(g * unit, 1, keepdims=True))
+
+
+def window_outputs(r, tok, cot, mask, gated, rows, out, ing):
+    half = tok.shape[0]
+    T = half // MB
+    gain = gain_row(r)
     swap = swap_of(r)
     back = onehot(placing(T, True))
-    half = MB * T
-    gated = mm(back, r.gated[...]).astype(BF)
-    source, scale, unit = normalise(r.tok[...], gain)
+    g = mm(back, gated[...]).astype(BF)
+    source, scale, unit = normalise(tok[...])
     outs = mm(r.outw[...], swap).astype(BF)
-    result = source + mm(gated[:half], r.outw[...]) + mm(gated[half:], outs)
-    r.out[...] = result.astype(BF)
-    grad = jnp.zeros((half, D), F32)
-    for c in range(0, 2 * E, 256):
-        g = mm(back, r.gp[HALO:, c : c + 256]).astype(BF)
-        win = r.inT[c : c + 256, :]
-        grad = grad + mm(g[:half], win) + mm(g[half:], mm(win, swap).astype(BF))
-    gain_term = jnp.sum(grad * unit, 0, keepdims=True)
+    out[...] = (source + mm(g[:half], r.outw[...]) + mm(g[half:], outs)).astype(BF)
+    hi, lo = split(rows[HALO:, :])
+    grad = (
+        mm(back[:half], hi)
+        + mm(back[:half], lo)
+        + mm(back[half:], mm(hi, swap).astype(BF))
+        + mm(back[half:], mm(lo, swap).astype(BF))
+    )
     g = grad * gain
-    mrow = jnp.concatenate([r.mask[0:1, :], r.mask[1:2, :]], 1)
+    mrow = jnp.concatenate([mask[0:1, :], mask[1:2, :]], 1)
     keep = onehot((iota((half, half), 0) == iota((half, half), 1)) & (mrow != 0))
-    r.ing[...] = scale * (g - unit * jnp.mean(g * unit, 1, keepdims=True)) + mm(keep, r.cot[...])
-    if halo:
-        rows = mm(r.gp[0:HALO, :E], r.inT[0:E, :])
-        hi, lo = split(rows)
-        rows = jnp.where(
-            (iota((HALO, D), 0) & 3) < 2, rows, mm(hi, swap) + mm(lo, swap)
-        )
-        put = onehot(edge_place(False) | edge_place(True))
-        tok = mm(put, r.edge[...])
-        _, scale, unit = normalise(tok, gain)
-        gain_term = gain_term + jnp.sum(rows * unit, 0, keepdims=True)
-        g = rows * gain
-        r.delta[...] = scale * (g - unit * jnp.mean(g * unit, 1, keepdims=True))
-    r.g_gain[...] = jnp.broadcast_to(gain_term, (8, D))
-    r.g_peT[...] = peT
+    ing[...] = scale * (g - unit * jnp.mean(g * unit, 1, keepdims=True)) + mm(keep, cot[...])
+
+
+def outputs_body(r):
+    window_outputs(r, r.l_tok, r.l_cot, r.l_mask, r.l_gated, r.l_rows, r.l_out, r.l_ing)
+    window_outputs(r, r.s_tok, r.s_cot, r.s_mask, r.s_gated, r.s_rows, r.s_out, r.s_ing)
 
 
 def post_scratch(T):
@@ -588,41 +659,42 @@
     )
 
 
-def post_outs(T):
-    return dict(
-        out=((MB * T, D), BF),
-        ing=((MB * T, D), F32),
-        g_inT=((2 * E, D), F32),
-        g_out=((E, D), F32),
-        g_peT=((LT, E), F32),
-        g_gain=((8, D), F32),
-    )
-
-
-def combine_body(r, radix, stride, first, last):
-    digit = (r.place[1] // stride) % radix
+GRADS = dict(
+    g_inT=((2 * E, D), F32), g_out=((E, D), F32), g_peT=((LT, E), F32), g_gain=((8, D), F32)
+)
+
+
+def rows_out(T):
+    return dict(rows=((4 * T + HALO, D), F32))
+
+
+def combine_body(r, stride, radix, first, following):
+    seq = lax.axis_index("seq")
+    digit = (seq // stride) % radix
+    last = following is None
+    fwd = (iota((8, LT), 0) & 3) < 2
+    rows = r.recv1.shape[0] - 16
     for m in range(radix):
+        if m == 0 and last:
+            continue
         src = r.own if m == 0 else getattr(r, f"recv{m}")
-        r.mem[m, 0:128, :] = src[0:128, :].astype(F32)
-        both = src[128:144, :].astype(F32)
-        r.mem[m, 128:136, :] = both[0:8] + both[8:16]
-    fwd = (iota((8, LT), 0) & 3) < 2
+        r.mem[m, 0:rows, :] = src[0:rows, :].astype(F32)
+        both = src[rows : rows + 16, :].astype(F32)
+        r.mem[m, rows : rows + 8, :] = both[0:8] + both[8:16]
     for half in range(2):
         asc = fwd if half == 0 else jnp.logical_not(fwd)
         place = jnp.where(asc, digit, radix - 1 - digit)
+        members = radix - 1 if last else radix
+        low = 0 if last else 64 * half
+
+        def member(f, at, es):
+            return jnp.where(asc, r.mem[f ^ digit, at, es], r.mem[(radix - 1 - f) ^ digit, at, es])
+
         for e in range(E // LT):
             es = lanes_of(e)
-            sums = []
-            for f in range(radix):
-                sums.append(
-                    jnp.where(
-                        asc,
-                        r.mem[f ^ digit, 128:136, es],
-                        r.mem[(radix - 1 - f) ^ digit, 128:136, es],
-                    )
-                )
+            sums = [member(f, slice(rows, rows + 8), es) for f in range(members)]
             before = jnp.zeros((8, LT), F32)
-            for f in range(radix):
+            for f in range(members):
                 before = before + jnp.where(f < place, sums[f], 0.0)
             old = None if first else r.spre[8 * half : 8 * half + 8, es]
             if not last:
@@ -631,12 +703,16 @@
                 at = slice(64 * half + 8 * k, 64 * half + 8 * k + 8)
                 rk = r.r2[8 * k : 8 * k + 8, es]
                 total = prefix = jnp.zeros((8, LT), F32)
-                for f in range(radix):
-                    part = jnp.where(
-                        asc, r.mem[f ^ digit, at, es], r.mem[(radix - 1 - f) ^ digit, at, es]
-                    )
-                    prefix = jnp.where(place == f, total, prefix)
-                    total = jnp.exp2(rk * sums[f]) * total + part
+                for f in range(members):
+                    part = member(f, slice(low + 8 * k, low + 8 * k + 8), es)
+                    if last:
+                        here = f < place
+                        total = jnp.where(here, jnp.exp2(rk * sums[f]) * total + part, total)
+                    else:
+                        prefix = jnp.where(place == f, total, prefix)
+                        total = jnp.exp2(rk * sums[f]) * total + part
+                if last:
+                    prefix = total
                 if not first:
                     prefix = jnp.exp2(rk * old) * prefix + r.prefix[at, es]
                 r.prefix_new[at, es] = prefix
@@ -647,8 +723,21 @@
                 for f in range(1, radix):
                     whole = whole + sums[f]
                 r.tot[128:136, es] = whole
-    if not last:
+    if last:
+        return
+    if not following[1]:
         write_element(r.element, r.tot)
+        return
+    next_stride, next_radix = following[0]
+    digit = (seq // next_stride) % next_radix
+    hi, lo = split(r.tot[128:136, :])
+    sums = jnp.concatenate([hi.astype(F32), lo.astype(F32)], 0).astype(BF)
+    first_half = (iota((64, E), 0) & 3) < 2
+    for m in range(1, next_radix):
+        out = getattr(r, f"half{m}")
+        up = (digit ^ m) > digit
+        out[0:64, :] = jnp.where(first_half == up, r.tot[0:64, :], r.tot[64:128, :]).astype(BF)
+        out[64:80, :] = sums
 
 
 def write_element(out, f32):
@@ -669,36 +758,41 @@
 ELEMENT = ((144, E), BF)
 
 
-def carry_send(element, count, stage):
+def carry_send(elements, count, stage):
     stride, radix = stage
     return [
-        lax.ppermute(element, "seq", [(i, i ^ (m * stride)) for i in range(count)])
+        lax.ppermute(elements[m - 1], "seq", [(i, i ^ (m * stride)) for i in range(count)])
         for m in range(1, radix)
     ]
 
 
-def combine(place, element, received, r2, before, stage, first, last):
-    stride, radix = stage
-    ins = dict(place=place, own=element, r2=r2)
+def combine_parts(own, received, r2, before, plan, at):
+    stride, radix = plan[at]
+    first, last = at == 0, at == len(plan) - 1
+    ins = dict(r2=r2)
+    if not last:
+        ins["own"] = own
     for m in range(1, radix):
         ins[f"recv{m}"] = received[m - 1]
     if not first:
         ins.update(prefix=before["prefix_new"], spre=before["spre_new"])
     outs = dict(prefix_new=((128, E), F32))
+    following = None
     if not last:
-        outs.update(spre_new=((16, E), F32), element=ELEMENT)
-    scratch = dict(mem=((radix, 136, E), F32))
+        ends = at + 1 == len(plan) - 1
+        following = (plan[at + 1], ends)
+        outs["spre_new"] = ((16, E), F32)
+        if ends:
+            outs.update({f"half{m}": ((80, E), BF) for m in range(1, plan[at + 1][1])})
+        else:
+            outs["element"] = ELEMENT
+    scratch = dict(mem=((radix, received[0].shape[0] - 8, E), F32))
     if not last:
         scratch["tot"] = ((136, E), F32)
-    return run(
-        f"combine{stride}",
-        functools.partial(
-            combine_body, radix=radix, stride=stride, first=first, last=last
-        ),
-        ins,
-        outs,
-        scratch,
-    )
+    body = functools.partial(
+        combine_body, stride=stride, radix=radix, first=first, following=following
+    )
+    return ins, outs, scratch, body
 
 
 def long_start_body(r, T, packed):
@@ -706,7 +800,9 @@
         unpack(r)
         r.gain[...] = gain_of(r)
     derive(r)
+    copies = send(r, [k for k in r.early if k not in PREP_OUTS])
     prep(r, T, True)
+    copies += send(r, PREP_OUTS)
     maps(r, T)
     scan_forward(r, T, None, False)
     scan_adjoint_local(r, T)
@@ -717,10 +813,19 @@
     total = lax.fori_loop(0, T // 2, add, jnp.zeros((8, E), F32))
     r.ends[128:136, :] = total + pltpu.roll(total, 4, 0)
     write_element(r.element, r.ends)
-
-
-def short_start_body(r, T):
+    for copy in copies:
+        copy.wait()
+
+
+def short_windows_body(r, T):
     prep(r, T, False)
+    copies = send(r, r.early)
+    maps(r, T)
+    scan_forward(r, T, None, True)
+    scan_backward(r, T, None)
+    post(r, T, False)
+    for copy in copies:
+        copy.wait()
 
 
 def fetch_start(r, names):
@@ -732,20 +837,17 @@
     return copies
 
 
-LATE = ("ip", "gate", "co", "sz", "V", "GR", "tok", "cot", "inT", "outw", "xwT", "dtw2")
-
-
-def windows_body(r, T, halo, names):
+def long_windows_body(r, T, names, combining):
     copies = fetch_start(r, names)
+    combining(r)
     maps(r, T)
-    start = r.carry if halo else None
-    scan_forward(r, T, start, True)
-    scan_backward(r, T, start)
+    scan_forward(r, T, r.prefix_new, True)
+    scan_backward(r, T, r.prefix_new)
     for copy in copies:
         copy.wait()
-    post(r, T, halo)
-    if halo:
-        finish_grads(r)
+    post(r, T, True)
+    param_grads(r)
+    finish_grads(r)
 
 
 def finish_grads(r):
@@ -753,8 +855,9 @@
     g_inT[...] += r.s_inT[...]
     g_out[...] += r.s_out[...]
     r.g_peT[...] += r.s_peT[...]
-    r.g_gain[...] += r.s_gain[...]
+    r.g_gain[...] = (r.g_gain[...] + r.s_gain[...]) / gain_row(r)
     if not hasattr(r, "keep"):
+        r.delta[...] = edge_delta(r)
         return
     lane, col = iota((D, E), 1), iota((D, E), 0)
     pick = onehot(((lane // 16) == (col // 8)) & ((lane % 16) == (col % 8)))
@@ -762,11 +865,11 @@
         iota((LT, E), 0) == AT_SMALL + 7, mm(r.g_gain[0:1, :].astype(BF), pick), 0.0
     )
     r.pe_out[...] = peT.T.astype(BF)
-    count = r.keep.shape[0] // PACK
-    mine = r.place[0]
-    for dst, d in ((r.keep, mine), (r.give, 1 - mine)):
+    count = r.keep.shape[0] // BLOCK
+    mine = lax.axis_index("dp")
+    for dst, d, step in ((r.keep, mine, BLOCK), (r.give, 1 - mine, PACK)):
         for j in range(count):
-            at = j * PACK
+            at = j * step
             in_at = pl.multiple_of(d * (count * IN_ROWS) + j * IN_ROWS, IN_ROWS)
             out_at = pl.multiple_of(d * (count * OUT_ROWS) + j * OUT_ROWS, OUT_ROWS)
             for half in range(2):
@@ -777,27 +880,49 @@
                 low = at + 2 * IN_ROWS + half * OUT_ROWS
                 dst[low : low + OUT_ROWS, :] = g_out[pl.ds(out_at, OUT_ROWS), lanes].astype(BF)
             dst[at + PACK - CH_ROWS : at + PACK, :] = r.pe_out[pl.ds(out_at, CH_ROWS), :]
+    for j in range(count):
+        r.keep[j * BLOCK + PACK : (j + 1) * BLOCK, :] = jnp.zeros((EDGE, LT), BF)
+    delta = edge_delta(r).astype(BF)
+    row, col = iota((8, HALO), 0), iota((8, HALO), 1)
+    of = 4 * (row & 3) + (row >> 2)
+    put_edges(r.keep, mm(onehot(col == of + 2), delta), mm(onehot(col == of), delta))
+
+
+def add_body(r):
+    count = r.keep.shape[0] // BLOCK
+    for j in range(count):
+        at = j * BLOCK
+        r.buf[at : at + PACK, :] = (
+            r.keep[at : at + PACK, :].astype(F32)
+            + r.got[j * PACK : (j + 1) * PACK, :].astype(F32)
+        ).astype(BF)
+        r.buf[at + PACK : at + BLOCK, :] = r.keep[at + PACK : at + BLOCK, :]
 
 
 def final_body(r, packed):
     r.grad[...] = r.ing[...]
     T = r.grad.shape[0] // MB
+    if packed:
+        from_prev, from_next = get_edges(r.parts)
+    else:
+        from_prev, from_next = r.from_prev[...], r.from_next[...]
     for mb in range(MB):
         for j in range(4):
+            prev = 4 * mb + j if packed else 4 * j + 2 + mb
+            follow = 4 * mb + j if packed else 4 * j + mb
             row = mb * T + T - 4 + j
-            r.grad[row : row + 1, :] += r.from_next[4 * j + mb : 4 * j + mb + 1, :]
+            r.grad[row : row + 1, :] += from_next[follow : follow + 1, :]
             row = mb * T + 3 - j
-            r.grad[row : row + 1, :] += r.from_prev[4 * j + 2 + mb : 4 * j + 3 + mb, :]
+            r.grad[row : row + 1, :] += from_prev[prev : prev + 1, :]
     if not packed:
         return
-    count = r.parts.shape[0] // PACK
+    count = r.parts.shape[0] // BLOCK
     total = r.parts[0:PACK, :].astype(F32)
     for j in range(1, count):
-        total = total + r.parts[j * PACK : (j + 1) * PACK, :].astype(F32)
+        total = total + r.parts[j * BLOCK : j * BLOCK + PACK, :].astype(F32)
     for half in range(2):
         lanes = slice(half * LT, (half + 1) * LT)
-        hi, lo = split(total[half * IN_ROWS : (half + 1) * IN_ROWS])
-        r.in_w[lanes, :] = mm(eye(LT), hi, NT) + mm(eye(LT), lo, NT)
+        r.in_wT[:, lanes] = total[half * IN_ROWS : (half + 1) * IN_ROWS]
         low = 2 * IN_ROWS + half * OUT_ROWS
         r.out_w[:, lanes] = total[low : low + OUT_ROWS]
     pe = total[PACK - CH_ROWS :]
@@ -856,21 +981,17 @@
     count = lax.axis_size("seq")
     span, short = long_tokens.shape[2], short_tokens.shape[2]
     packed = out_weight.shape[0] == OUT_ROWS and in_weight.shape[1] == IN_ROWS
-    place = jnp.stack([lax.axis_index("dp"), lax.axis_index("seq")]).astype(jnp.int32)
     comp = complement.reshape(1, D)
     up = [(i, i + 1) for i in range(count - 1)]
     down = [(i + 1, i) for i in range(count - 1)]
 
-    tail = lax.ppermute(long_tokens[:, 0, span - 4 :, :].reshape(8, D), "seq", up)
-    head = lax.ppermute(long_tokens[:, 0, :4, :].reshape(8, D), "seq", down)
-    edge = jnp.concatenate([tail, head], 0)
     if packed:
         buf = run(
             "pack",
             pack_body,
             dict(
                 gain=norm_gain.reshape(1, -1),
-                in_w=in_weight,
+                in_wT=in_weight.T,
                 conv_w=conv_weight,
                 conv_b=conv_bias.reshape(1, -1),
                 x_w=x_weight,
@@ -879,14 +1000,17 @@
                 a_log=a_log,
                 skip=d_skip.reshape(1, -1),
                 out_w=out_weight,
+                tok=long_tokens.reshape(MB * span, D),
             ),
-            dict(buf=((count * PACK, LT), BF)),
+            dict(buf=((count * BLOCK, LT), BF)),
             dict(rows=((8, CH_ROWS), F32)),
         )["buf"]
         mine = lax.all_to_all(buf, "seq", 0, 0, tiled=True)
         other = lax.ppermute(mine, "dp", [(0, 1), (1, 0)])
         weights_in = dict(mine=mine, other=other)
     else:
+        tail = lax.ppermute(long_tokens[:, 0, span - 4 :, :].reshape(8, D), "seq", up)
+        head = lax.ppermute(long_tokens[:, 0, :4, :].reshape(8, D), "seq", down)
 
         def whole(a, axis):
             return lax.all_gather(a, BOTH, axis=axis, tiled=True)
@@ -904,6 +1028,7 @@
             outw=whole(out_weight, 0),
             pe=whole(chan, 0),
             gain=whole(norm_gain, 0).reshape(1, D),
+            edge=jnp.concatenate([tail, head], 0),
         )
 
     def tokens_of(tok, cot, mask):
@@ -922,11 +1047,17 @@
         dtw2=((LT, E), BF),
         xwT=((LT, E), BF),
     )
-    unpacked = dict(inT=((2 * E, D), BF), outw=((E, D), BF), pe=((E, LT), BF), gain=((8, D), F32))
+    unpacked = dict(
+        inT=((2 * E, D), BF),
+        outw=((E, D), BF),
+        pe=((E, LT), BF),
+        gain=((8, D), F32),
+        edge=((HALO, D), BF),
+    )
     started = run(
         "long_start",
         functools.partial(long_start_body, T=span, packed=packed),
-        dict(place=place, comp=comp, edge=edge, **long_in, **weights_in),
+        dict(comp=comp, **long_in, **weights_in),
         dict(
             element=ELEMENT, **prep_outs(span), **derived, **(unpacked if packed else {})
         ),
@@ -937,97 +1068,131 @@
             ends=((136, E), F32),
         ),
         flops=1 << 33,
+        early=PREP_OUTS + tuple(derived) + (tuple(unpacked) if packed else ()),
+        vmem=62,
     )
     weights = {k: started[k] for k in derived}
     for k in unpacked:
         weights[k] = started[k] if packed else weights_in[k]
 
     plan = stages(count)
-    element, before = started["element"], None
-    received = carry_send(element, count, plan[0])
-    prepared = run(
-        "short_start",
-        functools.partial(short_start_body, T=short),
-        dict(comp=comp, **short_in, **{k: weights[k] for k in ("inT", "outw", "pe", "gain", "dtw2", "rowp")}),
-        prep_outs(short),
-        dict(il=((4 * short, E), BF)),
+    own, before = started["element"], None
+    received = carry_send([own] * 3, count, plan[0])
+    middle = dict(
+        gated=((4 * short, E), BF),
+        gp=((4 * short + HALO, 2 * E), BF),
+        il=((4 * short, E), BF),
+        gz=((4 * short, E), BF),
+        z=((4 * short, LT), BF),
+        V=((4 * short + HALO, D), BF),
+        GR=((4 * short, D), BF),
+        alog=((8 * NP, E), F32),
+        acc=((64, E), F32),
+    )
+    shorts = run(
+        "short_windows",
+        functools.partial(short_windows_body, T=short),
+        dict(
+            comp=comp,
+            **short_in,
+            **{k: weights[k] for k in ("inT", "outw", "pe", "gain", "dtw2", "xwT", "rowp", "r2")},
+        ),
+        middle,
+        {
+            k: v
+            for k, v in dict(scan_scratch(short), **post_scratch(short), **prep_outs(short)).items()
+            if k not in middle
+        },
+        flops=1 << 35,
+        early=("V", "GR"),
+        vmem=63,
+    )
+    for at in range(len(plan) - 1):
+        ins, outs, scratch, body = combine_parts(own, received, weights["r2"], before, plan, at)
+        before = run(f"combine{at}", body, ins, outs, scratch, vmem=8)
+        if at + 1 == len(plan) - 1:
+            sending = [before[f"half{m}"] for m in range(1, plan[at + 1][1])]
+        else:
+            own = before["element"]
+            sending = [own] * 3
+        received = carry_send(sending, count, plan[at + 1])
+    short_grads = run(
+        "short_grads",
+        param_grads,
+        dict(
+            comp=comp, rate=weights["rate"], inT=weights["inT"], **{k: shorts[k] for k in middle}
+        ),
+        dict(GRADS, **rows_out(short)),
         flops=1 << 33,
     )
 
-    def windows(name, T, halo, prep_out, inputs, extra, outs_more):
-        ins = dict(
-            comp=comp,
-            mask=inputs["mask"],
-            **{k: weights[k] for k in ("r2", "rowp", "rate", "gain")},
-            **{k: prep_out[k] for k in ("st", "si", "gm", "sel")},
-            **extra,
-        )
-        late = dict(
-            {k: prep_out[k] for k in ("ip", "gate", "co", "sz", "V", "GR")},
-            tok=inputs["tok"],
-            cot=inputs["cot"],
-            **{k: weights[k] for k in ("inT", "outw", "xwT", "dtw2")},
-        )
-        for k in ("s_inT", "s_out", "s_peT", "s_gain"):
-            if k in ins:
-                late[k] = ins.pop(k)
-        ins.update({k + "_far": v for k, v in late.items()})
-        names = tuple(late)
-        return run(
-            name,
-            functools.partial(windows_body, T=T, halo=halo, names=names),
-            ins,
-            dict(post_outs(T), **outs_more),
-            dict(
-                scan_scratch(T),
-                **post_scratch(T),
-                **{k: (v.shape, v.dtype) for k, v in late.items()},
-                sems=pltpu.SemaphoreType.DMA((len(names),)),
-                **(dict(pe_out=((E, LT), BF)) if halo and packed else {}),
-            ),
-            flops=1 << 35,
-            far=tuple(k + "_far" for k in names),
-        )
-
-    for at, stage in enumerate(plan[:-1]):
-        before = combine(place, element, received, weights["r2"], before, stage, at == 0, False)
-        element = before["element"]
-        received = carry_send(element, count, plan[at + 1])
-    shorts = windows("short_windows", short, False, prepared, short_in, {}, {})
-    last = len(plan) - 1
-    carry = combine(
-        place, element, received, weights["r2"], before, plan[last], last == 0, True
-    )["prefix_new"]
-    more = dict(delta=((HALO, D), F32))
+    ins, _, scratch, combining = combine_parts(
+        own, received, weights["r2"], before, plan, len(plan) - 1
+    )
+    ins.update(
+        comp=comp,
+        edge=weights["edge"],
+        **{k: weights[k] for k in ("rowp", "rate", "gain")},
+        **{k: started[k] for k in ("st", "si", "gm", "sel")},
+    )
+    late = dict(
+        {k: started[k] for k in ("ip", "gate", "co", "sz", "V", "GR")},
+        **{k: weights[k] for k in ("inT", "outw", "xwT", "dtw2")},
+        s_inT=short_grads["g_inT"],
+        s_out=short_grads["g_out"],
+        s_peT=short_grads["g_peT"],
+        s_gain=short_grads["g_gain"],
+    )
+    names = tuple(late)
+    ins.update({k + "_far": v for k, v in late.items()})
+    outs = dict(rows_out(span), gated=((4 * span, E), BF))
     if packed:
-        more.update(keep=((count * PACK, LT), BF), give=((count * PACK, LT), BF))
-    longs = windows(
+        outs.update(keep=((count * BLOCK, LT), BF), give=((count * PACK, LT), BF))
+        scratch.update(GRADS, pe_out=((E, LT), BF))
+    else:
+        outs.update(GRADS, delta=((HALO, D), F32))
+    scratch.update(prefix_new=((128, E), F32), sems=pltpu.SemaphoreType.DMA((len(names),)))
+    scratch.update(scan_scratch(span), **{k: (v.shape, v.dtype) for k, v in late.items()})
+    scratch.update({k: v for k, v in post_scratch(span).items() if k not in outs})
+    longs = run(
         "long_windows",
-        span,
-        True,
-        started,
-        long_in,
-        dict(
-            place=place,
-            carry=carry,
-            edge=edge,
-            s_inT=shorts["g_inT"],
-            s_out=shorts["g_out"],
-            s_peT=shorts["g_peT"],
-            s_gain=shorts["g_gain"],
-        ),
-        more,
-    )
-    from_next = lax.ppermute(longs["delta"], "seq", down)
-    from_prev = lax.ppermute(longs["delta"], "seq", up)
-    ins = dict(ing=longs["ing"], from_next=from_next, from_prev=from_prev)
+        functools.partial(long_windows_body, T=span, names=names, combining=combining),
+        ins,
+        outs,
+        scratch,
+        flops=1 << 35,
+        far=tuple(k + "_far" for k in names),
+    )
+
+    outs = dict(
+        l_out=((MB * span, D), BF),
+        l_ing=((MB * span, D), F32),
+        s_out=((MB * short, D), BF),
+        s_ing=((MB * short, D), F32),
+    )
+    ins = dict(comp=comp, outw=weights["outw"], gain=weights["gain"])
+    ins.update({"l_" + k: v for k, v in long_in.items()}, l_gated=longs["gated"], l_rows=longs["rows"])
+    ins.update(
+        {"s_" + k: v for k, v in short_in.items()},
+        s_gated=shorts["gated"],
+        s_rows=short_grads["rows"],
+    )
+    finished = run("outputs", outputs_body, ins, outs, flops=1 << 32, vmem=32)
+    ins = dict(ing=finished["l_ing"])
     outs = dict(grad=((MB * span, D), F32))
     if packed:
         got = lax.ppermute(longs["give"], "dp", [(0, 1), (1, 0)])
-        ins["parts"] = lax.all_to_all(longs["keep"] + got, "seq", 0, 0, tiled=True)
+        buf = run(
+            "add",
+            add_body,
+            dict(keep=longs["keep"], got=got),
+            dict(buf=((count * BLOCK, LT), BF)),
+            vmem=8,
+        )["buf"]
+        ins["parts"] = lax.all_to_all(buf, "seq", 0, 0, tiled=True)
         outs.update(
             gain=((1, D // (2 * count)), F32),
-            in_w=((D, IN_ROWS), F32),
+            in_wT=((IN_ROWS, D), F32),
             conv_w=((4, CH_ROWS), F32),
             conv_b=((1, CH_ROWS), F32),
             x_w=((CH_ROWS, 3 * N), F32),
@@ -1037,9 +1202,13 @@
             skip=((1, CH_ROWS), F32),
             out_w=((OUT_ROWS, D), F32),
         )
-    done = run("final", functools.partial(final_body, packed=packed), ins, outs)
+    else:
+        ins["from_next"] = lax.ppermute(longs["delta"], "seq", down)
+        ins["from_prev"] = lax.ppermute(longs["delta"], "seq", up)
+    done = run("final", functools.partial(final_body, packed=packed), ins, outs, vmem=8)
     if packed:
         grads = {k: done[k] for k in outs if k != "grad"}
+        grads["in_w"] = grads["in_wT"].T
         for k in ("gain", "conv_b", "dt_b", "skip"):
             grads[k] = grads[k].reshape(-1)
     else:
@@ -1062,10 +1231,10 @@
         )
     order = ("gain", "in_w", "conv_w", "conv_b", "x_w", "dt_w", "dt_b", "a_log", "skip", "out_w")
     return (
-        longs["out"].reshape(long_tokens.shape),
-        shorts["out"].reshape(short_tokens.shape),
+        finished["l_out"].reshape(long_tokens.shape),
+        finished["s_out"].reshape(short_tokens.shape),
         done["grad"].reshape(long_tokens.shape),
-        shorts["ing"].reshape(short_tokens.shape),
+        finished["s_ing"].reshape(short_tokens.shape),
     ) + tuple(grads[k] for k in order)
 
 

time: 158 us -> 123 us (0.78)
  Pallas kernels: 87.4 us -> 65.7 us
  starting transfers between devices: 23 us -> 11.6 us
  local copies, waits for them, and re-layouts: 6.89 us -> 3.26 us
  waiting for transfers between devices: 14.7 us -> 17.4 us
  other arithmetic: 2.51 us -> 0 us
    pallas_call x8 -> x9, Pallas kernels: 87.4 us -> 65.7 us  [run(): pl.pallas_call(kernel, out_shape=tuple((jax.ShapeDtypeStruct(*v) for v in...]
    ppermute x10 -> x6, starting transfers between devices: 18.7 us -> 7.94 us  [carry_send(): lax.ppermute(elements[m - 1], 'seq', [(i, i ^ m * stride) for i in range(...]
    all_to_all x1, waiting for transfers between devices: 4.63 us -> 12.6 us  [local(): ins['parts'] = lax.all_to_all(buf, 'seq', 0, 0, tiled=True)]
    ppermute x10 -> x6, waiting for transfers between devices: 8.01 us -> 0.93 us  [carry_send(): lax.ppermute(elements[m - 1], 'seq', [(i, i ^ m * stride) for i in range(...]
    unnamed x29 -> x46, local copies, waits for them, and re-layouts: 6.1 us -> 3.26 us
    add x1 -> x0, other arithmetic: 1.92 us -> none  [local(): ins['parts'] = lax.all_to_all(longs['keep'] + got, 'seq', 0, 0, tiled=True)]
    ppermute x1, waiting for transfers between devices: 0.01 us -> 1.91 us  [local(): other = lax.ppermute(mine, 'dp', [(0, 1), (1, 0)])]
  transfers between devices with their start and end apart: 13 -> 9, of which waited for: 5 -> 4; matrix products, arithmetic and copies ran while one was open for 1% -> 0% of each run, Pallas kernels for 29% -> 29%
where the time goes in v1:
time: 123 us; the launch traced here: 122 us
  Pallas kernels  65.7 us (53%)
  blocking collectives  23.4 us (19%)
  waiting for transfers between devices  17.4 us (14%)
  starting transfers between devices  11.6 us (9%)
  local copies, waits for them, and re-layouts  3.26 us (3%)
    pallas_call x9, Pallas kernels, run(): pl.pallas_call(kernel, out_shape=tuple((jax.ShapeDtypeStruct(*v) for v in...  65.7 us
    all_to_all x1, blocking collectives, local(): mine = lax.all_to_all(buf, 'seq', 0, 0, tiled=True)  23.4 us
    all_to_all x1, waiting for transfers between devices, local(): ins['parts'] = lax.all_to_all(buf, 'seq', 0, 0, tiled=True)  12.6 us
    ppermute x6, starting transfers between devices, carry_send(): lax.ppermute(elements[m - 1], 'seq', [(i, i ^ m * stride) for i in range(...  7.94 us
    all_to_all x1, starting transfers between devices, local(): ins['parts'] = lax.all_to_all(buf, 'seq', 0, 0, tiled=True)  3.57 us
    unnamed x46, local copies, waits for them, and re-layouts  3.26 us
  transfers between devices with their start and end apart: 9, of which 4 were waited for; matrix products, arithmetic and copies ran while one was open for 0% of the time, Pallas kernels for 29%

profile of v1, /device:TPU:0, one launch (start us, length us, event | category | flops | bytes accessed | tf_op | source)
XLA Modules:
  0.0 122.3 jit_solution(7099838307573980454)
XLA Ops:
  0.6 2.1 %pack.1 = bf16[2048,128]{1,0:T(8,128)(2,1)} custom-call(f32[1,8]{1,0:T(1,128)} %bitcast.56, bf16[32,256]{1,0:T(8,128)(2,1)} %bitcast.55, f32[4,16]{1,0:T(4,128)} %refs_2_.1, f32[1,16]{1,0:T(1,128)} %bitcast.57, bf16[16,48]{1,0:T(8,128)(2,1)} %refs_4_.1, bf16[16,16]{1,0:T(8,128)(2,1)} %refs_5_.1, f32[1,16]{1,0:T(1,128)} %bitcast.58, f32[16,16]{1,0:T(8,128)} %refs_7_.1, ...), custom_call_target="tpu_custom_call" | custom-call | bytes 1048576 | tf_op jit(solution)/shard_map/pack/pallas_call | solution.py:74
  2.7 23.4 %all_to_all.22 = bf16[16,128,128]{2,1,0:T(8,128)(2,1)S(1)} all-to-all(bf16[16,128,128]{2,1,0:T(8,128)(2,1)} %bitcast.52), channel_id=1, replica_groups=mesh['dp'=2,'seq'=16] {'seq'}, dimensions={0} | all-to-all | bytes 1048576 | tf_op jit(solution)/shard_map/all_to_all | solution.py:1008
  26.2 0.0 copy-start.18
  26.2 0.0 collective-permute-start
  26.2 1.9 %collective-permute-done.refs_5_ = bf16[2048,128]{1,0:T(8,128)(2,1)S(1)} collective-permute-done((bf16[2048,128]{1,0:T(8,128)(2,1)S(1)}, bf16[2048,128]{1,0:T(8,128)(2,1)S(1)}, u32[]{:S(2)}, u32[]{:S(2)}) %collective-permute-start) | collective-permute-done | bytes 524320 | tf_op jit(solution)/shard_map/ppermute | solution.py:1009
  28.1 0.0 copy-start.19
  28.1 0.0 copy-done.18
  28.1 0.8 copy-done.19
  28.9 9.6 %long_start.1 = (bf16[144,512]{1,0:T(8,128)(2,1)}, bf16[272,256]{1,0:T(8,128)(2,1)}, bf16[256,256]{1,0:T(8,128)(2,1)}, f32[272,512]{1,0:T(8,128)}, f32[256,512]{...) custom-call(s32[1,256]{1,0:T(1,128)} %bitcast.43, ...), custom_call_target="tpu_custom_call" | custom-call | flops 8589934592 | bytes 1048576 | tf_op jit(solution)/shard_map/long_start/pallas_call | solution.py:74
  38.5 0.6 collective-permute-start.1
  39.1 0.9 collective-permute-start.2
  40.0 2.0 %collective-permute-start.3 = (bf16[144,512]{1,0:T(8,128)(2,1)}, bf16[144,512]{1,0:T(8,128)(2,1)S(1)}, u32[]{:S(2)}, u32[]{:S(2)}) collective-permute-start(bf16[144,512]{1,0:T(8,128)(2,1)} %get-tuple-element.76.refs_1_), channel_id=1, source_target_pairs={{0,3},{1,2},{2,1},{3,0},{4,7},{5,6},{6,5},{7,4},{8,11},{9,10},{10,... | collective-permute-start | bytes 442376 | tf_op jit(solution)/shard_map/ppermute | solution.py:764
  42.1 28.0 %short_windows.1 = (bf16[512,512]{1,0:T(8,128)(2,1)}, bf16[528,1024]{1,0:T(8,128)(2,1)}, bf16[512,512]{1,0:T(8,128)(2,1)}, bf16[512,512]{1,0:T(8,128)(2,1)}, bf1...) custom-call(s32[1,256]{1,0:T(1,128)} %bitcast.44, ...), custom_call_target="tpu_custom_call" | custom-call | flops 34359738368 | bytes 1048576 | tf_op jit(solution)/shard_map/short_windows/pallas_call | solution.py:74
  70.1 0.0 collective-permute-done.1.refs_2_
  70.1 0.0 collective-permute-done.2.refs_3_
  70.1 0.0 collective-permute-done.3.refs_4_
  70.1 0.0 copy-done.1
  70.1 0.0 copy-done.2
  70.1 0.3 combine0.1
  70.5 0.0 copy-start.4
  70.5 0.7 copy-done.4
  71.2 1.3 %collective-permute-start.4 = (bf16[80,512]{1,0:T(8,128)(2,1)S(1)}, bf16[80,512]{1,0:T(8,128)(2,1)S(1)}, u32[]{:S(2)}, u32[]{:S(2)}) collective-permute-start(bf16[80,512]{1,0:T(8,128)(2,1)S(1)} %get-tuple-element.77), channel_id=1, source_target_pairs={{0,4},{1,5},{2,6},{3,7},{4,0},{5,1},{6,2},{7,3},{8,12},{9,13},{10,... | collective-permute-start | bytes 245768 | tf_op jit(solution)/shard_map/ppermute | solution.py:764
  72.4 0.9 collective-permute-start.5
  73.3 2.2 %collective-permute-start.6 = (bf16[80,512]{1,0:T(8,128)(2,1)S(1)}, bf16[80,512]{1,0:T(8,128)(2,1)S(1)}, u32[]{:S(2)}, u32[]{:S(2)}) collective-permute-start(bf16[80,512]{1,0:T(8,128)(2,1)S(1)} %get-tuple-element.79), channel_id=1, source_target_pairs={{0,12},{1,13},{2,14},{3,15},{4,8},{5,9},{6,10},{7,11},{8,4},{9,5},... | collective-permute-start | bytes 245768 | tf_op jit(solution)/shard_map/ppermute | solution.py:764
  75.6 4.6 %short_grads.1 = (f32[1024,256]{1,0:T(8,128)}, f32[512,256]{1,0:T(8,128)}, f32[128,512]{1,0:T(8,128)}, f32[8,256]{1,0:T(8,128)}, f32[528,256]{1,0:T(8,128)}) custom-call(s32[1,256]{1,0:T(1,128)} %bitcast.45, f32[16,512]{1,0:T(8,128)} %get-tuple-element.84.refs_1_.refs_9_, bf16[1024,256]{1,0:T(8,128)(2,1)} %get-tuple-element.95.refs_4_.refs_2_.refs_21_, ...), custom_call_target="tpu_custom_call" | custom-call | flops 8589934592 | bytes 1048576 | tf_op jit(solution)/shard_map/short_grads/pallas_call | solution.py:74
  80.2 0.0 copy-done.8
  80.2 0.0 collective-permute-done.4.refs_1_
  80.2 0.0 copy-start.20
  80.2 0.9 collective-permute-done.5.refs_2_
  81.1 0.0 collective-permute-done.6.refs_3_
  81.1 0.0 copy-done.20
  81.1 0.6 copy-done.21
  81.7 0.0 copy-done.22
  81.8 16.6 %long_windows.1 = (f32[272,256]{1,0:T(8,128)}, bf16[256,512]{1,0:T(8,128)(2,1)}, bf16[2048,128]{1,0:T(8,128)(2,1)}, bf16[1792,128]{1,0:T(8,128)(2,1)}) custom-call(f32[64,512]{1,0:T(8,128)} %get-tuple-element.75.refs_0_.refs_11_, bf16[80,512]{1,0:T(8,128)(2,1)} %copy-done.20, bf16[80,512]{1,0:T(8,128)(2,1)} %copy-done.21, bf16[80,512]{1,0:T(8,128)(2,1)} %copy-done.22, ...), custom_call_target="tpu_custom_call" | custom-call | flops 34359738368 | bytes 1048576 | tf_op jit(solution)/shard_map/long_windows/pallas_call | solution.py:74
  98.4 0.1 collective-permute-start.7
  98.5 2.0 %collective-permute-done.7.refs_1_ = bf16[1792,128]{1,0:T(8,128)(2,1)S(1)} collective-permute-done((bf16[1792,128]{1,0:T(8,128)(2,1)}, bf16[1792,128]{1,0:T(8,128)(2,1)S(1)}, u32[]{:S(2)}, u32[]{:S(2)}) %collective-permute-start.7) | collective-permute-done | bytes 458784 | tf_op jit(solution)/shard_map/ppermute | solution.py:1184
  100.5 1.0 copy-done
  101.5 0.0 copy-start.9
  101.6 0.0 copy-start.10
  101.6 0.0 copy-start.11
  101.6 0.0 copy-start.12
  101.6 0.0 copy-start.13
  101.6 0.0 copy-start.14
  101.6 0.0 copy-start.15
  101.6 0.0 copy-start.16
  101.6 0.0 copy-start.17
  101.6 0.9 add.1
  102.5 3.6 %all-to-all-start.1 = ((bf16[16,128,128]{2,1,0:T(8,128)(2,1)}), bf16[16,128,128]{2,1,0:T(8,128)(2,1)S(1)}, u32[]{:S(2)}, u32[]{:S(2)}) async-start(bf16[16,128,128]{2,1,0:T(8,128)(2,1)} %bitcast.18), calls=%async_computation.1 | async-start | bytes 1048576 | tf_op jit(solution)/shard_map/all_to_all | solution.py:1192
  106.1 0.0 copy-done.3
  106.1 0.0 copy-done.5
  106.1 0.0 copy-done.6
  106.1 0.0 copy-done.7
  106.2 0.0 copy-done.9
  106.2 0.0 copy-done.10
  106.2 0.0 copy-done.11
  106.2 0.0 copy-done.12
  106.2 0.0 copy-done.13
  106.2 0.0 copy-done.14
  106.2 0.0 copy-done.15
  106.2 0.0 copy-done.16
  106.2 0.0 copy-done.17
  106.2 2.7 %outputs.1 = (bf16[128,256]{1,0:T(8,128)(2,1)}, f32[128,256]{1,0:T(8,128)S(1)}, bf16[256,256]{1,0:T(8,128)(2,1)}, f32[256,256]{1,0:T(8,128)}) custom-call(s32[1,256]{1,0:T(1,128)S(1)} %bitcast.47, bf16[512,256]{1,0:T(8,128)(2,1)S(1)} %copy-done.15, f32[8,256]{1,0:T(8,128)S(1)} %copy-done.17, bf16[128,256]{1,0:T(8,128)(2,1)S(1)} %bitcast.36, ...), custom_call_target="tpu_custom_call" | custom-call | flops 4294967296 | bytes 1048576 | tf_op jit(solution)/shard_map/outputs/pallas_call | solution.py:74
  109.0 12.6 %all-to-all-done.1 = bf16[16,128,128]{2,1,0:T(8,128)(2,1)S(1)} async-done(((bf16[16,128,128]{2,1,0:T(8,128)(2,1)}), bf16[16,128,128]{2,1,0:T(8,128)(2,1)S(1)}, u32[]{:S(2)}, u32[]{:S(2)}) %all-to-all-start.1) | async-done | bytes 524320 | tf_op jit(solution)/shard_map/all_to_all | solution.py:1192
  121.5 0.8 final.1
  (10 shorter events, 0.0 us)
Async XLA Ops:
  26.2 1.9 %copy-start.18 = (bf16[16,128,128]{2,1,0:T(8,128)(2,1)}, bf16[16,128,128]{2,1,0:T(8,128)(2,1)S(1)}, u32[]{:S(2)}) copy-start(bf16[16,128,128]{2,1,0:T(8,128)(2,1)S(1)} %all_to_all.22) | copy-start | bytes 1572868
  26.2 1.9 %collective-permute-start = (bf16[2048,128]{1,0:T(8,128)(2,1)S(1)}, bf16[2048,128]{1,0:T(8,128)(2,1)S(1)}, u32[]{:S(2)}, u32[]{:S(2)}) collective-permute-start(bf16[2048,128]{1,0:T(8,128)(2,1)S(1)} %bitcast.53), channel_id=1, source_target_pairs={{0,16},{16,0},{1,17},{17,1},{2,18},{18,2},{3,19},{19,3},{4,20},{20... | collective-permute-start | bytes 1572872 | tf_op jit(solution)/shard_map/ppermute | solution.py:1009
  28.1 0.8 copy-start.19
  38.5 31.6 %collective-permute-start.1 = (bf16[144,512]{1,0:T(8,128)(2,1)}, bf16[144,512]{1,0:T(8,128)(2,1)S(1)}, u32[]{:S(2)}, u32[]{:S(2)}) collective-permute-start(bf16[144,512]{1,0:T(8,128)(2,1)} %get-tuple-element.76.refs_1_), channel_id=1, source_target_pairs={{0,1},{1,0},{2,3},{3,2},{4,5},{5,4},{6,7},{7,6},{8,9},{9,8},{10,11... | collective-permute-start | bytes 442376 | tf_op jit(solution)/shard_map/ppermute | solution.py:764
  39.1 31.0 %collective-permute-start.2 = (bf16[144,512]{1,0:T(8,128)(2,1)}, bf16[144,512]{1,0:T(8,128)(2,1)S(1)}, u32[]{:S(2)}, u32[]{:S(2)}) collective-permute-start(bf16[144,512]{1,0:T(8,128)(2,1)} %get-tuple-element.76.refs_1_), channel_id=1, source_target_pairs={{0,2},{1,3},{2,0},{3,1},{4,6},{5,7},{6,4},{7,5},{8,10},{9,11},{10,... | collective-permute-start | bytes 442376 | tf_op jit(solution)/shard_map/ppermute | solution.py:764
  40.0 30.1 %collective-permute-start.3 = (bf16[144,512]{1,0:T(8,128)(2,1)}, bf16[144,512]{1,0:T(8,128)(2,1)S(1)}, u32[]{:S(2)}, u32[]{:S(2)}) collective-permute-start(bf16[144,512]{1,0:T(8,128)(2,1)} %get-tuple-element.76.refs_1_), channel_id=1, source_target_pairs={{0,3},{1,2},{2,1},{3,0},{4,7},{5,6},{6,5},{7,4},{8,11},{9,10},{10,... | collective-permute-start | bytes 442376 | tf_op jit(solution)/shard_map/ppermute | solution.py:764
  42.0 28.1 %copy-start.1 = (bf16[144,512]{1,0:T(8,128)(2,1)S(1)}, bf16[144,512]{1,0:T(8,128)(2,1)}, u32[]{:S(2)}) copy-start(bf16[144,512]{1,0:T(8,128)(2,1)} %get-tuple-element.76.refs_1_) | copy-start | bytes 442372
  42.0 28.1 %copy-start.2 = (f32[64,512]{1,0:T(8,128)S(1)}, f32[64,512]{1,0:T(8,128)}, u32[]{:S(2)}) copy-start(f32[64,512]{1,0:T(8,128)} %get-tuple-element.75.refs_0_.refs_11_) | copy-start | bytes 393220
  70.5 0.7 copy-start.4
  71.2 9.0 %copy-start.8 = (f32[16,512]{1,0:T(8,128)}, f32[16,512]{1,0:T(8,128)S(1)}, u32[]{:S(2)}) copy-start(f32[16,512]{1,0:T(8,128)S(1)} %get-tuple-element.81.refs_5_) | copy-start | bytes 98308
  71.2 9.0 %collective-permute-start.4 = (bf16[80,512]{1,0:T(8,128)(2,1)S(1)}, bf16[80,512]{1,0:T(8,128)(2,1)S(1)}, u32[]{:S(2)}, u32[]{:S(2)}) collective-permute-start(bf16[80,512]{1,0:T(8,128)(2,1)S(1)} %get-tuple-element.77), channel_id=1, source_target_pairs={{0,4},{1,5},{2,6},{3,7},{4,0},{5,1},{6,2},{7,3},{8,12},{9,13},{10,... | collective-permute-start | bytes 245768 | tf_op jit(solution)/shard_map/ppermute | solution.py:764
  72.4 8.6 %collective-permute-start.5 = (bf16[80,512]{1,0:T(8,128)(2,1)S(1)}, bf16[80,512]{1,0:T(8,128)(2,1)S(1)}, u32[]{:S(2)}, u32[]{:S(2)}) collective-permute-start(bf16[80,512]{1,0:T(8,128)(2,1)S(1)} %get-tuple-element.78), channel_id=1, source_target_pairs={{0,8},{1,9},{2,10},{3,11},{4,12},{5,13},{6,14},{7,15},{8,0},{9,1},... | collective-permute-start | bytes 245768 | tf_op jit(solution)/shard_map/ppermute | solution.py:764
  73.3 7.8 %collective-permute-start.6 = (bf16[80,512]{1,0:T(8,128)(2,1)S(1)}, bf16[80,512]{1,0:T(8,128)(2,1)S(1)}, u32[]{:S(2)}, u32[]{:S(2)}) collective-permute-start(bf16[80,512]{1,0:T(8,128)(2,1)S(1)} %get-tuple-element.79), channel_id=1, source_target_pairs={{0,12},{1,13},{2,14},{3,15},{4,8},{5,9},{6,10},{7,11},{8,4},{9,5},... | collective-permute-start | bytes 245768 | tf_op jit(solution)/shard_map/ppermute | solution.py:764
  80.2 0.9 copy-start.20
  81.1 0.6 copy-start.21
  81.1 0.7 copy-start.22
  98.4 2.1 %collective-permute-start.7 = (bf16[1792,128]{1,0:T(8,128)(2,1)}, bf16[1792,128]{1,0:T(8,128)(2,1)S(1)}, u32[]{:S(2)}, u32[]{:S(2)}) collective-permute-start(bf16[1792,128]{1,0:T(8,128)(2,1)} %get-tuple-element.119), channel_id=1, source_target_pairs={{0,16},{16,0},{1,17},{17,1},{2,18},{18,2},{3,19},{19,3},{4,20},{20... | collective-permute-start | bytes 1376264 | tf_op jit(solution)/shard_map/ppermute | solution.py:1184
  100.5 1.0 copy-start
  101.5 4.6 %copy-start.3 = (bf16[2,1,64,256]{3,2,1,0:T(8,128)(2,1)S(1)}, bf16[2,1,64,256]{3,2,1,0:T(8,128)(2,1)}, u32[]{:S(2)}) copy-start(bf16[2,1,64,256]{3,2,1,0:T(8,128)(2,1)} %param.17) | copy-start | bytes 196612
  101.5 4.6 %copy-start.5 = (bf16[2,1,128,256]{3,2,1,0:T(8,128)(2,1)S(1)}, bf16[2,1,128,256]{3,2,1,0:T(8,128)(2,1)}, u32[]{:S(2)}) copy-start(bf16[2,1,128,256]{3,2,1,0:T(8,128)(2,1)} %param.18) | copy-start | bytes 393220
  101.5 4.6 %copy-start.6 = (bf16[2,1,128,256]{3,2,1,0:T(8,128)(2,1)S(1)}, bf16[2,1,128,256]{3,2,1,0:T(8,128)(2,1)}, u32[]{:S(2)}) copy-start(bf16[2,1,128,256]{3,2,1,0:T(8,128)(2,1)} %param.20) | copy-start | bytes 393220
  101.5 4.6 %copy-start.7 = (bf16[2,1,64,256]{3,2,1,0:T(8,128)(2,1)S(1)}, bf16[2,1,64,256]{3,2,1,0:T(8,128)(2,1)}, u32[]{:S(2)}) copy-start(bf16[2,1,64,256]{3,2,1,0:T(8,128)(2,1)} %param.19) | copy-start | bytes 196612
  101.5 4.6 %copy-start.9 = (s32[256]{0:T(256)S(1)}, s32[256]{0:T(256)}, u32[]{:S(2)}) copy-start(s32[256]{0:T(256)} %param.23) | copy-start | bytes 3076
  101.6 4.6 %copy-start.10 = (s32[2,1,64]{2,1,0:T(1,128)S(1)}, s32[2,1,64]{2,1,0:T(1,128)}, u32[]{:S(2)}) copy-start(s32[2,1,64]{2,1,0:T(1,128)} %param.21) | copy-start | bytes 1540
  101.6 4.6 %copy-start.11 = (s32[2,1,128]{2,1,0:T(1,128)S(1)}, s32[2,1,128]{2,1,0:T(1,128)}, u32[]{:S(2)}) copy-start(s32[2,1,128]{2,1,0:T(1,128)} %param.22) | copy-start | bytes 3076
  101.6 4.6 %copy-start.12 = (f32[528,256]{1,0:T(8,128)S(1)}, f32[528,256]{1,0:T(8,128)}, u32[]{:S(2)}) copy-start(f32[528,256]{1,0:T(8,128)} %get-tuple-element.114.refs_12_) | copy-start | bytes 1622020
  101.6 4.6 %copy-start.13 = (bf16[512,512]{1,0:T(8,128)(2,1)S(1)}, bf16[512,512]{1,0:T(8,128)(2,1)}, u32[]{:S(2)}) copy-start(bf16[512,512]{1,0:T(8,128)(2,1)} %get-tuple-element.99.refs_3_.refs_11_) | copy-start | bytes 1572868
  101.6 4.6 %copy-start.14 = (f32[272,256]{1,0:T(8,128)S(1)}, f32[272,256]{1,0:T(8,128)}, u32[]{:S(2)}) copy-start(f32[272,256]{1,0:T(8,128)} %get-tuple-element.113.refs_7_) | copy-start | bytes 835588
  101.6 4.6 %copy-start.15 = (bf16[512,256]{1,0:T(8,128)(2,1)S(1)}, bf16[512,256]{1,0:T(8,128)(2,1)}, u32[]{:S(2)}) copy-start(bf16[512,256]{1,0:T(8,128)(2,1)} %get-tuple-element.73.refs_5_.refs_22_.refs_1_) | copy-start | bytes 786436
  101.6 4.6 %copy-start.16 = (bf16[256,512]{1,0:T(8,128)(2,1)S(1)}, bf16[256,512]{1,0:T(8,128)(2,1)}, u32[]{:S(2)}) copy-start(bf16[256,512]{1,0:T(8,128)(2,1)} %get-tuple-element.112.refs_6_) | copy-start | bytes 786436
  101.6 4.6 %copy-start.17 = (f32[8,256]{1,0:T(8,128)S(1)}, f32[8,256]{1,0:T(8,128)}, u32[]{:S(2)}) copy-start(f32[8,256]{1,0:T(8,128)} %get-tuple-element.74.refs_7_.refs_10_.refs_2_) | copy-start | bytes 24580
  102.5 19.0 %all-to-all-start.1 = ((bf16[16,128,128]{2,1,0:T(8,128)(2,1)}), bf16[16,128,128]{2,1,0:T(8,128)(2,1)S(1)}, u32[]{:S(2)}, u32[]{:S(2)}) async-start(bf16[16,128,128]{2,1,0:T(8,128)(2,1)} %bitcast.18), calls=%async_computation.1 | async-start | bytes 1048576 | tf_op jit(solution)/shard_map/all_to_all | solution.py:1192

commit v2 on v1

v2 whole, which is shorter than its diff:
```python
import functools
import types

import jax
import jax.numpy as jnp
from jax import lax
from jax.experimental import pallas as pl
from jax.experimental.pallas import tpu as pltpu
from jax.sharding import PartitionSpec as P

EPS = 1e-05
D, E, N, MB, HALO = 256, 512, 16, 2, 16
LT = 128
NP = N // 2
LOG2E = 1.4426950408889634
LN2 = 0.6931471805599453
F32, BF = jnp.float32, jnp.bfloat16
NT = (((1,), (1,)), ((), ()))
TN = (((0,), (0,)), ((), ()))
BOTH = ("dp", "seq")
IN_ROWS, OUT_ROWS, CH_ROWS = 32, 16, 16
PACK = 2 * IN_ROWS + 2 * OUT_ROWS + CH_ROWS
EDGE = 16
GATHER = PACK + 2 * EDGE
FAR = (8, 4)
SLOTS = (0, 8, 4, 12)
SUM_SLOTS = (0, 4, 8, 12)
AT_DT, AT_A, AT_SMALL = 48, 64, 96


def mm(a, b, dims=None):
    if dims is None:
        return jnp.dot(a, b, preferred_element_type=F32)
    return lax.dot_general(a, b, dims, preferred_element_type=F32)


def iota(shape, axis):
    return lax.broadcasted_iota(jnp.int32, shape, axis)


def onehot(cond):
    return jnp.where(cond, 1.0, 0.0).astype(BF)


def eye(n):
    return onehot(iota((n, n), 0) == iota((n, n), 1))


def split(x):
    hi = x.astype(BF)
    return hi, (x - hi.astype(F32)).astype(BF)


def silu_of_half(h):
    th = jnp.tanh(h)
    value = h * th + h
    u = 0.5 * th
    return value, (0.5 + u) + value * (0.5 - u)


def plus(total, x):
    return x if total is None else total + x


def loop(count, body):
    lax.fori_loop(0, count, lambda i, c: (body(i), c)[1], 0)


def run(name, body, ins, outs, scratch=None, flops=0, far=(), early=(), placed=(), vmem=60):
    scratch = dict(scratch or {}, **{k: outs[k] for k in early})
    scratch.update({k: (ins[k].shape, ins[k].dtype) for k in far})
    if far:
        scratch["in_sems"] = pltpu.SemaphoreType.DMA((len(far),))
    if early:
        scratch["out_sems"] = pltpu.SemaphoreType.DMA((len(early),))
    in_names, scratch_names = [k + "_far" if k in far else k for k in ins], list(scratch)
    out_names = [k + "_out" if k in early or k in placed else k for k in outs]

    def kernel(*refs):
        r = types.SimpleNamespace(**dict(zip(in_names + out_names + scratch_names, refs)))
        r.early, r.sent, r.fetched = tuple(early), [], []
        body(r)
        for copy in r.sent:
            copy.wait()

    def spec(key):
        return pl.BlockSpec(memory_space=pltpu.HBM if key in far else pltpu.VMEM)

    result = pl.pallas_call(
        kernel,
        out_shape=tuple(jax.ShapeDtypeStruct(*v) for v in outs.values()),
        in_specs=[spec(k) for k in ins],
        out_specs=tuple(
            pl.BlockSpec(memory_space=pltpu.HBM if k in early or k in placed else pltpu.VMEM)
            for k in outs
        ),
        scratch_shapes=[
            pltpu.VMEM(*scratch[k]) if isinstance(scratch[k], tuple) else scratch[k]
            for k in scratch_names
        ],
        compiler_params=pltpu.CompilerParams(vmem_limit_bytes=vmem << 20),
        cost_estimate=pl.CostEstimate(flops=flops, bytes_accessed=1 << 20, transcendentals=0),
        name=name,
    )(*ins.values())
    return dict(zip(outs, result))


def send(r, *names):
    for name in names:
        if name in r.early:
            copy = pltpu.make_async_copy(
                getattr(r, name), getattr(r, name + "_out"), r.out_sems.at[r.early.index(name)]
            )
            copy.start()
            r.sent.append(copy)


def fetch(r, *names):
    for name in names:
        copy = pltpu.make_async_copy(
            getattr(r, name + "_far"), getattr(r, name), r.in_sems.at[len(r.fetched)]
        )
        copy.start()
        r.fetched.append((name, copy))


def arrived(r, *names):
    for name, copy in r.fetched:
        if name in names:
            copy.wait()


def pack_body(r):
    r.rows[...] = jnp.zeros((8, CH_ROWS), F32)
    r.rows[0:4, :] = r.conv_w[...]
    r.rows[4:5, :] = r.conv_b[...]
    r.rows[5:6, :] = r.dt_b[...]
    r.rows[6:7, :] = r.skip[...]
    r.rows[7:8, 0 : r.gain.shape[1]] = r.gain[...]
    in_t = r.in_wT[...]
    small = jnp.concatenate(split(r.rows[...]), 0)

    def place(a, at, turned=False):
        n = a.shape[0 if turned else 1]
        return mm(a, onehot(iota((n, LT), 0) + at == iota((n, LT), 1)), TN if turned else None)

    a_hi, a_lo = split(r.a_log[...])
    chan = (
        place(r.x_w[...], 0)
        + place(r.dt_w[...], AT_DT, True)
        + place(a_hi, AT_A)
        + place(a_lo, AT_A + N)
        + place(small, AT_SMALL, True)
    ).astype(BF)
    out_w = r.out_w[...]
    for half in range(2):
        lanes = slice(half * LT, (half + 1) * LT)
        r.buf[half * IN_ROWS : (half + 1) * IN_ROWS, :] = in_t[:, lanes]
        low = 2 * IN_ROWS + half * OUT_ROWS
        r.buf[low : low + OUT_ROWS, :] = out_w[:, lanes]
    r.buf[PACK - CH_ROWS : PACK, :] = chan
    T = r.tok.shape[0] // MB
    for which, first in enumerate((T - 16, 0)):
        rows = [r.tok[mb * T + first : mb * T + first + 16, :].astype(F32) for mb in range(MB)]
        at = 12 if first else 0
        x = jnp.concatenate([x[at : at + 4] for x in rows], 0)
        r.buf[PACK + which * EDGE : PACK + (which + 1) * EDGE, :] = halves(x)


def halves(x):
    return jnp.concatenate([x[:, :LT], x[:, LT:]], 0).astype(BF)


def get_edges(buf, step, at):
    seq = lax.axis_index("seq")
    count = buf.shape[0] // step
    result = []
    before, after = jnp.maximum(seq - 1, 0), jnp.minimum(seq + 1, count - 1)
    for j, low, there in ((before, at[0], seq > 0), (after, at[1], seq < count - 1)):
        x = buf[pl.ds(pl.multiple_of(j * step + low, 16), EDGE), :].astype(F32)
        x = jnp.concatenate([x[:8], x[8:]], 1)
        result.append(jnp.where(there, x, 0.0))
    return result


def unpack(r):
    mine, seq = lax.axis_index("dp"), lax.axis_index("seq")
    count = E // (2 * OUT_ROWS)
    for near in range(4):
        for src, d in ((getattr(r, f"mine{near}"), mine), (getattr(r, f"other{near}"), 1 - mine)):
            for q, far in enumerate(SLOTS):
                at = q * GATHER
                dev = seq ^ (near | far)
                in_at = pl.multiple_of((d * count + dev) * IN_ROWS, IN_ROWS)
                out_at = pl.multiple_of((d * count + dev) * OUT_ROWS, OUT_ROWS)
                for half in range(2):
                    lanes = slice(half * LT, (half + 1) * LT)
                    r.inT[pl.ds(in_at, IN_ROWS), lanes] = src[
                        at + half * IN_ROWS : at + (half + 1) * IN_ROWS, :
                    ]
                    low = at + 2 * IN_ROWS + half * OUT_ROWS
                    r.outw[pl.ds(out_at, OUT_ROWS), lanes] = src[low : low + OUT_ROWS, :]
                r.pe[pl.ds(out_at, CH_ROWS), :] = src[at + PACK - CH_ROWS : at + PACK, :]
                if d is mine:
                    r.edges[pl.ds(pl.multiple_of(dev * 2 * EDGE, 2 * EDGE), 2 * EDGE), :] = src[
                        at + PACK : at + GATHER, :
                    ]
    r.edge[...] = jnp.concatenate(get_edges(r.edges, 2 * EDGE, (0, EDGE)), 0).astype(BF)


def join_body(r):
    rows = r.a.shape[0]
    r.both[0:rows, :] = r.a[...]
    r.both[rows:, :] = r.b[...]


def gather(buf):
    def swapped(x, mask):
        count = lax.axis_size("seq")
        return lax.ppermute(x, "seq", [(i, i ^ mask) for i in range(count)])

    for mask in FAR:
        buf = run(
            f"join{mask}",
            join_body,
            dict(a=buf, b=swapped(buf, mask)),
            dict(both=((2 * buf.shape[0], LT), BF)),
            vmem=8,
        )["both"]
    mine = [buf] + [swapped(buf, near) for near in range(1, 4)]
    other = [lax.ppermute(x, "dp", [(0, 1), (1, 0)]) for x in mine]
    return dict(
        {f"mine{i}": x for i, x in enumerate(mine)}, **{f"other{i}": x for i, x in enumerate(other)}
    )


def derive(r):
    peT = mm(eye(LT), r.pe[...], NT)
    small = peT[AT_SMALL : AT_SMALL + 8] + peT[AT_SMALL + 8 : AT_SMALL + 16]
    r.rowp[...] = small
    rate = -jnp.exp(peT[AT_A : AT_A + N] + peT[AT_A + N : AT_A + 2 * N])
    r.rate[...] = rate
    for n in range(N):
        r.r2[4 * n : 4 * n + 4, :] = jnp.broadcast_to(rate[n : n + 1] * LOG2E, (4, E))
    dt = peT[AT_DT : AT_DT + N]
    r.dtw2[...] = jnp.concatenate([dt, dt, jnp.zeros((LT - 2 * N, E), F32)], 0).astype(BF)
    r.xwT[...] = jnp.where(iota((LT, E), 0) < 3 * N, peT, 0.0).astype(BF)


def gain_of(r):
    per = E // (D // 8)
    low = mm(eye(LT), r.pe[...], NT)[AT_SMALL : AT_SMALL + 16].astype(BF)
    lane, col = iota((E, D), 0), iota((E, D), 1)
    pick = onehot(((lane // per) == (col // 8)) & ((lane % per) == (col % 8)))
    g = mm(low, pick)
    return g[0:8] + g[8:16]


def placing(T, transposed):
    shape = (2 * MB * T, 2 * MB * T)
    row, col = iota(shape, 1 if transposed else 0), iota(shape, 0 if transposed else 1)
    t, scan = row >> 2, row & 3
    turn = T.bit_length() - 1
    pos, src = col & (T - 1), col >> turn
    want = jnp.where(scan >= 2, T - 1 - t, t)
    return (src == scan) & (pos == want)


def gain_row(r):
    return r.gain[0:1, :] if r.gain.shape[0] == 1 else r.gain[7:8, :]


def normalise(tok):
    source = tok.astype(F32)
    scale = lax.rsqrt(jnp.mean(source * source, 1, keepdims=True) + EPS)
    return source, scale, source * scale


def swap_of(r):
    return onehot(iota((D, D), 0) == jnp.broadcast_to(r.comp[...], (D, D)))


def prep(r, T, halo, ready=None):
    R = 4 * T
    B = 64
    swap = swap_of(r)
    put = placing(T, False)
    mrow = jnp.concatenate([r.mask[0:1, :], r.mask[1:2, :]], 1)
    mrow = jnp.concatenate([mrow, mrow], 1)
    cot = r.cot[...]
    r.GR[...] = mm(
        onehot(put & (mrow != 0)), jnp.concatenate([cot, mm(cot, swap).astype(BF)], 0)
    ).astype(BF)
    _, _, unit = normalise(r.tok[...])
    if ready is not None:
        ready()
    gain = gain_row(r)
    normed = (unit * gain).astype(BF)
    r.V[HALO:, :] = mm(
        onehot(put), jnp.concatenate([normed, mm(normed, swap).astype(BF)], 0)
    ).astype(BF)
    if halo:
        hn = (normalise(r.edge[...])[2] * gain).astype(BF)
        r.V[0:HALO, :] = (
            mm(onehot(edge_place(False)), hn)
            + mm(onehot(edge_place(True)), mm(hn, swap).astype(BF))
        ).astype(BF)
        r.ip[0:HALO, :] = mm(r.V[0:HALO, :], r.inT[0:E, :], NT)
    else:
        r.V[0:HALO, :] = jnp.zeros((HALO, D), BF)
        r.ip[0:HALO, :] = jnp.zeros((HALO, E), F32)
    for c in range(0, E, 256):
        r.ip[HALO:, c : c + 256] = mm(r.V[HALO:, :], r.inT[c : c + 256, :], NT)
        r.silu[:, c : c + 256] = mm(r.V[HALO:, :], r.inT[E + c : E + c + 256, :], NT)
    for c in range(0, E, 256):
        r.gm[:, c : c + 256] = mm(r.GR[...], r.outw[c : c + 256, :], NT)
    w = [0.5 * r.rowp[k : k + 1, :] for k in range(5)]

    def first(i):
        r0 = pl.multiple_of(i * B, B)
        at = pl.ds(r0, B)
        x, mid = shifted(r.ip, r0, True, B)
        half = w[4] + w[0] * mid[8 : 8 + B] + w[1] * x[8 : 8 + B]
        half = half + w[2] * mid[HALO : HALO + B] + w[3] * x[HALO : HALO + B]
        inner, slope = silu_of_half(half)
        r.inner[at, :] = inner
        r.slope[at, :] = slope
        r.il[at, :] = inner.astype(BF)
        silu, slope = silu_of_half(0.5 * r.silu[at, :])
        r.silu[at, :] = silu
        r.gslope[at, :] = slope
        r.gm[at, :] = r.gm[at, :] * silu

    loop(R // B, first)
    sel = mm(r.il[...], r.pe[...])
    r.sel[...] = sel
    lane = iota((R, LT), 1)
    low = jnp.where(lane < N, sel, 0.0)
    hi = low.astype(BF).astype(F32)
    both = (hi + pltpu.roll(low - hi, N, 1)).astype(BF)
    for c in range(0, E, 256):
        r.st[:, c : c + 256] = mm(both, r.dtw2[:, c : c + 256])

    def second(i):
        at = pl.ds(pl.multiple_of(i * B, B), B)
        z = r.st[at, :] + r.rowp[5:6, :]
        u = jnp.exp2(jnp.abs(z) * -LOG2E)
        near = u * (1.0 - u * (0.5 - u * (1.0 / 3.0)))
        st = jnp.maximum(z, 0.0) + jnp.where(u < 0.01, near, jnp.log(1.0 + u))
        r.st[at, :] = st
        r.sz[at, :] = jnp.exp(z - st)
        r.si[at, :] = r.inner[at, :] * st

    loop(R // B, second)


B = 32


def shifted(ref, r0, before, B=B):
    x = ref[pl.ds(r0 + (0 if before else HALO), B + HALO), :]
    return x, pltpu.roll(x, 4 if before else B + HALO - 4, 0)


def edge_place(rev):
    row, col = iota((HALO, HALO), 0), iota((HALO, HALO), 1)
    j, scan = row >> 2, row & 3
    if rev:
        return (scan >= 2) & (col == 8 + (scan - 2) * 4 + (3 - j))
    return (scan < 2) & (col == scan * 4 + j)


def maps(r, T):
    R = 4 * T
    sel = r.sel[...]
    lane = iota((R, LT), 1)
    kept = jnp.where((lane >= N) & (lane < 3 * N), sel, 0.0)
    hi = kept.astype(BF).astype(F32)
    both = (hi + pltpu.roll(kept - hi, 64, 1)).astype(BF)
    G = 128
    r8, r4 = iota((2 * G, G), 0), iota((2 * G, G), 1)
    twice = onehot(((r8 >> 3) * 4 + (r8 & 3)) == r4)
    own = (iota((2 * G, LT), 1) & 1) == ((iota((2 * G, LT), 0) >> 2) & 1)
    l, c = iota((LT, NP * LT), 0), iota((LT, NP * LT), 1)
    l = l & 63
    spread_in = onehot((l >= N) & (l < 2 * N) & (((l - N) >> 1) == (c >> 7)))
    spread_out = onehot((l >= 2 * N) & (l < 3 * N) & (((l - 2 * N) >> 1) == (c >> 7)))
    for g in range(R // G):
        left = jnp.where(own, mm(twice, both[g * G : (g + 1) * G]), 0.0).astype(BF)
        r.imb[g * 2 * G : (g + 1) * 2 * G, :] = mm(left, spread_in)
        r.omb[g * 2 * G : (g + 1) * 2 * G, :] = mm(left, spread_out)


def dup(x, low):
    turned = pltpu.roll(x, 4, 0)
    return jnp.where(low, x, turned), jnp.where(low, turned, x)


def lanes_of(e):
    return slice(e * LT, (e + 1) * LT)


def scan_forward(r, T, start, full, U=16, tiles=range(E // LT)):
    low = iota((8, LT), 0) < 4
    for e in tiles:
        es = lanes_of(e)
        if start is None:
            first = tuple(jnp.zeros((8, LT), F32) for _ in range(NP))
        else:
            first = tuple(start[8 * k : 8 * k + 8, es] for k in range(NP))
        if full:
            for k in range(NP):
                r.states[0, 8 * k : 8 * k + 8, es] = first[k]

        def body(i, state):
            state = list(state)
            for u in range(U // 2):
                pair = i * (U // 2) + u
                row = pl.multiple_of(pair * 8, 8)
                st = dup(r.st[pl.ds(row, 8), es], low)
                si = dup(r.si[pl.ds(row, 8), es], low)
                ys = []
                for h in range(2):
                    t = pair * 2 + h
                    r8 = pl.multiple_of(t * 8, 8)
                    acc = None
                    for k in range(NP):
                        decay = jnp.exp2(st[h] * r.r2[8 * k : 8 * k + 8, es])
                        state[k] = decay * state[k] + si[h] * r.imb[pl.ds(r8, 8), lanes_of(k)]
                        if full:
                            r.states[t + 1, 8 * k : 8 * k + 8, es] = state[k]
                            y = state[k] * r.omb[pl.ds(r8, 8), lanes_of(k)]
                            acc = y if acc is None else acc + y
                    if full:
                        ys.append(acc + pltpu.roll(acc, 4, 0))
                if full:
                    r.mix[pl.ds(row, 8), es] = jnp.where(low, ys[0], ys[1])
            return tuple(state)

        last = lax.fori_loop(0, T // U, body, first)
        if not full:
            for k in range(NP):
                r.ends[8 * k : 8 * k + 8, es] = last[k]


def scan_adjoint_local(r, T, U=8, tiles=range(E // LT)):
    low = iota((8, LT), 0) < 4
    for e in tiles:
        es = lanes_of(e)

        def body(i, b):
            b = list(b)
            for u in range(U // 2):
                pair = T // 2 - 1 - (i * (U // 2) + u)
                row = pl.multiple_of(pair * 8, 8)
                st = dup(r.st[pl.ds(row, 8), es], low)
                gm = dup(r.gm[pl.ds(row, 8), es], low)
                for h in (1, 0):
                    r8 = pl.multiple_of((pair * 2 + h) * 8, 8)
                    for k in range(NP):
                        a = gm[h] * r.omb[pl.ds(r8, 8), lanes_of(k)] + b[k]
                        b[k] = jnp.exp2(st[h] * r.r2[8 * k : 8 * k + 8, es]) * a
            return tuple(b)

        last = lax.fori_loop(0, T // U, body, tuple(jnp.zeros((8, LT), F32) for _ in range(NP)))
        for k in range(NP):
            r.ends[64 + 8 * k : 64 + 8 * k + 8, es] = last[k]


def scan_backward(r, T, start, group=2, unroll=4):
    low = iota((8, LT), 0) < 4
    r.alog[...] = jnp.zeros((8 * NP, E), F32)
    r.b[...] = jnp.zeros((8 * NP, E), F32) if start is None else start[64:128, :]
    groups = E // LT // group
    for g in range(groups):
        tiles = [lanes_of(g * group + e) for e in range(group)]

        def body(i, g=g, tiles=tiles):
            for u in range(unroll):
                pair = T // 2 - 1 - (i * unroll + u)
                row = pl.multiple_of(pair * 8, 8)
                r16 = pl.multiple_of(pair * 16, 16)
                st = [dup(r.st[pl.ds(row, 8), es], low) for es in tiles]
                si = [dup(r.si[pl.ds(row, 8), es], low) for es in tiles]
                gm = [dup(r.gm[pl.ds(row, 8), es], low) for es in tiles]
                q = [[None, None] for _ in tiles]
                p = [[None, None] for _ in tiles]
                for k in range(NP):
                    ks = slice(8 * k, 8 * k + 8)
                    im = [r.imb[pl.ds(r16 + 8 * h, 8), lanes_of(k)] for h in range(2)]
                    om = [r.omb[pl.ds(r16 + 8 * h, 8), lanes_of(k)] for h in range(2)]
                    xi, xo = [None, None], [None, None]
                    for e, es in enumerate(tiles):
                        rk = r.r2[ks, es]
                        b = r.b[ks, es]
                        states = [r.states[2 * pair + h, ks, es] for h in range(3)]
                        rates = None
                        for h in (1, 0):
                            a = gm[e][h] * om[h] + b
                            b = jnp.exp2(st[e][h] * rk) * a
                            w = b * states[h]
                            q[e][h] = plus(q[e][h], w * rk)
                            rates = plus(rates, w * st[e][h])
                            p[e][h] = plus(p[e][h], a * im[h])
                            xi[h] = plus(xi[h], a * si[e][h])
                            xo[h] = plus(xo[h], states[h + 1] * gm[e][h])
                        r.b[ks, es] = b
                        r.alog[ks, es] += rates
                    cs = lanes_of(g * NP + k)
                    r.xi[pl.ds(r16, 16), cs] = jnp.concatenate(xi, 0).astype(BF)
                    r.xo[pl.ds(r16, 16), cs] = jnp.concatenate(xo, 0).astype(BF)
                for e, es in enumerate(tiles):
                    for out, v in ((r.q, q[e]), (r.p, p[e])):
                        v = [x + pltpu.roll(x, 4, 0) for x in v]
                        out[pl.ds(row, 8), es] = jnp.where(low, v[0], v[1])

        loop(T // 2 // unroll, body)
    rl, rc = iota((NP * LT, LT), 0), iota((NP * LT, LT), 1)
    red = onehot((rl >> 7) == (rc >> 1))
    W = NP * LT
    for out, x in ((r.yi, r.xi), (r.yo, r.xo)):
        total = x[:, :W]
        for g in range(1, groups):
            total = total + x[:, g * W : (g + 1) * W]
        out[...] = mm(total, red)
    G = 256
    own = (iota((G, LT), 1) & 1) == ((iota((G, LT), 0) >> 2) & 1)
    valid = own & (iota((G, LT), 1) < N)
    r8, r4 = iota((G // 2, G), 1), iota((G // 2, G), 0)
    fold = onehot(((r8 >> 3) * 4 + (r8 & 3)) == r4)
    for g in range(8 * T // G):
        at = slice(g * G, (g + 1) * G)
        y = pltpu.roll(jnp.where(valid, r.yi[at, :], 0.0), N, 1) + pltpu.roll(
            jnp.where(valid, r.yo[at, :], 0.0), 2 * N, 1
        )
        hi, lo = split(y)
        r.gsel[g * G // 2 : (g + 1) * G // 2, :] = mm(fold, hi) + mm(fold, lo)


def scan_scratch(T):
    return dict(
        states=((T + 1, 8 * NP, E), F32),
        imb=((8 * T, NP * LT), F32),
        omb=((8 * T, NP * LT), F32),
        xi=((8 * T, 2 * NP * LT), BF),
        xo=((8 * T, 2 * NP * LT), BF),
        b=((8 * NP, E), F32),
        yi=((8 * T, LT), F32),
        yo=((8 * T, LT), F32),
        mix=((4 * T, E), F32),
        q=((4 * T, E), F32),
        p=((4 * T, E), F32),
        alog=((8 * NP, E), F32),
        gsel=((4 * T, LT), F32),
    )


LATE = ("ip", "inner", "slope", "silu", "gslope", "sz", "V", "GR", "xwT", "rate")
LATE_LONG = LATE + ("inT", "outw", "dtw2")


def post(r, T, halo):
    R = 4 * T
    r.acc[...] = jnp.zeros((64, E), F32)
    arrived(r, *LATE)
    for c in range(0, E, 256):
        r.gg[:, c : c + 256] = mm(r.GR[...], r.outw[c : c + 256, :], NT)

    def first(i):
        at = pl.ds(pl.multiple_of(i * B, B), B)
        gp_at = pl.ds(pl.multiple_of(HALO + i * B, 16), B)
        for e in range(E // LT):
            es = lanes_of(e)
            skip = r.rowp[6:7, es]
            inner, gm, p = r.inner[at, es], r.gm[at, es], r.p[at, es]
            mixed = r.mix[at, es] + skip * inner
            r.il[at, es] = inner.astype(BF)
            r.gated[at, es] = (mixed * r.silu[at, es]).astype(BF)
            gate = r.gg[at, es] * mixed * r.gslope[at, es]
            r.gp[gp_at, E + e * LT : E + (e + 1) * LT] = gate.astype(BF)
            r.gz[at, es] = ((r.q[at, es] * LN2 + inner * p) * r.sz[at, es]).astype(BF)
            r.acc[48:56, es] += fold8(gm * inner)
            r.gg[at, es] = r.st[at, es] * p + gm * skip

    loop(R // B, first)
    lane = iota((R, LT), 1)
    gs_low = jnp.where(lane < N, mm(r.gz[...], r.dtw2[...], NT), r.gsel[...])
    gs_low = jnp.where(lane < 3 * N, gs_low, 0.0)
    r.z[...] = (
        gs_low
        + jnp.where((lane >= AT_DT) & (lane < AT_DT + N), pltpu.roll(r.sel[...], AT_DT, 1), 0.0)
        + jnp.where(lane == AT_SMALL + 5, 1.0, 0.0)
    ).astype(BF)
    gsb = gs_low.astype(BF)
    for c in range(0, E, 256):
        r.mix[:, c : c + 256] = mm(gsb, r.xwT[:, c : c + 256])
    r.gco[0:HALO, :] = jnp.zeros((HALO, E), F32)
    r.gco[HALO + R :, :] = jnp.zeros((HALO, E), F32)

    def second(i):
        r0 = pl.multiple_of(i * B, B)
        at = pl.ds(r0, B)
        x, mid = shifted(r.ip, r0, True)
        gco = (r.gg[at, :] + r.mix[at, :]) * r.slope[at, :]
        r.gco[pl.ds(r0 + HALO, B), :] = gco
        taps = (mid[8 : 8 + B], x[8 : 8 + B], mid[HALO : HALO + B], x[HALO : HALO + B])
        for k, v in enumerate(taps):
            r.acc[8 * k : 8 * k + 8, :] += fold8(gco * v)
        r.acc[32:40, :] += fold8(gco)

    loop(R // B, second)
    w = [r.rowp[k : k + 1, :] for k in range(4)]

    def third(i):
        r0 = pl.multiple_of(i * B, B)
        x, mid = shifted(r.gco, r0, False)
        rows = w[3] * x[0:B] + w[2] * mid[0:B] + w[1] * x[8 : 8 + B] + w[0] * mid[8 : 8 + B]
        r.gp[pl.ds(pl.multiple_of(r0 + HALO, 16), B), :E] = rows.astype(BF)

    loop(R // B, third)
    if halo:
        x = r.gco[0 : 2 * HALO, :]
        mid = pltpu.roll(x, 2 * HALO - 4, 0)
        rows = w[3] * x[0:16] + w[2] * mid[0:16] + w[1] * x[8:24] + w[0] * mid[8:24]
        r.gp[0:HALO, :E] = rows.astype(BF)
        r.gp[0:HALO, E:] = jnp.zeros((HALO, E), BF)
    else:
        r.gp[0:HALO, :] = jnp.zeros((HALO, 2 * E), BF)


def fold8(x):
    result = x[0:8]
    for j in range(8, x.shape[0], 8):
        result = result + x[j : j + 8]
    return result


def param_grads(r):
    zT = mm(eye(LT), r.z[...], NT).astype(BF)
    row = iota((LT, E), 0)
    peT = jnp.where(row < AT_DT, mm(zT, r.il[...]), 0.0)
    from_gz = ((row >= AT_DT) & (row < AT_A)) | (row == AT_SMALL + 5)
    peT = peT + jnp.where(from_gz, mm(zT, r.gz[...]), 0.0)
    rr, cc = iota((LT, 64), 0), iota((LT, 64), 1)
    hi, lo = split(r.alog[...])
    fold = onehot((rr >= AT_A) & (rr - AT_A == (cc >> 2)))
    rate = jnp.concatenate(
        [jnp.zeros((AT_A, E), F32), r.rate[...], jnp.zeros((LT - AT_A - N, E), F32)], 0
    )
    peT = peT + (mm(fold, hi) + mm(fold, lo)) * rate
    hi, lo = split(r.acc[...])
    fold = onehot((rr >= AT_SMALL) & (rr - AT_SMALL == (cc >> 3)))
    r.g_peT[...] = peT + mm(fold, hi) + mm(fold, lo)
    r.g_out[...] = mm(r.gated[...], r.GR[...], TN)
    for c in range(0, 2 * E, 256):
        r.g_inT[c : c + 256, :] = mm(r.gp[:, c : c + 256], r.V[...], TN)
    rows = mm(r.gp[...], r.inT[...])
    r.rows[...] = rows
    term = rows * r.V[...].astype(F32)
    first = (iota(term.shape, 0) & 3) < 2
    fwd = jnp.sum(jnp.where(first, term, 0.0), 0, keepdims=True)
    rev = jnp.sum(jnp.where(first, 0.0, term), 0, keepdims=True)
    both = jnp.concatenate([fwd, rev, jnp.zeros((6, D), F32)], 0)
    hi, lo = split(both)
    swap = swap_of(r)
    r.g_gain[...] = both + pltpu.roll(mm(hi, swap) + mm(lo, swap), 7, 0)


def edge_delta(r):
    swap = swap_of(r)
    hi, lo = split(r.rows[0:HALO, :])
    grad = jnp.where(
        (iota((HALO, D), 0) & 3) < 2, r.rows[0:HALO, :], mm(hi, swap) + mm(lo, swap)
    )
    _, scale, unit = normalise(mm(onehot(edge_place(False) | edge_place(True)), r.edge[...]))
    g = grad * gain_row(r)
    return scale * (g - unit * jnp.mean(g * unit, 1, keepdims=True))


def window_outputs(r, tok, cot, mask, gated, rows, out, ing):
    half = tok.shape[0]
    T = half // MB
    gain = gain_row(r)
    swap = swap_of(r)
    back = onehot(placing(T, True))
    g = mm(back, gated[...]).astype(BF)
    source, scale, unit = normalise(tok[...])
    outs = mm(r.outw[...], swap).astype(BF)
    out[...] = (source + mm(g[:half], r.outw[...]) + mm(g[half:], outs)).astype(BF)
    hi, lo = split(rows[HALO:, :])
    grad = (
        mm(back[:half], hi)
        + mm(back[:half], lo)
        + mm(back[half:], mm(hi, swap).astype(BF))
        + mm(back[half:], mm(lo, swap).astype(BF))
    )
    g = grad * gain
    mrow = jnp.concatenate([mask[0:1, :], mask[1:2, :]], 1)
    keep = onehot((iota((half, half), 0) == iota((half, half), 1)) & (mrow != 0))
    ing[...] = scale * (g - unit * jnp.mean(g * unit, 1, keepdims=True)) + mm(keep, cot[...])


def outputs_body(r):
    window_outputs(r, r.l_tok, r.l_cot, r.l_mask, r.l_gated, r.l_rows, r.l_out, r.l_ing)
    window_outputs(r, r.s_tok, r.s_cot, r.s_mask, r.s_gated, r.s_rows, r.s_out, r.s_ing)
    r.mark[...] = jnp.zeros((8, LT), F32)


def post_scratch(T):
    R = 4 * T
    return dict(
        acc=((64, E), F32),
        gg=((R, E), F32),
        gco=((R + 2 * HALO, E), F32),
        il=((R, E), BF),
        gated=((R, E), BF),
        gz=((R, E), BF),
        z=((R, LT), BF),
        gp=((R + HALO, 2 * E), BF),
    )


GRADS = dict(
    g_inT=((2 * E, D), F32), g_out=((E, D), F32), g_peT=((LT, E), F32), g_gain=((8, D), F32)
)


def rows_out(T):
    return dict(rows=((4 * T + HALO, D), F32))


STATE_ROWS = 4 * 8 * NP
ELEMENT = STATE_ROWS + 4 * 8


def to_spans(r, at, rows):
    seq = lax.axis_index("seq")
    count = r.carry_out.shape[0] // ELEMENT

    def start(j):
        dst = r.carry_out.at[pl.ds(pl.multiple_of(j * ELEMENT + at, 32), rows), :]

        @pl.when(j > seq)
        def _():
            pltpu.make_async_copy(r.later.at[at : at + rows, :], dst, r.carry_sem).start()

        @pl.when(j <= seq)
        def _():
            pltpu.make_async_copy(r.earlier.at[at : at + rows, :], dst, r.carry_sem).start()

    loop(count, start)


def send_sums(r, T):
    def add(i, total):
        return total + r.st[pl.ds(pl.multiple_of(i * 8, 8), 8), :]

    sums = lax.fori_loop(0, T // 2, add, jnp.zeros((8, E), F32))
    sums = sums + pltpu.roll(sums, 4, 0)
    sums = jnp.concatenate([sums[:, lanes_of(e)] for e in range(E // LT)], 0).astype(BF)
    r.later[STATE_ROWS:, :] = sums
    r.earlier[STATE_ROWS:, :] = sums
    to_spans(r, STATE_ROWS, 32)


def send_elements(r, e):
    normed = (iota((8 * NP, LT), 0) & 3) < 2
    state, adjoint = r.ends[0:64, lanes_of(e)], r.ends[64:128, lanes_of(e)]
    at = 64 * e
    r.later[at : at + 64, :] = jnp.where(normed, state, adjoint).astype(BF)
    r.earlier[at : at + 64, :] = jnp.where(normed, adjoint, state).astype(BF)
    to_spans(r, at, 64)


def wait_elements(r):
    pltpu.make_async_copy(r.carry_out, r.carry_out, r.carry_sem).wait()


def enter(r):
    seq = lax.axis_index("seq")
    count = r.elements.shape[0] // ELEMENT
    r.fold[...] = jnp.zeros((16 * NP, E), F32)

    def add(half, j):
        base = j * ELEMENT
        sums = r.elements[pl.ds(pl.multiple_of(base + STATE_ROWS, 32), 32), :].astype(F32)
        for e in range(E // LT):
            es = lanes_of(e)
            x = r.elements[pl.ds(pl.multiple_of(base + e * 64, 32), 64), :].astype(F32)
            for k in range(NP):
                ks = slice(8 * k, 8 * k + 8)
                at = slice(64 * half + 8 * k, 64 * half + 8 * k + 8)
                decay = jnp.exp2(r.r2[ks, es] * sums[8 * e : 8 * e + 8])
                r.fold[at, es] = decay * r.fold[at, es] + x[ks]

    loop(seq, lambda i: add(0, i))
    loop(count - 1 - seq, lambda i: add(1, count - 1 - i))
    normed = (iota((8 * NP, E), 0) & 3) < 2
    r.entering[0:64, :] = jnp.where(normed, r.fold[0:64, :], r.fold[64:128, :])
    r.entering[64:128, :] = jnp.where(normed, r.fold[64:128, :], r.fold[0:64, :])


def long_start_body(r, T, packed):

    def ready():
        if packed:
            unpack(r)
            r.gain[...] = gain_of(r)
        derive(r)
        send(r, *(k for k in r.early if k not in PREP_OUTS))

    prep(r, T, True, ready)
    send(r, *PREP_OUTS)
    maps(r, T)
    send_sums(r, T)
    for e in range(E // LT):
        scan_forward(r, T, None, False, tiles=(e,))
        scan_adjoint_local(r, T, tiles=(e,))
        send_elements(r, e)
    wait_elements(r)


def short_windows_body(r, T):
    prep(r, T, False)
    maps(r, T)
    scan_forward(r, T, None, True)
    scan_backward(r, T, None)
    post(r, T, False)
    param_grads(r)


FROM_SHORT = ("s_inT", "s_out", "s_peT", "s_gain")
LONG_FIRST = ("sel", "elements", "r2", "st", "si", "gm")
LONG_FAR = LONG_FIRST + LATE_LONG + FROM_SHORT


def long_windows_body(r, T):
    fetch(r, *LONG_FIRST)
    arrived(r, "sel")
    maps(r, T)
    arrived(r, "elements", "r2")
    enter(r)
    arrived(r, "st", "si", "gm")
    fetch(r, *LATE_LONG, *FROM_SHORT)
    scan_forward(r, T, r.entering, True)
    scan_backward(r, T, r.entering)
    arrived(r, "inT", "outw", "dtw2")
    post(r, T, True)
    param_grads(r)
    arrived(r, *FROM_SHORT)
    finish_grads(r)


def finish_grads(r):
    r.g_peT[...] += r.s_peT[...]
    r.g_gain[...] = (r.g_gain[...] + r.s_gain[...]) / gain_row(r)
    if not hasattr(r, "give"):
        r.g_inT[...] += r.s_inT[...]
        r.g_out[...] += r.s_out[...]
        r.delta[...] = edge_delta(r)
        return
    lane, col = iota((D, E), 1), iota((D, E), 0)
    pick = onehot(((lane // 16) == (col // 8)) & ((lane % 16) == (col % 8)))
    peT = r.g_peT[...] + jnp.where(
        iota((LT, E), 0) == AT_SMALL + 7, mm(r.g_gain[0:1, :].astype(BF), pick), 0.0
    )
    r.pe_out[...] = peT.T.astype(BF)
    mine, seq = lax.axis_index("dp"), lax.axis_index("seq")
    count = E // (2 * OUT_ROWS)
    delta = edge_delta(r).astype(BF)
    row, col = iota((8, HALO), 0), iota((8, HALO), 1)
    of = 4 * (row & 3) + (row >> 2)
    r.deltas[0:EDGE, :] = halves(mm(onehot(col == of), delta))
    r.deltas[EDGE:, :] = halves(mm(onehot(col == of + 2), delta))
    slots = [(4 * near + q, seq ^ (near | far)) for near in range(4) for q, far in enumerate(SUM_SLOTS)]
    for dst, d, step in ((r.give, 1 - mine, PACK), (r.keep, mine, GATHER)):
        for slot, dev in slots:
            at = slot * step
            in_at = pl.multiple_of((d * count + dev) * IN_ROWS, IN_ROWS)
            out_at = pl.multiple_of((d * count + dev) * OUT_ROWS, OUT_ROWS)
            for half in range(2):
                lanes = slice(half * LT, (half + 1) * LT)
                rows = pl.ds(in_at, IN_ROWS)
                dst[at + half * IN_ROWS : at + (half + 1) * IN_ROWS, :] = (
                    r.g_inT[rows, lanes] + r.s_inT[rows, lanes]
                ).astype(BF)
                low = at + 2 * IN_ROWS + half * OUT_ROWS
                rows = pl.ds(out_at, OUT_ROWS)
                dst[low : low + OUT_ROWS, :] = (r.g_out[rows, lanes] + r.s_out[rows, lanes]).astype(BF)
            dst[at + PACK - CH_ROWS : at + PACK, :] = r.pe_out[pl.ds(out_at, CH_ROWS), :]
    zero = jnp.zeros((EDGE, LT), BF)
    for slot, dev in slots:
        at = slot * GATHER + PACK
        r.keep[at : at + EDGE, :] = jnp.where(dev == seq - 1, r.deltas[0:EDGE, :], zero)
        r.keep[at + EDGE : at + 2 * EDGE, :] = jnp.where(dev == seq + 1, r.deltas[EDGE:, :], zero)


def total(*parts):
    result = parts[0].astype(F32)
    for x in parts[1:]:
        result = result + x.astype(F32)
    return result


def add_core_body(r):
    fetch(r, "keep")
    arrived(r, "keep")
    for near in range(4):
        part = getattr(r, f"part{near}")
        for q in range(4):
            at, keep, got = q * GATHER, (4 * near + q) * GATHER, (4 * near + q) * PACK
            part[at : at + PACK, :] = total(
                r.keep[keep : keep + PACK, :], r.got[got : got + PACK, :]
            ).astype(BF)
            part[at + PACK : at + GATHER, :] = r.keep[keep + PACK : keep + GATHER, :]


def add_near_body(r):
    for i, dst in enumerate((r.low, r.high)):
        at = slice(i * 2 * GATHER, (i + 1) * 2 * GATHER)
        dst[...] = total(r.part0[at, :], r.got1[at, :], r.got2[at, :], r.got3[at, :]).astype(BF)


def add_far_body(r):
    r.own[...] = total(r.low[0:GATHER, :], r.got[0:GATHER, :]).astype(BF)
    r.last[...] = total(r.low[GATHER:, :], r.got[GATHER:, :]).astype(BF)


def scatter(give, keep, after):
    def swapped(x, mask):
        count = lax.axis_size("seq")
        return lax.ppermute(x, "seq", [(i, i ^ mask) for i in range(count)])

    got = lax.ppermute(give, "dp", [(0, 1), (1, 0)])
    four = ((4 * GATHER, LT), BF)
    parts = run(
        "add_core",
        add_core_body,
        dict(got=got, keep=keep),
        {f"part{i}": four for i in range(4)},
        far=("keep",),
        vmem=8,
    )
    near = {f"got{i}": swapped(parts[f"part{i}"], i) for i in range(1, 4)}
    two = ((2 * GATHER, LT), BF)
    sums = run(
        "add_near",
        add_near_body,
        dict(part0=parts["part0"], after=after, **near),
        dict(low=two, high=two),
        vmem=8,
    )
    one = ((GATHER, LT), BF)
    ends = run(
        "add_far",
        add_far_body,
        dict(low=sums["low"], got=swapped(sums["high"], 8)),
        dict(own=one, last=one),
        vmem=8,
    )
    return ends["own"], swapped(ends["last"], 4)


def final_body(r, packed):
    r.grad[...] = r.ing[...]
    T = r.grad.shape[0] // MB
    if packed:
        block = total(r.own[...], r.got[...])
        from_next, from_prev = (
            jnp.concatenate([x[:8], x[8:]], 1)
            for x in (block[PACK : PACK + EDGE], block[PACK + EDGE :])
        )
    else:
        from_prev, from_next = r.from_prev[...], r.from_next[...]
    for mb in range(MB):
        for j in range(4):
            prev = 4 * mb + j if packed else 4 * j + 2 + mb
            follow = 4 * mb + j if packed else 4 * j + mb
            row = mb * T + T - 4 + j
            r.grad[row : row + 1, :] += from_next[follow : follow + 1, :]
            row = mb * T + 3 - j
            r.grad[row : row + 1, :] += from_prev[prev : prev + 1, :]
    if not packed:
        return
    for half in range(2):
        lanes = slice(half * LT, (half + 1) * LT)
        r.in_wT[:, lanes] = block[half * IN_ROWS : (half + 1) * IN_ROWS]
        low = 2 * IN_ROWS + half * OUT_ROWS
        r.out_w[:, lanes] = block[low : low + OUT_ROWS]
    pe = block[PACK - CH_ROWS : PACK]
    hi, lo = split(pe)
    peT = mm(eye(LT), hi, NT) + mm(eye(LT), lo, NT)
    r.x_w[...] = pe[:, : 3 * N]
    r.a_log[...] = pe[:, AT_A : AT_A + N]
    r.dt_w[...] = peT[AT_DT : AT_DT + N]
    small = peT[AT_SMALL : AT_SMALL + 8]
    r.conv_w[...] = small[0:4]
    r.conv_b[...] = small[4:5]
    r.dt_b[...] = small[5:6]
    r.skip[...] = small[6:7]
    r.gain[...] = small[7:8, 0 : r.gain.shape[1]]


PREP_OUTS = ("V", "GR", "ip", "inner", "slope", "silu", "gslope", "st", "sz", "si", "gm", "sel")


def prep_outs(T):
    R = 4 * T
    wide = ((R, E), F32)
    return dict(
        V=((R + HALO, D), BF),
        GR=((R, D), BF),
        ip=((R + HALO, E), F32),
        inner=wide,
        slope=wide,
        silu=wide,
        gslope=wide,
        st=wide,
        sz=wide,
        si=wide,
        gm=wide,
        sel=((R, LT), F32),
    )


def local(
    long_tokens,
    short_tokens,
    long_cotangent,
    short_cotangent,
    long_mask,
    short_mask,
    complement,
    norm_gain,
    in_weight,
    conv_weight,
    conv_bias,
    x_weight,
    dt_weight,
    dt_bias,
    a_log,
    d_skip,
    out_weight,
):
    count = lax.axis_size("seq")
    span, short = long_tokens.shape[2], short_tokens.shape[2]
    packed = count == 16 and out_weight.shape[0] == OUT_ROWS and in_weight.shape[1] == IN_ROWS
    comp = complement.reshape(1, D)
    up = [(i, i + 1) for i in range(count - 1)]
    down = [(i + 1, i) for i in range(count - 1)]

    if packed:
        buf = run(
            "pack",
            pack_body,
            dict(
                gain=norm_gain.reshape(1, -1),
                in_wT=in_weight.T,
                conv_w=conv_weight,
                conv_b=conv_bias.reshape(1, -1),
                x_w=x_weight,
                dt_w=dt_weight,
                dt_b=dt_bias.reshape(1, -1),
                a_log=a_log,
                skip=d_skip.reshape(1, -1),
                out_w=out_weight,
                tok=long_tokens.reshape(MB * span, D),
            ),
            dict(buf=((GATHER, LT), BF)),
            dict(rows=((8, CH_ROWS), F32)),
        )["buf"]
        weights_in = gather(buf)
    else:
        tail = lax.ppermute(long_tokens[:, 0, span - 4 :, :].reshape(8, D), "seq", up)
        head = lax.ppermute(long_tokens[:, 0, :4, :].reshape(8, D), "seq", down)

        def whole(a, axis):
            return lax.all_gather(a, BOTH, axis=axis, tiled=True)

        small = jnp.stack([*conv_weight, conv_bias, dt_bias, d_skip, jnp.zeros_like(d_skip)])
        columns = jnp.concatenate([a_log, small.T], 1)
        hi = columns.astype(BF)
        lo = (columns - hi.astype(F32)).astype(BF)
        zero = jnp.zeros((columns.shape[0], LT - AT_SMALL - 16), BF)
        chan = jnp.concatenate(
            [x_weight, dt_weight.T, hi[:, :N], lo[:, :N], hi[:, N:], lo[:, N:], zero], 1
        )
        weights_in = dict(
            inT=whole(in_weight.T, 0),
            outw=whole(out_weight, 0),
            pe=whole(chan, 0),
            gain=whole(norm_gain, 0).reshape(1, D),
            edge=jnp.concatenate([tail, head], 0),
        )

    def tokens_of(tok, cot, mask):
        T = tok.shape[2]
        return dict(
            tok=tok.reshape(MB * T, D), cot=cot.reshape(MB * T, D), mask=mask.reshape(MB, T)
        )

    long_in = tokens_of(long_tokens, long_cotangent, long_mask)
    short_in = tokens_of(short_tokens, short_cotangent, short_mask)

    derived = dict(
        r2=((8 * NP, E), F32),
        rowp=((8, E), F32),
        rate=((N, E), F32),
        dtw2=((LT, E), BF),
        xwT=((LT, E), BF),
    )
    unpacked = dict(
        inT=((2 * E, D), BF),
        outw=((E, D), BF),
        pe=((E, LT), BF),
        gain=((8, D), F32),
        edge=((HALO, D), BF),
    )
    started = run(
        "long_start",
        functools.partial(long_start_body, T=span, packed=packed),
        dict(comp=comp, **long_in, **weights_in),
        dict(
            carry=((count * ELEMENT, LT), BF), **prep_outs(span), **derived, **(unpacked if packed else {})
        ),
        dict(
            il=((4 * span, E), BF),
            imb=((8 * span, NP * LT), F32),
            omb=((8 * span, NP * LT), F32),
            ends=((128, E), F32),
            later=((ELEMENT, LT), BF),
            earlier=((ELEMENT, LT), BF),
            carry_sem=pltpu.SemaphoreType.DMA,
            **(dict(edges=((count * 2 * EDGE, LT), BF)) if packed else {}),
        ),
        flops=1 << 33,
        early=PREP_OUTS + tuple(derived) + (tuple(unpacked) if packed else ()),
        placed=("carry",),
        vmem=62,
    )
    weights = {k: started[k] for k in derived}
    for k in unpacked:
        weights[k] = started[k] if packed else weights_in[k]

    elements = lax.all_to_all(started["carry"], "seq", 0, 0, tiled=True)
    shorts = run(
        "short_windows",
        functools.partial(short_windows_body, T=short),
        dict(
            comp=comp,
            **short_in,
            **{
                k: weights[k]
                for k in ("inT", "outw", "pe", "gain", "dtw2", "xwT", "rowp", "r2", "rate")
            },
        ),
        dict(GRADS, **rows_out(short), gated=((4 * short, E), BF)),
        {
            k: v
            for k, v in dict(scan_scratch(short), **post_scratch(short), **prep_outs(short)).items()
            if k != "gated"
        },
        flops=1 << 36,
        vmem=63,
    )

    ins = dict(
        elements=elements,
        comp=comp,
        **{k: weights[k] for k in ("edge", "r2", "rowp", "rate", "gain", "inT", "outw", "xwT", "dtw2")},
        **{k: started[k] for k in PREP_OUTS},
        s_inT=shorts["g_inT"],
        s_out=shorts["g_out"],
        s_peT=shorts["g_peT"],
        s_gain=shorts["g_gain"],
    )
    outs = dict(rows_out(span), gated=((4 * span, E), BF))
    scratch = dict(entering=((16 * NP, E), F32), fold=((16 * NP, E), F32))
    if packed:
        outs.update(give=((count * PACK, LT), BF), keep=((count * GATHER, LT), BF))
        scratch.update(GRADS, pe_out=((E, LT), BF), deltas=((2 * EDGE, LT), BF))
    else:
        outs.update(GRADS, delta=((HALO, D), F32))
    scratch.update(scan_scratch(span))
    scratch.update({k: v for k, v in post_scratch(span).items() if k not in outs})
    longs = run(
        "long_windows",
        functools.partial(long_windows_body, T=span),
        ins,
        outs,
        scratch,
        flops=1 << 35,
        far=tuple(k for k in LONG_FAR),
    )

    outs = dict(
        l_out=((MB * span, D), BF),
        l_ing=((MB * span, D), F32),
        s_out=((MB * short, D), BF),
        s_ing=((MB * short, D), F32),
        mark=((8, LT), F32),
    )
    ins = dict(comp=comp, outw=weights["outw"], gain=weights["gain"])
    ins.update({"l_" + k: v for k, v in long_in.items()}, l_gated=longs["gated"], l_rows=longs["rows"])
    ins.update(
        {"s_" + k: v for k, v in short_in.items()},
        s_gated=shorts["gated"],
        s_rows=shorts["rows"],
    )
    finished = run("outputs", outputs_body, ins, outs, flops=1 << 32, vmem=32)
    ins = dict(ing=finished["l_ing"])
    outs = dict(grad=((MB * span, D), F32))
    if packed:
        ins["own"], ins["got"] = scatter(longs["give"], longs["keep"], finished["mark"])
        outs.update(
            gain=((1, D // (2 * count)), F32),
            in_wT=((IN_ROWS, D), F32),
            conv_w=((4, CH_ROWS), F32),
            conv_b=((1, CH_ROWS), F32),
            x_w=((CH_ROWS, 3 * N), F32),
            dt_w=((N, CH_ROWS), F32),
            dt_b=((1, CH_ROWS), F32),
            a_log=((CH_ROWS, N), F32),
            skip=((1, CH_ROWS), F32),
            out_w=((OUT_ROWS, D), F32),
        )
    else:
        ins["from_next"] = lax.ppermute(longs["delta"], "seq", down)
        ins["from_prev"] = lax.ppermute(longs["delta"], "seq", up)
    done = run("final", functools.partial(final_body, packed=packed), ins, outs, vmem=8)
    if packed:
        grads = {k: done[k] for k in outs if k != "grad"}
        grads["in_w"] = grads["in_wT"].T
        for k in ("gain", "conv_b", "dt_b", "skip"):
            grads[k] = grads[k].reshape(-1)
    else:

        def own(a, axis=0):
            return lax.psum_scatter(a, BOTH, scatter_dimension=axis, tiled=True)

        pe = own(longs["g_peT"].T)
        grads = dict(
            gain=own(longs["g_gain"][0]),
            in_w=own(longs["g_inT"]).T,
            conv_w=pe[:, AT_SMALL : AT_SMALL + 4].T,
            conv_b=pe[:, AT_SMALL + 4],
            x_w=pe[:, : 3 * N],
            dt_w=pe[:, AT_DT : AT_DT + N].T,
            dt_b=pe[:, AT_SMALL + 5],
            a_log=pe[:, AT_A : AT_A + N],
            skip=pe[:, AT_SMALL + 6],
            out_w=own(longs["g_out"]),
        )
    order = ("gain", "in_w", "conv_w", "conv_b", "x_w", "dt_w", "dt_b", "a_log", "skip", "out_w")
    return (
        finished["l_out"].reshape(long_tokens.shape),
        finished["s_out"].reshape(short_tokens.shape),
        done["grad"].reshape(long_tokens.shape),
        finished["s_ing"].reshape(short_tokens.shape),
    ) + tuple(grads[k] for k in order)


def solution(mesh):
    long_spec, short_spec = P(None, "dp", "seq", None), P(None, BOTH, None, None)
    rows, columns, vector = P(BOTH, None), P(None, BOTH), P(BOTH)
    params = (vector, columns, columns, vector, rows, columns, vector, rows, vector, rows)
    return jax.shard_map(
        local,
        mesh=mesh,
        in_specs=(
            long_spec,
            short_spec,
            long_spec,
            short_spec,
            P(None, "dp", "seq"),
            P(None, BOTH, None),
            P(),
        )
        + params,
        out_specs=(long_spec, short_spec, long_spec, short_spec) + params,
        check_vma=False,
    )
```

time: 123 us -> 111 us (0.902)
  blocking collectives: 23.4 us -> 0 us
  starting transfers between devices: 11.6 us -> 23.2 us
  Pallas kernels: 65.7 us -> 60.7 us
  waiting for transfers between devices: 17.4 us -> 21.3 us
    all_to_all x1 -> x0, blocking collectives: 23.4 us -> none  [local(): mine = lax.all_to_all(buf, 'seq', 0, 0, tiled=True)]
    ppermute x8 -> x15, waiting for transfers between devices: 4.85 us -> 21.3 us  [the longest x10 18.3 us: swapped(): return lax.ppermute(x, 'seq', [(i, i ^ mask) for i in range(count)])]
    all_to_all x1, waiting for transfers between devices: 12.6 us -> 0.01 us  [local(): elements = lax.all_to_all(started['carry'], 'seq', 0, 0, tiled=True)]
    ppermute x8 -> x15, starting transfers between devices: 8.01 us -> 17.1 us  [the longest x10 16.6 us: swapped(): return lax.ppermute(x, 'seq', [(i, i ^ mask) for i in range(count)])]
    pallas_call x9 -> x11, Pallas kernels: 65.7 us -> 60.7 us  [run(): pl.pallas_call(kernel, out_shape=tuple((jax.ShapeDtypeStruct(*v) for v in...]
    all_to_all x1, starting transfers between devices: 3.57 us -> 6.19 us  [local(): elements = lax.all_to_all(started['carry'], 'seq', 0, 0, tiled=True)]
  transfers between devices with their start and end apart: 9 -> 16, of which waited for: 4 -> 11; matrix products, arithmetic and copies ran while one was open for 0% -> 0% of each run, Pallas kernels for 29% -> 28%
where the time goes in v2:
time: 111 us
  Pallas kernels  60.7 us (55%)
  starting transfers between devices  23.2 us (21%)
  waiting for transfers between devices  21.3 us (19%)
  local copies, waits for them, and re-layouts  4.43 us (4%)
    pallas_call x11, Pallas kernels, run(): pl.pallas_call(kernel, out_shape=tuple((jax.ShapeDtypeStruct(*v) for v in...  60.7 us
    ppermute x10, waiting for transfers between devices, swapped(): return lax.ppermute(x, 'seq', [(i, i ^ mask) for i in range(count)])  18.3 us
    ppermute x10, starting transfers between devices, swapped(): return lax.ppermute(x, 'seq', [(i, i ^ mask) for i in range(count)])  16.6 us
    all_to_all x1, starting transfers between devices, local(): elements = lax.all_to_all(started['carry'], 'seq', 0, 0, tiled=True)  6.19 us
    unnamed x46, local copies, waits for them, and re-layouts  4.43 us
  transfers between devices with their start and end apart: 16, of which 11 were waited for; matrix products, arithmetic and copies ran while one was open for 0% of the time, Pallas kernels for 28%

profile of v2, /device:TPU:0, one launch (start us, length us, event | category | flops | bytes accessed | tf_op | source)
XLA Modules:
  0.0 110.6 jit_solution(7619967482882731064)
XLA Ops:
  0.6 1.8 %pack.1.refs_0_ = bf16[144,128]{1,0:T(8,128)(2,1)} custom-call(f32[1,8]{1,0:T(1,128)} %bitcast.50, bf16[32,256]{1,0:T(8,128)(2,1)} %bitcast.49, f32[4,16]{1,0:T(4,128)} %refs_2_.1, f32[1,16]{1,0:T(1,128)} %bitcast.51, bf16[16,48]{1,0:T(8,128)(2,1)} %refs_4_.1, bf16[16,16]{1,0:T(8,128)(2,1)} %refs_5_.1, f32[1,16]{1,0:T(1,128)} %bitcast.52, f32[16,16]{1,0:T(8,128)} %refs_7_.1, ...), custom_call_target="tpu_custom_call" | custom-call | bytes 1048576 | tf_op jit(solution)/shard_map/pack/pallas_call | solution.py:89
  2.4 4.0 %collective-permute-start = (bf16[144,128]{1,0:T(8,128)(2,1)}, bf16[144,128]{1,0:T(8,128)(2,1)S(1)}, u32[]{:S(2)}, u32[]{:S(2)}) collective-permute-start(bf16[144,128]{1,0:T(8,128)(2,1)} %pack.1.refs_0_), channel_id=1, source_target_pairs={{0,8},{1,9},{2,10},{3,11},{4,12},{5,13},{6,14},{7,15},{8,0},{9,1},... | collective-permute-start | bytes 110600 | tf_op jit(solution)/shard_map/ppermute | solution.py:220
  6.5 2.5 %collective-permute-done.refs_1_ = bf16[144,128]{1,0:T(8,128)(2,1)S(1)} collective-permute-done((bf16[144,128]{1,0:T(8,128)(2,1)}, bf16[144,128]{1,0:T(8,128)(2,1)S(1)}, u32[]{:S(2)}, u32[]{:S(2)}) %collective-permute-start) | collective-permute-done | bytes 36896 | tf_op jit(solution)/shard_map/ppermute | solution.py:220
  9.0 0.8 copy-done.2
  9.8 1.5 %collective-permute-start.1 = (bf16[288,128]{1,0:T(8,128)(2,1)S(1)}, bf16[288,128]{1,0:T(8,128)(2,1)S(1)}, u32[]{:S(2)}, u32[]{:S(2)}) collective-permute-start(bf16[288,128]{1,0:T(8,128)(2,1)S(1)} %join8.1.refs_0_), channel_id=1, source_target_pairs={{0,4},{1,5},{2,6},{3,7},{4,0},{5,1},{6,2},{7,3},{8,12},{9,13},{10,... | collective-permute-start | bytes 221192 | tf_op jit(solution)/shard_map/ppermute | solution.py:220
  11.3 2.8 %collective-permute-done.1.refs_1_ = bf16[288,128]{1,0:T(8,128)(2,1)S(1)} collective-permute-done((bf16[288,128]{1,0:T(8,128)(2,1)S(1)}, bf16[288,128]{1,0:T(8,128)(2,1)S(1)}, u32[]{:S(2)}, u32[]{:S(2)}) %collective-permute-start.1) | collective-permute-done | bytes 73760 | tf_op jit(solution)/shard_map/ppermute | solution.py:220
  14.2 0.0 copy-start.1
  14.2 2.7 %collective-permute-start.4 = (bf16[576,128]{1,0:T(8,128)(2,1)S(1)}, bf16[576,128]{1,0:T(8,128)(2,1)S(1)}, u32[]{:S(2)}, u32[]{:S(2)}) collective-permute-start(bf16[576,128]{1,0:T(8,128)(2,1)S(1)} %join4.1.refs_4_), channel_id=1, source_target_pairs={{0,3},{1,2},{2,1},{3,0},{4,7},{5,6},{6,5},{7,4},{8,11},{9,10},{10,... | collective-permute-start | bytes 442376 | tf_op jit(solution)/shard_map/ppermute | solution.py:220
  16.9 0.5 collective-permute-start.3
  17.4 0.3 collective-permute-start.2
  17.7 0.0 collective-permute-start.5
  17.7 3.1 %collective-permute-done.4.refs_7_ = bf16[576,128]{1,0:T(8,128)(2,1)S(1)} collective-permute-done((bf16[576,128]{1,0:T(8,128)(2,1)S(1)}, bf16[576,128]{1,0:T(8,128)(2,1)S(1)}, u32[]{:S(2)}, u32[]{:S(2)}) %collective-permute-start.4) | collective-permute-done | bytes 147488 | tf_op jit(solution)/shard_map/ppermute | solution.py:220
  20.8 0.0 collective-permute-start.8
  20.8 1.5 %collective-permute-done.3.refs_6_ = bf16[576,128]{1,0:T(8,128)(2,1)S(1)} collective-permute-done((bf16[576,128]{1,0:T(8,128)(2,1)S(1)}, bf16[576,128]{1,0:T(8,128)(2,1)S(1)}, u32[]{:S(2)}, u32[]{:S(2)}) %collective-permute-start.3) | collective-permute-done | bytes 147488 | tf_op jit(solution)/shard_map/ppermute | solution.py:220
  22.4 0.0 collective-permute-start.7
  22.4 0.1 collective-permute-done.2.refs_5_
  22.5 0.4 collective-permute-start.6
  22.9 0.0 collective-permute-done.5.refs_8_
  22.9 0.0 collective-permute-done.8.refs_11_
  22.9 0.0 copy-start.20
  22.9 0.8 collective-permute-done.7.refs_10_
  23.8 0.2 collective-permute-done.6.refs_9_
  24.0 0.0 copy-done.1
  24.0 0.0 copy-done.16
  24.0 0.0 copy-done.18
  24.0 0.0 copy-done.19
  24.0 0.0 copy-done.20
  24.0 0.4 copy-done.21
  24.4 0.2 copy-done.22
  24.6 10.2 %long_start.1 = (bf16[4608,128]{1,0:T(8,128)(2,1)}, bf16[272,256]{1,0:T(8,128)(2,1)}, bf16[256,256]{1,0:T(8,128)(2,1)}, f32[272,512]{1,0:T(8,128)}, f32[256,512]...) custom-call(s32[1,256]{1,0:T(1,128)} %bitcast.40, ...), custom_call_target="tpu_custom_call" | custom-call | flops 8589934592 | bytes 1048576 | tf_op jit(solution)/shard_map/long_start/pallas_call | solution.py:89
  34.9 6.2 %all-to-all-start = ((bf16[16,288,128]{2,1,0:T(8,128)(2,1)}), bf16[16,288,128]{2,1,0:T(8,128)(2,1)}, u32[]{:S(2)}, u32[]{:S(2)}) async-start(bf16[16,288,128]{2,1,0:T(8,128)(2,1)} %bitcast.48), calls=%async_computation | async-start | bytes 2359296 | tf_op jit(solution)/shard_map/all_to_all | solution.py:1145
  41.1 28.3 %short_windows.1 = (f32[1024,256]{1,0:T(8,128)}, f32[512,256]{1,0:T(8,128)}, f32[128,512]{1,0:T(8,128)}, f32[8,256]{1,0:T(8,128)}, f32[528,256]{1,0:T(8,128)}, /*index=5*/bf16[512,512]{1,0:T(8,128)(2,1)}) custom-call(s32[1,256]{1,0:T(1,128)} %bitcast.41, bf16[256,256]{1,0:T(8,128)(2,1)} %bitcast.34, bf16[256,256]{1,0:T(8,128)(2,1)} %bitcast.36, ...), custom_call_target="tpu_custom_call" | custom-call | flops 68719476736 | bytes 1048576 | tf_op jit(solution)/shard_map/short_windows/pallas_call | solution.py:89
  69.4 0.0 all-to-all-done
  69.4 0.0 copy-start.3
  69.4 0.0 copy-start.4
  69.4 0.0 copy-start.5
  69.4 0.0 copy-start.6
  69.4 0.0 copy-start.7
  69.4 0.0 copy-start.8
  69.5 0.0 copy-start.9
  69.5 0.0 copy-start.10
  69.5 0.0 copy-start.11
  69.5 0.0 copy-start.13
  69.5 0.0 copy-start.15
  69.5 16.5 %long_windows.1 = (f32[272,256]{1,0:T(8,128)}, bf16[256,512]{1,0:T(8,128)(2,1)}, bf16[1792,128]{1,0:T(8,128)(2,1)}, bf16[2304,128]{1,0:T(8,128)(2,1)}) custom-call(bf16[4608,128]{1,0:T(8,128)(2,1)} %bitcast.10.refs_0_, s32[1,256]{1,0:T(1,128)} %bitcast.42, bf16[16,256]{1,0:T(8,128)(2,1)} %get-tuple-element.74.refs_2_, ...), custom_call_target="tpu_custom_call" | custom-call | flops 34359738368 | bytes 1048576 | tf_op jit(solution)/shard_map/long_windows/pallas_call | solution.py:89
  86.0 0.1 collective-permute-start.9
  86.1 2.0 %collective-permute-done.9.refs_0_ = bf16[1792,128]{1,0:T(8,128)(2,1)S(1)} collective-permute-done((bf16[1792,128]{1,0:T(8,128)(2,1)}, bf16[1792,128]{1,0:T(8,128)(2,1)S(1)}, u32[]{:S(2)}, u32[]{:S(2)}) %collective-permute-start.9) | collective-permute-done | bytes 458784 | tf_op jit(solution)/shard_map/ppermute | solution.py:934
  88.1 1.1 copy-done
  89.2 0.2 add_core.1
  89.4 1.9 %collective-permute-start.10 = (bf16[576,128]{1,0:T(8,128)(2,1)S(1)}, bf16[576,128]{1,0:T(8,128)(2,1)S(1)}, u32[]{:S(2)}, u32[]{:S(2)}) collective-permute-start(bf16[576,128]{1,0:T(8,128)(2,1)S(1)} %get-tuple-element.109), channel_id=1, source_target_pairs={{0,1},{1,0},{2,3},{3,2},{4,5},{5,4},{6,7},{7,6},{8,9},{9,8},{10,11... | collective-permute-start | bytes 442376 | tf_op jit(solution)/shard_map/ppermute | solution.py:932
  91.3 1.5 %collective-permute-start.11 = (bf16[576,128]{1,0:T(8,128)(2,1)S(1)}, bf16[576,128]{1,0:T(8,128)(2,1)S(1)}, u32[]{:S(2)}, u32[]{:S(2)}) collective-permute-start(bf16[576,128]{1,0:T(8,128)(2,1)S(1)} %get-tuple-element.110), channel_id=1, source_target_pairs={{0,2},{1,3},{2,0},{3,1},{4,6},{5,7},{6,4},{7,5},{8,10},{9,11},{10,... | collective-permute-start | bytes 442376 | tf_op jit(solution)/shard_map/ppermute | solution.py:932
  92.8 0.1 collective-permute-start.12
  93.1 0.9 copy-done.12
  94.0 0.9 copy-done.14
  95.0 2.7 %outputs.1 = (bf16[128,256]{1,0:T(8,128)(2,1)}, f32[128,256]{1,0:T(8,128)S(1)}, bf16[256,256]{1,0:T(8,128)(2,1)}, f32[256,256]{1,0:T(8,128)}, f32[8,128]{1,0:T(8,128)S(1)}) custom-call(s32[1,256]{1,0:T(1,128)S(1)} %bitcast.43, bf16[512,256]{1,0:T(8,128)(2,1)S(1)} %copy-done.13, f32[8,256]{1,0:T(8,128)S(1)} %copy-done.15, bf16[128,256]{1,0:T(8,128)(2,1)S(1)} %bitcast.33, ...), custom_call_target="tpu_custom_call" | custom-call | flops 4294967296 | bytes 1048576 | tf_op jit(solution)/shard_map/outputs/pallas_call | solution.py:89
  97.6 0.0 collective-permute-done.10.refs_2_
  97.7 2.5 %collective-permute-done.11.refs_3_ = bf16[576,128]{1,0:T(8,128)(2,1)S(1)} collective-permute-done((bf16[576,128]{1,0:T(8,128)(2,1)S(1)}, bf16[576,128]{1,0:T(8,128)(2,1)S(1)}, u32[]{:S(2)}, u32[]{:S(2)}) %collective-permute-start.11) | collective-permute-done | bytes 147488 | tf_op jit(solution)/shard_map/ppermute | solution.py:932
  100.1 0.0 collective-permute-done.12.refs_4_
  100.1 0.1 add_near.1
  100.2 2.4 %collective-permute-start.13 = (bf16[288,128]{1,0:T(8,128)(2,1)S(1)}, bf16[288,128]{1,0:T(8,128)(2,1)S(1)}, u32[]{:S(2)}, u32[]{:S(2)}) collective-permute-start(bf16[288,128]{1,0:T(8,128)(2,1)S(1)} %get-tuple-element.113), channel_id=1, source_target_pairs={{0,8},{1,9},{2,10},{3,11},{4,12},{5,13},{6,14},{7,15},{8,0},{9,1},... | collective-permute-start | bytes 221192 | tf_op jit(solution)/shard_map/ppermute | solution.py:932
  102.6 3.1 %collective-permute-done.13.refs_1_ = bf16[288,128]{1,0:T(8,128)(2,1)S(1)} collective-permute-done((bf16[288,128]{1,0:T(8,128)(2,1)S(1)}, bf16[288,128]{1,0:T(8,128)(2,1)S(1)}, u32[]{:S(2)}, u32[]{:S(2)}) %collective-permute-start.13) | collective-permute-done | bytes 73760 | tf_op jit(solution)/shard_map/ppermute | solution.py:932
  105.8 1.5 %collective-permute-start.14 = (bf16[144,128]{1,0:T(8,128)(2,1)S(1)}, bf16[144,128]{1,0:T(8,128)(2,1)S(1)}, u32[]{:S(2)}, u32[]{:S(2)}) collective-permute-start(bf16[144,128]{1,0:T(8,128)(2,1)S(1)} %get-tuple-element.115), channel_id=1, source_target_pairs={{0,4},{1,5},{2,6},{3,7},{4,0},{5,1},{6,2},{7,3},{8,12},{9,13},{10,... | collective-permute-start | bytes 110600 | tf_op jit(solution)/shard_map/ppermute | solution.py:932
  107.3 2.5 %collective-permute-done.14.refs_2_ = bf16[144,128]{1,0:T(8,128)(2,1)S(1)} collective-permute-done((bf16[144,128]{1,0:T(8,128)(2,1)S(1)}, bf16[144,128]{1,0:T(8,128)(2,1)S(1)}, u32[]{:S(2)}, u32[]{:S(2)}) %collective-permute-start.14) | collective-permute-done | bytes 36896 | tf_op jit(solution)/shard_map/ppermute | solution.py:932
  109.8 0.8 final.1
  (25 shorter events, 0.1 us)
Async XLA Ops:
  2.4 6.6 %collective-permute-start = (bf16[144,128]{1,0:T(8,128)(2,1)}, bf16[144,128]{1,0:T(8,128)(2,1)S(1)}, u32[]{:S(2)}, u32[]{:S(2)}) collective-permute-start(bf16[144,128]{1,0:T(8,128)(2,1)} %pack.1.refs_0_), channel_id=1, source_target_pairs={{0,8},{1,9},{2,10},{3,11},{4,12},{5,13},{6,14},{7,15},{8,0},{9,1},... | collective-permute-start | bytes 110600 | tf_op jit(solution)/shard_map/ppermute | solution.py:220
  9.0 0.8 copy-start.2
  9.8 4.4 %collective-permute-start.1 = (bf16[288,128]{1,0:T(8,128)(2,1)S(1)}, bf16[288,128]{1,0:T(8,128)(2,1)S(1)}, u32[]{:S(2)}, u32[]{:S(2)}) collective-permute-start(bf16[288,128]{1,0:T(8,128)(2,1)S(1)} %join8.1.refs_0_), channel_id=1, source_target_pairs={{0,4},{1,5},{2,6},{3,7},{4,0},{5,1},{6,2},{7,3},{8,12},{9,13},{10,... | collective-permute-start | bytes 221192 | tf_op jit(solution)/shard_map/ppermute | solution.py:220
  14.2 9.8 %copy-start.1 = (bf16[576,128]{1,0:T(8,128)(2,1)}, bf16[576,128]{1,0:T(8,128)(2,1)S(1)}, u32[]{:S(2)}) copy-start(bf16[576,128]{1,0:T(8,128)(2,1)S(1)} %join4.1.refs_4_) | copy-start | bytes 442372
  14.2 6.7 %collective-permute-start.4 = (bf16[576,128]{1,0:T(8,128)(2,1)S(1)}, bf16[576,128]{1,0:T(8,128)(2,1)S(1)}, u32[]{:S(2)}, u32[]{:S(2)}) collective-permute-start(bf16[576,128]{1,0:T(8,128)(2,1)S(1)} %join4.1.refs_4_), channel_id=1, source_target_pairs={{0,3},{1,2},{2,1},{3,0},{4,7},{5,6},{6,5},{7,4},{8,11},{9,10},{10,... | collective-permute-start | bytes 442376 | tf_op jit(solution)/shard_map/ppermute | solution.py:220
  16.9 5.5 %collective-permute-start.3 = (bf16[576,128]{1,0:T(8,128)(2,1)S(1)}, bf16[576,128]{1,0:T(8,128)(2,1)S(1)}, u32[]{:S(2)}, u32[]{:S(2)}) collective-permute-start(bf16[576,128]{1,0:T(8,128)(2,1)S(1)} %join4.1.refs_4_), channel_id=1, source_target_pairs={{0,2},{1,3},{2,0},{3,1},{4,6},{5,7},{6,4},{7,5},{8,10},{9,11},{10,... | collective-permute-start | bytes 442376 | tf_op jit(solution)/shard_map/ppermute | solution.py:220
  17.4 5.1 %collective-permute-start.2 = (bf16[576,128]{1,0:T(8,128)(2,1)S(1)}, bf16[576,128]{1,0:T(8,128)(2,1)S(1)}, u32[]{:S(2)}, u32[]{:S(2)}) collective-permute-start(bf16[576,128]{1,0:T(8,128)(2,1)S(1)} %join4.1.refs_4_), channel_id=1, source_target_pairs={{0,1},{1,0},{2,3},{3,2},{4,5},{5,4},{6,7},{7,6},{8,9},{9,8},{10,11... | collective-permute-start | bytes 442376 | tf_op jit(solution)/shard_map/ppermute | solution.py:220
  17.7 5.2 %collective-permute-start.5 = (bf16[576,128]{1,0:T(8,128)(2,1)S(1)}, bf16[576,128]{1,0:T(8,128)(2,1)S(1)}, u32[]{:S(2)}, u32[]{:S(2)}) collective-permute-start(bf16[576,128]{1,0:T(8,128)(2,1)S(1)} %join4.1.refs_4_), channel_id=1, source_target_pairs={{0,16},{16,0},{1,17},{17,1},{2,18},{18,2},{3,19},{19,3},{4,20},{20... | collective-permute-start | bytes 442376 | tf_op jit(solution)/shard_map/ppermute | solution.py:231
  20.8 3.1 %copy-start.16 = (bf16[576,128]{1,0:T(8,128)(2,1)}, bf16[576,128]{1,0:T(8,128)(2,1)S(1)}, u32[]{:S(2)}) copy-start(bf16[576,128]{1,0:T(8,128)(2,1)S(1)} %collective-permute-done.4.refs_7_) | copy-start | bytes 442372
  20.8 2.1 %collective-permute-start.8 = (bf16[576,128]{1,0:T(8,128)(2,1)S(1)}, bf16[576,128]{1,0:T(8,128)(2,1)S(1)}, u32[]{:S(2)}, u32[]{:S(2)}) collective-permute-start(bf16[576,128]{1,0:T(8,128)(2,1)S(1)} %collective-permute-done.4.refs_7_), channel_id=1, source_target_pairs={{0,16},{16,0},{1,17},{17,1},{2,18},{18,2},{3,19},{19,3},{4,20},{20... | collective-permute-start | bytes 442376 | tf_op jit(solution)/shard_map/ppermute | solution.py:231
  22.4 1.6 %copy-start.17 = (bf16[576,128]{1,0:T(8,128)(2,1)}, bf16[576,128]{1,0:T(8,128)(2,1)S(1)}, u32[]{:S(2)}) copy-start(bf16[576,128]{1,0:T(8,128)(2,1)S(1)} %collective-permute-done.3.refs_6_) | copy-start | bytes 442372
  22.4 1.4 %collective-permute-start.7 = (bf16[576,128]{1,0:T(8,128)(2,1)S(1)}, bf16[576,128]{1,0:T(8,128)(2,1)S(1)}, u32[]{:S(2)}, u32[]{:S(2)}) collective-permute-start(bf16[576,128]{1,0:T(8,128)(2,1)S(1)} %collective-permute-done.3.refs_6_), channel_id=1, source_target_pairs={{0,16},{16,0},{1,17},{17,1},{2,18},{18,2},{3,19},{19,3},{4,20},{20... | collective-permute-start | bytes 442376 | tf_op jit(solution)/shard_map/ppermute | solution.py:231
  22.5 1.4 %copy-start.18 = (bf16[576,128]{1,0:T(8,128)(2,1)}, bf16[576,128]{1,0:T(8,128)(2,1)S(1)}, u32[]{:S(2)}) copy-start(bf16[576,128]{1,0:T(8,128)(2,1)S(1)} %collective-permute-done.2.refs_5_) | copy-start | bytes 442372
  22.5 1.4 %collective-permute-start.6 = (bf16[576,128]{1,0:T(8,128)(2,1)S(1)}, bf16[576,128]{1,0:T(8,128)(2,1)S(1)}, u32[]{:S(2)}, u32[]{:S(2)}) collective-permute-start(bf16[576,128]{1,0:T(8,128)(2,1)S(1)} %collective-permute-done.2.refs_5_), channel_id=1, source_target_pairs={{0,16},{16,0},{1,17},{17,1},{2,18},{18,2},{3,19},{19,3},{4,20},{20... | collective-permute-start | bytes 442376 | tf_op jit(solution)/shard_map/ppermute | solution.py:231
  22.9 1.1 copy-start.19
  22.9 1.1 copy-start.20
  23.8 0.7 copy-start.21
  24.0 0.7 copy-start.22
  34.9 34.5 %all-to-all-start = ((bf16[16,288,128]{2,1,0:T(8,128)(2,1)}), bf16[16,288,128]{2,1,0:T(8,128)(2,1)}, u32[]{:S(2)}, u32[]{:S(2)}) async-start(bf16[16,288,128]{2,1,0:T(8,128)(2,1)} %bitcast.48), calls=%async_computation | async-start | bytes 2359296 | tf_op jit(solution)/shard_map/all_to_all | solution.py:1145
  69.4 23.6 %copy-start.3 = (bf16[2,1,64,256]{3,2,1,0:T(8,128)(2,1)S(1)}, bf16[2,1,64,256]{3,2,1,0:T(8,128)(2,1)}, u32[]{:S(2)}) copy-start(bf16[2,1,64,256]{3,2,1,0:T(8,128)(2,1)} %param.17) | copy-start | bytes 196612
  69.4 23.6 %copy-start.4 = (bf16[2,1,128,256]{3,2,1,0:T(8,128)(2,1)S(1)}, bf16[2,1,128,256]{3,2,1,0:T(8,128)(2,1)}, u32[]{:S(2)}) copy-start(bf16[2,1,128,256]{3,2,1,0:T(8,128)(2,1)} %param.18) | copy-start | bytes 393220
  69.4 23.6 %copy-start.5 = (bf16[2,1,128,256]{3,2,1,0:T(8,128)(2,1)S(1)}, bf16[2,1,128,256]{3,2,1,0:T(8,128)(2,1)}, u32[]{:S(2)}) copy-start(bf16[2,1,128,256]{3,2,1,0:T(8,128)(2,1)} %param.20) | copy-start | bytes 393220
  69.4 23.6 %copy-start.6 = (bf16[2,1,64,256]{3,2,1,0:T(8,128)(2,1)S(1)}, bf16[2,1,64,256]{3,2,1,0:T(8,128)(2,1)}, u32[]{:S(2)}) copy-start(bf16[2,1,64,256]{3,2,1,0:T(8,128)(2,1)} %param.19) | copy-start | bytes 196612
  69.4 23.6 %copy-start.7 = (s32[256]{0:T(256)S(1)}, s32[256]{0:T(256)}, u32[]{:S(2)}) copy-start(s32[256]{0:T(256)} %param.23) | copy-start | bytes 3076
  69.4 23.6 %copy-start.8 = (s32[2,1,64]{2,1,0:T(1,128)S(1)}, s32[2,1,64]{2,1,0:T(1,128)}, u32[]{:S(2)}) copy-start(s32[2,1,64]{2,1,0:T(1,128)} %param.21) | copy-start | bytes 1540
  69.5 23.6 %copy-start.9 = (s32[2,1,128]{2,1,0:T(1,128)S(1)}, s32[2,1,128]{2,1,0:T(1,128)}, u32[]{:S(2)}) copy-start(s32[2,1,128]{2,1,0:T(1,128)} %param.22) | copy-start | bytes 3076
  69.5 23.6 %copy-start.10 = (f32[528,256]{1,0:T(8,128)S(1)}, f32[528,256]{1,0:T(8,128)}, u32[]{:S(2)}) copy-start(f32[528,256]{1,0:T(8,128)} %get-tuple-element.101.refs_12_) | copy-start | bytes 1622020
  69.5 23.6 %copy-start.11 = (bf16[512,512]{1,0:T(8,128)(2,1)S(1)}, bf16[512,512]{1,0:T(8,128)(2,1)}, u32[]{:S(2)}) copy-start(bf16[512,512]{1,0:T(8,128)(2,1)} %get-tuple-element.100.refs_11_) | copy-start | bytes 1572868
  69.5 23.6 %copy-start.13 = (bf16[512,256]{1,0:T(8,128)(2,1)S(1)}, bf16[512,256]{1,0:T(8,128)(2,1)}, u32[]{:S(2)}) copy-start(bf16[512,256]{1,0:T(8,128)(2,1)} %get-tuple-element.71.refs_5_.refs_8_.refs_1_) | copy-start | bytes 786436
  69.5 23.6 %copy-start.15 = (f32[8,256]{1,0:T(8,128)S(1)}, f32[8,256]{1,0:T(8,128)}, u32[]{:S(2)}) copy-start(f32[8,256]{1,0:T(8,128)} %get-tuple-element.72.refs_7_.refs_6_.refs_2_) | copy-start | bytes 24580
  86.0 2.1 %collective-permute-start.9 = (bf16[1792,128]{1,0:T(8,128)(2,1)}, bf16[1792,128]{1,0:T(8,128)(2,1)S(1)}, u32[]{:S(2)}, u32[]{:S(2)}) collective-permute-start(bf16[1792,128]{1,0:T(8,128)(2,1)} %get-tuple-element.105), channel_id=1, source_target_pairs={{0,16},{16,0},{1,17},{17,1},{2,18},{18,2},{3,19},{19,3},{4,20},{20... | collective-permute-start | bytes 1376264 | tf_op jit(solution)/shard_map/ppermute | solution.py:934
  88.1 1.1 copy-start
  89.4 8.2 %collective-permute-start.10 = (bf16[576,128]{1,0:T(8,128)(2,1)S(1)}, bf16[576,128]{1,0:T(8,128)(2,1)S(1)}, u32[]{:S(2)}, u32[]{:S(2)}) collective-permute-start(bf16[576,128]{1,0:T(8,128)(2,1)S(1)} %get-tuple-element.109), channel_id=1, source_target_pairs={{0,1},{1,0},{2,3},{3,2},{4,5},{5,4},{6,7},{7,6},{8,9},{9,8},{10,11... | collective-permute-start | bytes 442376 | tf_op jit(solution)/shard_map/ppermute | solution.py:932
  91.3 8.8 %collective-permute-start.11 = (bf16[576,128]{1,0:T(8,128)(2,1)S(1)}, bf16[576,128]{1,0:T(8,128)(2,1)S(1)}, u32[]{:S(2)}, u32[]{:S(2)}) collective-permute-start(bf16[576,128]{1,0:T(8,128)(2,1)S(1)} %get-tuple-element.110), channel_id=1, source_target_pairs={{0,2},{1,3},{2,0},{3,1},{4,6},{5,7},{6,4},{7,5},{8,10},{9,11},{10,... | collective-permute-start | bytes 442376 | tf_op jit(solution)/shard_map/ppermute | solution.py:932
  92.8 7.3 %collective-permute-start.12 = (bf16[576,128]{1,0:T(8,128)(2,1)S(1)}, bf16[576,128]{1,0:T(8,128)(2,1)S(1)}, u32[]{:S(2)}, u32[]{:S(2)}) collective-permute-start(bf16[576,128]{1,0:T(8,128)(2,1)S(1)} %get-tuple-element.111), channel_id=1, source_target_pairs={{0,3},{1,2},{2,1},{3,0},{4,7},{5,6},{6,5},{7,4},{8,11},{9,10},{10,... | collective-permute-start | bytes 442376 | tf_op jit(solution)/shard_map/ppermute | solution.py:932
  93.1 1.0 copy-start.12
  94.0 0.9 copy-start.14
  100.2 5.5 %collective-permute-start.13 = (bf16[288,128]{1,0:T(8,128)(2,1)S(1)}, bf16[288,128]{1,0:T(8,128)(2,1)S(1)}, u32[]{:S(2)}, u32[]{:S(2)}) collective-permute-start(bf16[288,128]{1,0:T(8,128)(2,1)S(1)} %get-tuple-element.113), channel_id=1, source_target_pairs={{0,8},{1,9},{2,10},{3,11},{4,12},{5,13},{6,14},{7,15},{8,0},{9,1},... | collective-permute-start | bytes 221192 | tf_op jit(solution)/shard_map/ppermute | solution.py:932
  105.8 4.0 %collective-permute-start.14 = (bf16[144,128]{1,0:T(8,128)(2,1)S(1)}, bf16[144,128]{1,0:T(8,128)(2,1)S(1)}, u32[]{:S(2)}, u32[]{:S(2)}) collective-permute-start(bf16[144,128]{1,0:T(8,128)(2,1)S(1)} %get-tuple-element.115), channel_id=1, source_target_pairs={{0,4},{1,5},{2,6},{3,7},{4,0},{5,1},{6,2},{7,3},{8,12},{9,13},{10,... | collective-permute-start | bytes 110600 | tf_op jit(solution)/shard_map/ppermute | solution.py:932

commit v3 on v2

--- a/solution.py
+++ b/solution.py
@@ -66,7 +66,7 @@
     lax.fori_loop(0, count, lambda i, c: (body(i), c)[1], 0)
 
 
-def run(name, body, ins, outs, scratch=None, flops=0, far=(), early=(), placed=(), vmem=60):
+def run(name, body, ins, outs, scratch=None, flops=0, far=(), early=(), placed=(), pin=None, vmem=60):
     scratch = dict(scratch or {}, **{k: outs[k] for k in early})
     scratch.update({k: (ins[k].shape, ins[k].dtype) for k in far})
     if far:
@@ -88,7 +88,9 @@
 
     result = pl.pallas_call(
         kernel,
-        out_shape=tuple(jax.ShapeDtypeStruct(*v) for v in outs.values()),
+        out_shape=tuple(
+            pin[k](*v) if pin and k in pin else jax.ShapeDtypeStruct(*v) for k, v in outs.items()
+        ),
         in_specs=[spec(k) for k in ins],
         out_specs=tuple(
             pl.BlockSpec(memory_space=pltpu.HBM if k in early or k in placed else pltpu.VMEM)
@@ -159,6 +161,8 @@
         low = 2 * IN_ROWS + half * OUT_ROWS
         r.buf[low : low + OUT_ROWS, :] = out_w[:, lanes]
     r.buf[PACK - CH_ROWS : PACK, :] = chan
+    for name in ("comp", "tok", "cot", "mask"):
+        getattr(r, name + "_near")[...] = getattr(r, name)[...]
     T = r.tok.shape[0] // MB
     for which, first in enumerate((T - 16, 0)):
         rows = [r.tok[mb * T + first : mb * T + first + 16, :].astype(F32) for mb in range(MB)]
@@ -533,8 +537,7 @@
         y = pltpu.roll(jnp.where(valid, r.yi[at, :], 0.0), N, 1) + pltpu.roll(
             jnp.where(valid, r.yo[at, :], 0.0), 2 * N, 1
         )
-        hi, lo = split(y)
-        r.gsel[g * G // 2 : (g + 1) * G // 2, :] = mm(fold, hi) + mm(fold, lo)
+        r.gsel[g * G // 2 : (g + 1) * G // 2, :] = mm(fold, y.astype(BF))
 
 
 def scan_scratch(T):
@@ -1049,8 +1052,19 @@
     up = [(i, i + 1) for i in range(count - 1)]
     down = [(i + 1, i) for i in range(count - 1)]
 
+    def tokens_of(tok, cot, mask):
+        T = tok.shape[2]
+        return dict(
+            tok=tok.reshape(MB * T, D), cot=cot.reshape(MB * T, D), mask=mask.reshape(MB, T)
+        )
+
+    long_in = tokens_of(long_tokens, long_cotangent, long_mask)
+    short_in = tokens_of(short_tokens, short_cotangent, short_mask)
+
+    near = dict(comp=comp, **long_in)
+
     if packed:
-        buf = run(
+        packing = run(
             "pack",
             pack_body,
             dict(
@@ -1064,12 +1078,18 @@
                 a_log=a_log,
                 skip=d_skip.reshape(1, -1),
                 out_w=out_weight,
-                tok=long_tokens.reshape(MB * span, D),
+                comp=comp,
+                **long_in,
             ),
-            dict(buf=((GATHER, LT), BF)),
+            dict(
+                buf=((GATHER, LT), BF),
+                **{k + "_near": (v.shape, v.dtype) for k, v in near.items()},
+            ),
             dict(rows=((8, CH_ROWS), F32)),
-        )["buf"]
-        weights_in = gather(buf)
+            pin={k: pltpu.VMEM for k in ("buf", *(k + "_near" for k in near))},
+        )
+        weights_in = gather(packing["buf"])
+        near = {k: packing[k + "_near"] for k in near}
     else:
         tail = lax.ppermute(long_tokens[:, 0, span - 4 :, :].reshape(8, D), "seq", up)
         head = lax.ppermute(long_tokens[:, 0, :4, :].reshape(8, D), "seq", down)
@@ -1093,15 +1113,6 @@
             edge=jnp.concatenate([tail, head], 0),
         )
 
-    def tokens_of(tok, cot, mask):
-        T = tok.shape[2]
-        return dict(
-            tok=tok.reshape(MB * T, D), cot=cot.reshape(MB * T, D), mask=mask.reshape(MB, T)
-        )
-
-    long_in = tokens_of(long_tokens, long_cotangent, long_mask)
-    short_in = tokens_of(short_tokens, short_cotangent, short_mask)
-
     derived = dict(
         r2=((8 * NP, E), F32),
         rowp=((8, E), F32),
@@ -1119,7 +1130,7 @@
     started = run(
         "long_start",
         functools.partial(long_start_body, T=span, packed=packed),
-        dict(comp=comp, **long_in, **weights_in),
+        dict(near, **weights_in),
         dict(
             carry=((count * ELEMENT, LT), BF), **prep_outs(span), **derived, **(unpacked if packed else {})
         ),
@@ -1136,7 +1147,11 @@
         flops=1 << 33,
         early=PREP_OUTS + tuple(derived) + (tuple(unpacked) if packed else ()),
         placed=("carry",),
-        vmem=62,
+        pin={
+            k: pltpu.HBM
+            for k in PREP_OUTS + tuple(derived) + (tuple(unpacked) if packed else ()) + ("carry",)
+        },
+        vmem=40,
     )
     weights = {k: started[k] for k in derived}
     for k in unpacked:
@@ -1191,6 +1206,8 @@
         scratch,
         flops=1 << 35,
         far=tuple(k for k in LONG_FAR),
+        pin=dict(give=pltpu.VMEM, keep=pltpu.VMEM) if packed else None,
+        vmem=56,
     )
 
     outs = dict(

time: 111 us -> 106 us (0.955)
  local copies, waits for them, and re-layouts: 4.43 us -> 1.96 us
  Pallas kernels: 60.7 us -> 58.4 us
    unnamed x46 -> x26, local copies, waits for them, and re-layouts: 4.43 us -> 1.96 us
    pallas_call x11, Pallas kernels: 60.7 us -> 58.4 us  [run(): pl.pallas_call(kernel, out_shape=tuple((pin[k](*v) if pin and k in pin el...]
  transfers between devices with their start and end apart: 16 -> 16, of which waited for: 11 -> 11; matrix products, arithmetic and copies ran while one was open for 0% -> 0% of each run, Pallas kernels for 28% -> 29%
where the time goes in v3:
time: 106 us
  Pallas kernels  58.4 us (55%)
  starting transfers between devices  23.3 us (22%)
  waiting for transfers between devices  21 us (20%)
  local copies, waits for them, and re-layouts  1.96 us (2%)
    pallas_call x11, Pallas kernels, run(): pl.pallas_call(kernel, out_shape=tuple((pin[k](*v) if pin and k in pin el...  58.4 us
    ppermute x10, waiting for transfers between devices, swapped(): return lax.ppermute(x, 'seq', [(i, i ^ mask) for i in range(count)])  18.2 us
    ppermute x10, starting transfers between devices, swapped(): return lax.ppermute(x, 'seq', [(i, i ^ mask) for i in range(count)])  16.6 us
    all_to_all x1, starting transfers between devices, local(): elements = lax.all_to_all(started['carry'], 'seq', 0, 0, tiled=True)  6.19 us
  transfers between devices with their start and end apart: 16, of which 11 were waited for; matrix products, arithmetic and copies ran while one was open for 0% of the time, Pallas kernels for 29%

profile of v3, /device:TPU:0, one launch (start us, length us, event | category | flops | bytes accessed | tf_op | source)
XLA Modules:
  0.0 105.6 jit_solution(16295614230687003353)
XLA Ops:
  0.6 1.2 %pack.1 = (bf16[144,128]{1,0:T(8,128)(2,1)S(1)}, s32[1,256]{1,0:T(1,128)S(1)}, bf16[128,256]{1,0:T(8,128)(2,1)S(1)}, bf16[128,256]{1,0:T(8,128)(2,1)S(1)}, s32[2,64]{1,0:T(2,128)S(1)}) custom-call(f32[1,8]{1,0:T(1,128)} %bitcast.49, bf16[32,256]{1,0:T(8,128)(2,1)} %bitcast.48, f32[4,16]{1,0:T(4,128)} %refs_2_.1, f32[1,16]{1,0:T(1,128)} %bitcast.50, ...), custom_call_target="tpu_custom_call" | custom-call | bytes 1048576 | tf_op jit(solution)/shard_map/pack/pallas_call | solution.py:89
  1.9 4.1 %collective-permute-start = (bf16[144,128]{1,0:T(8,128)(2,1)S(1)}, bf16[144,128]{1,0:T(8,128)(2,1)S(1)}, u32[]{:S(2)}, u32[]{:S(2)}) collective-permute-start(bf16[144,128]{1,0:T(8,128)(2,1)S(1)} %get-tuple-element.80.refs_0_), channel_id=1, source_target_pairs={{0,8},{1,9},{2,10},{3,11},{4,12},{5,13},{6,14},{7,15},{8,0},{9,1},... | collective-permute-start | bytes 110600 | tf_op jit(solution)/shard_map/ppermute | solution.py:224
  6.0 2.3 %collective-permute-done.refs_1_ = bf16[144,128]{1,0:T(8,128)(2,1)S(1)} collective-permute-done((bf16[144,128]{1,0:T(8,128)(2,1)S(1)}, bf16[144,128]{1,0:T(8,128)(2,1)S(1)}, u32[]{:S(2)}, u32[]{:S(2)}) %collective-permute-start) | collective-permute-done | bytes 36896 | tf_op jit(solution)/shard_map/ppermute | solution.py:224
  8.3 1.5 %collective-permute-start.1 = (bf16[288,128]{1,0:T(8,128)(2,1)S(1)}, bf16[288,128]{1,0:T(8,128)(2,1)S(1)}, u32[]{:S(2)}, u32[]{:S(2)}) collective-permute-start(bf16[288,128]{1,0:T(8,128)(2,1)S(1)} %join8.1.refs_0_), channel_id=1, source_target_pairs={{0,4},{1,5},{2,6},{3,7},{4,0},{5,1},{6,2},{7,3},{8,12},{9,13},{10,... | collective-permute-start | bytes 221192 | tf_op jit(solution)/shard_map/ppermute | solution.py:224
  9.8 2.8 %collective-permute-done.1.refs_1_ = bf16[288,128]{1,0:T(8,128)(2,1)S(1)} collective-permute-done((bf16[288,128]{1,0:T(8,128)(2,1)S(1)}, bf16[288,128]{1,0:T(8,128)(2,1)S(1)}, u32[]{:S(2)}, u32[]{:S(2)}) %collective-permute-start.1) | collective-permute-done | bytes 73760 | tf_op jit(solution)/shard_map/ppermute | solution.py:224
  12.7 2.7 %collective-permute-start.4 = (bf16[576,128]{1,0:T(8,128)(2,1)S(1)}, bf16[576,128]{1,0:T(8,128)(2,1)S(1)}, u32[]{:S(2)}, u32[]{:S(2)}) collective-permute-start(bf16[576,128]{1,0:T(8,128)(2,1)S(1)} %join4.1.refs_4_), channel_id=1, source_target_pairs={{0,3},{1,2},{2,1},{3,0},{4,7},{5,6},{6,5},{7,4},{8,11},{9,10},{10,... | collective-permute-start | bytes 442376 | tf_op jit(solution)/shard_map/ppermute | solution.py:224
  15.4 0.5 collective-permute-start.3
  15.9 0.3 collective-permute-start.2
  16.2 0.0 collective-permute-start.5
  16.2 3.1 %collective-permute-done.4.refs_7_ = bf16[576,128]{1,0:T(8,128)(2,1)S(1)} collective-permute-done((bf16[576,128]{1,0:T(8,128)(2,1)S(1)}, bf16[576,128]{1,0:T(8,128)(2,1)S(1)}, u32[]{:S(2)}, u32[]{:S(2)}) %collective-permute-start.4) | collective-permute-done | bytes 147488 | tf_op jit(solution)/shard_map/ppermute | solution.py:224
  19.3 0.0 collective-permute-start.8
  19.3 1.5 %collective-permute-done.3.refs_6_ = bf16[576,128]{1,0:T(8,128)(2,1)S(1)} collective-permute-done((bf16[576,128]{1,0:T(8,128)(2,1)S(1)}, bf16[576,128]{1,0:T(8,128)(2,1)S(1)}, u32[]{:S(2)}, u32[]{:S(2)}) %collective-permute-start.3) | collective-permute-done | bytes 147488 | tf_op jit(solution)/shard_map/ppermute | solution.py:224
  20.9 0.0 collective-permute-start.7
  20.9 0.1 collective-permute-done.2.refs_5_
  21.0 0.4 collective-permute-start.6
  21.4 0.0 collective-permute-done.5.refs_8_
  21.4 0.0 collective-permute-done.8.refs_11_
  21.4 0.9 collective-permute-done.7.refs_10_
  22.3 0.2 collective-permute-done.6.refs_9_
  22.5 8.8 %long_start.1 = (bf16[4608,128]{1,0:T(8,128)(2,1)}, bf16[272,256]{1,0:T(8,128)(2,1)}, bf16[256,256]{1,0:T(8,128)(2,1)}, f32[272,512]{1,0:T(8,128)}, f32[256,512]...) custom-call(s32[1,256]{1,0:T(1,128)S(1)} %get-tuple-element.76.refs_, ...), custom_call_target="tpu_custom_call" | custom-call | flops 8589934592 | bytes 1048576 | tf_op jit(solution)/shard_map/long_start/pallas_call | solution.py:89
  31.3 6.2 %all-to-all-start = ((bf16[16,288,128]{2,1,0:T(8,128)(2,1)}), bf16[16,288,128]{2,1,0:T(8,128)(2,1)}, u32[]{:S(2)}, u32[]{:S(2)}) async-start(bf16[16,288,128]{2,1,0:T(8,128)(2,1)} %bitcast.47), calls=%async_computation | async-start | bytes 2359296 | tf_op jit(solution)/shard_map/all_to_all | solution.py:1160
  37.5 28.2 %short_windows.1 = (f32[1024,256]{1,0:T(8,128)}, f32[512,256]{1,0:T(8,128)}, f32[128,512]{1,0:T(8,128)}, f32[8,256]{1,0:T(8,128)}, f32[528,256]{1,0:T(8,128)}, /*index=5*/bf16[512,512]{1,0:T(8,128)(2,1)}) custom-call(s32[1,256]{1,0:T(1,128)} %bitcast.36, bf16[256,256]{1,0:T(8,128)(2,1)} %bitcast.41, bf16[256,256]{1,0:T(8,128)(2,1)} %bitcast.43, ...), custom_call_target="tpu_custom_call" | custom-call | flops 68719476736 | bytes 1048576 | tf_op jit(solution)/shard_map/short_windows/pallas_call | solution.py:89
  65.7 0.0 all-to-all-done
  65.7 0.0 copy-start
  65.8 0.0 copy-start.1
  65.8 0.0 copy-start.2
  65.8 0.0 copy-start.3
  65.8 0.0 copy-start.4
  65.8 0.0 copy-start.5
  65.8 0.0 copy-start.6
  65.8 0.0 copy-start.7
  65.8 0.0 copy-start.8
  65.9 0.0 copy-start.10
  65.9 0.0 copy-start.12
  65.9 16.3 %long_windows.1 = (f32[272,256]{1,0:T(8,128)}, bf16[256,512]{1,0:T(8,128)(2,1)}, bf16[1792,128]{1,0:T(8,128)(2,1)S(1)}, bf16[2304,128]{1,0:T(8,128)(2,1)S(1)}) custom-call(bf16[4608,128]{1,0:T(8,128)(2,1)} %bitcast.10.refs_0_, s32[1,256]{1,0:T(1,128)} %bitcast.37, bf16[16,256]{1,0:T(8,128)(2,1)} %get-tuple-element.84.refs_2_, ...), custom_call_target="tpu_custom_call" | custom-call | flops 34359738368 | bytes 1048576 | tf_op jit(solution)/shard_map/long_windows/pallas_call | solution.py:89
  82.2 0.1 collective-permute-start.9
  82.3 1.8 %collective-permute-done.9.refs_0_ = bf16[1792,128]{1,0:T(8,128)(2,1)S(1)} collective-permute-done((bf16[1792,128]{1,0:T(8,128)(2,1)S(1)}, bf16[1792,128]{1,0:T(8,128)(2,1)S(1)}, u32[]{:S(2)}, u32[]{:S(2)}) %collective-permute-start.9) | collective-permute-done | bytes 458784 | tf_op jit(solution)/shard_map/ppermute | solution.py:937
  84.1 0.2 add_core.1
  84.3 1.9 %collective-permute-start.10 = (bf16[576,128]{1,0:T(8,128)(2,1)S(1)}, bf16[576,128]{1,0:T(8,128)(2,1)S(1)}, u32[]{:S(2)}, u32[]{:S(2)}) collective-permute-start(bf16[576,128]{1,0:T(8,128)(2,1)S(1)} %get-tuple-element.119), channel_id=1, source_target_pairs={{0,1},{1,0},{2,3},{3,2},{4,5},{5,4},{6,7},{7,6},{8,9},{9,8},{10,11... | collective-permute-start | bytes 442376 | tf_op jit(solution)/shard_map/ppermute | solution.py:935
  86.3 1.5 %collective-permute-start.11 = (bf16[576,128]{1,0:T(8,128)(2,1)S(1)}, bf16[576,128]{1,0:T(8,128)(2,1)S(1)}, u32[]{:S(2)}, u32[]{:S(2)}) collective-permute-start(bf16[576,128]{1,0:T(8,128)(2,1)S(1)} %get-tuple-element.120), channel_id=1, source_target_pairs={{0,2},{1,3},{2,0},{3,1},{4,6},{5,7},{6,4},{7,5},{8,10},{9,11},{10,... | collective-permute-start | bytes 442376 | tf_op jit(solution)/shard_map/ppermute | solution.py:935
  87.7 0.2 collective-permute-start.12
  87.9 0.0 copy-done
  87.9 0.0 copy-done.1
  87.9 0.0 copy-done.2
  87.9 0.0 copy-done.3
  87.9 0.0 copy-done.4
  87.9 0.0 copy-done.5
  87.9 0.0 copy-done.6
  87.9 0.0 copy-done.7
  87.9 0.0 copy-done.8
  88.0 0.0 copy-done.10
  88.0 0.0 copy-done.12
  88.0 0.9 copy-done.9
  88.9 0.9 copy-done.11
  89.9 2.7 %outputs.1 = (bf16[128,256]{1,0:T(8,128)(2,1)}, f32[128,256]{1,0:T(8,128)S(1)}, bf16[256,256]{1,0:T(8,128)(2,1)}, f32[256,256]{1,0:T(8,128)}, f32[8,128]{1,0:T(8,128)S(1)}) custom-call(s32[1,256]{1,0:T(1,128)S(1)} %bitcast.38, bf16[512,256]{1,0:T(8,128)(2,1)S(1)} %copy-done.10, f32[8,256]{1,0:T(8,128)S(1)} %copy-done.12, bf16[128,256]{1,0:T(8,128)(2,1)S(1)} %bitcast.32, ...), custom_call_target="tpu_custom_call" | custom-call | flops 4294967296 | bytes 1048576 | tf_op jit(solution)/shard_map/outputs/pallas_call | solution.py:89
  92.6 0.0 collective-permute-done.10.refs_2_
  92.6 2.5 %collective-permute-done.11.refs_3_ = bf16[576,128]{1,0:T(8,128)(2,1)S(1)} collective-permute-done((bf16[576,128]{1,0:T(8,128)(2,1)S(1)}, bf16[576,128]{1,0:T(8,128)(2,1)S(1)}, u32[]{:S(2)}, u32[]{:S(2)}) %collective-permute-start.11) | collective-permute-done | bytes 147488 | tf_op jit(solution)/shard_map/ppermute | solution.py:935
  95.0 0.0 collective-permute-done.12.refs_4_
  95.0 0.1 add_near.1
  95.1 2.4 %collective-permute-start.13 = (bf16[288,128]{1,0:T(8,128)(2,1)S(1)}, bf16[288,128]{1,0:T(8,128)(2,1)S(1)}, u32[]{:S(2)}, u32[]{:S(2)}) collective-permute-start(bf16[288,128]{1,0:T(8,128)(2,1)S(1)} %get-tuple-element.123), channel_id=1, source_target_pairs={{0,8},{1,9},{2,10},{3,11},{4,12},{5,13},{6,14},{7,15},{8,0},{9,1},... | collective-permute-start | bytes 221192 | tf_op jit(solution)/shard_map/ppermute | solution.py:935
  97.6 3.2 %collective-permute-done.13.refs_1_ = bf16[288,128]{1,0:T(8,128)(2,1)S(1)} collective-permute-done((bf16[288,128]{1,0:T(8,128)(2,1)S(1)}, bf16[288,128]{1,0:T(8,128)(2,1)S(1)}, u32[]{:S(2)}, u32[]{:S(2)}) %collective-permute-start.13) | collective-permute-done | bytes 73760 | tf_op jit(solution)/shard_map/ppermute | solution.py:935
  100.8 1.5 %collective-permute-start.14 = (bf16[144,128]{1,0:T(8,128)(2,1)S(1)}, bf16[144,128]{1,0:T(8,128)(2,1)S(1)}, u32[]{:S(2)}, u32[]{:S(2)}) collective-permute-start(bf16[144,128]{1,0:T(8,128)(2,1)S(1)} %get-tuple-element.125), channel_id=1, source_target_pairs={{0,4},{1,5},{2,6},{3,7},{4,0},{5,1},{6,2},{7,3},{8,12},{9,13},{10,... | collective-permute-start | bytes 110600 | tf_op jit(solution)/shard_map/ppermute | solution.py:935
  102.3 2.5 %collective-permute-done.14.refs_2_ = bf16[144,128]{1,0:T(8,128)(2,1)S(1)} collective-permute-done((bf16[144,128]{1,0:T(8,128)(2,1)S(1)}, bf16[144,128]{1,0:T(8,128)(2,1)S(1)}, u32[]{:S(2)}, u32[]{:S(2)}) %collective-permute-start.14) | collective-permute-done | bytes 36896 | tf_op jit(solution)/shard_map/ppermute | solution.py:935
  104.8 0.8 final.1
  (5 shorter events, 0.0 us)
Async XLA Ops:
  1.9 6.4 %collective-permute-start = (bf16[144,128]{1,0:T(8,128)(2,1)S(1)}, bf16[144,128]{1,0:T(8,128)(2,1)S(1)}, u32[]{:S(2)}, u32[]{:S(2)}) collective-permute-start(bf16[144,128]{1,0:T(8,128)(2,1)S(1)} %get-tuple-element.80.refs_0_), channel_id=1, source_target_pairs={{0,8},{1,9},{2,10},{3,11},{4,12},{5,13},{6,14},{7,15},{8,0},{9,1},... | collective-permute-start | bytes 110600 | tf_op jit(solution)/shard_map/ppermute | solution.py:224
  8.3 4.4 %collective-permute-start.1 = (bf16[288,128]{1,0:T(8,128)(2,1)S(1)}, bf16[288,128]{1,0:T(8,128)(2,1)S(1)}, u32[]{:S(2)}, u32[]{:S(2)}) collective-permute-start(bf16[288,128]{1,0:T(8,128)(2,1)S(1)} %join8.1.refs_0_), channel_id=1, source_target_pairs={{0,4},{1,5},{2,6},{3,7},{4,0},{5,1},{6,2},{7,3},{8,12},{9,13},{10,... | collective-permute-start | bytes 221192 | tf_op jit(solution)/shard_map/ppermute | solution.py:224
  12.7 6.7 %collective-permute-start.4 = (bf16[576,128]{1,0:T(8,128)(2,1)S(1)}, bf16[576,128]{1,0:T(8,128)(2,1)S(1)}, u32[]{:S(2)}, u32[]{:S(2)}) collective-permute-start(bf16[576,128]{1,0:T(8,128)(2,1)S(1)} %join4.1.refs_4_), channel_id=1, source_target_pairs={{0,3},{1,2},{2,1},{3,0},{4,7},{5,6},{6,5},{7,4},{8,11},{9,10},{10,... | collective-permute-start | bytes 442376 | tf_op jit(solution)/shard_map/ppermute | solution.py:224
  15.4 5.5 %collective-permute-start.3 = (bf16[576,128]{1,0:T(8,128)(2,1)S(1)}, bf16[576,128]{1,0:T(8,128)(2,1)S(1)}, u32[]{:S(2)}, u32[]{:S(2)}) collective-permute-start(bf16[576,128]{1,0:T(8,128)(2,1)S(1)} %join4.1.refs_4_), channel_id=1, source_target_pairs={{0,2},{1,3},{2,0},{3,1},{4,6},{5,7},{6,4},{7,5},{8,10},{9,11},{10,... | collective-permute-start | bytes 442376 | tf_op jit(solution)/shard_map/ppermute | solution.py:224
  15.9 5.1 %collective-permute-start.2 = (bf16[576,128]{1,0:T(8,128)(2,1)S(1)}, bf16[576,128]{1,0:T(8,128)(2,1)S(1)}, u32[]{:S(2)}, u32[]{:S(2)}) collective-permute-start(bf16[576,128]{1,0:T(8,128)(2,1)S(1)} %join4.1.refs_4_), channel_id=1, source_target_pairs={{0,1},{1,0},{2,3},{3,2},{4,5},{5,4},{6,7},{7,6},{8,9},{9,8},{10,11... | collective-permute-start | bytes 442376 | tf_op jit(solution)/shard_map/ppermute | solution.py:224
  16.2 5.2 %collective-permute-start.5 = (bf16[576,128]{1,0:T(8,128)(2,1)S(1)}, bf16[576,128]{1,0:T(8,128)(2,1)S(1)}, u32[]{:S(2)}, u32[]{:S(2)}) collective-permute-start(bf16[576,128]{1,0:T(8,128)(2,1)S(1)} %join4.1.refs_4_), channel_id=1, source_target_pairs={{0,16},{16,0},{1,17},{17,1},{2,18},{18,2},{3,19},{19,3},{4,20},{20... | collective-permute-start | bytes 442376 | tf_op jit(solution)/shard_map/ppermute | solution.py:235
  19.3 2.1 %collective-permute-start.8 = (bf16[576,128]{1,0:T(8,128)(2,1)S(1)}, bf16[576,128]{1,0:T(8,128)(2,1)S(1)}, u32[]{:S(2)}, u32[]{:S(2)}) collective-permute-start(bf16[576,128]{1,0:T(8,128)(2,1)S(1)} %collective-permute-done.4.refs_7_), channel_id=1, source_target_pairs={{0,16},{16,0},{1,17},{17,1},{2,18},{18,2},{3,19},{19,3},{4,20},{20... | collective-permute-start | bytes 442376 | tf_op jit(solution)/shard_map/ppermute | solution.py:235
  20.9 1.4 %collective-permute-start.7 = (bf16[576,128]{1,0:T(8,128)(2,1)S(1)}, bf16[576,128]{1,0:T(8,128)(2,1)S(1)}, u32[]{:S(2)}, u32[]{:S(2)}) collective-permute-start(bf16[576,128]{1,0:T(8,128)(2,1)S(1)} %collective-permute-done.3.refs_6_), channel_id=1, source_target_pairs={{0,16},{16,0},{1,17},{17,1},{2,18},{18,2},{3,19},{19,3},{4,20},{20... | collective-permute-start | bytes 442376 | tf_op jit(solution)/shard_map/ppermute | solution.py:235
  21.0 1.4 %collective-permute-start.6 = (bf16[576,128]{1,0:T(8,128)(2,1)S(1)}, bf16[576,128]{1,0:T(8,128)(2,1)S(1)}, u32[]{:S(2)}, u32[]{:S(2)}) collective-permute-start(bf16[576,128]{1,0:T(8,128)(2,1)S(1)} %collective-permute-done.2.refs_5_), channel_id=1, source_target_pairs={{0,16},{16,0},{1,17},{17,1},{2,18},{18,2},{3,19},{19,3},{4,20},{20... | collective-permute-start | bytes 442376 | tf_op jit(solution)/shard_map/ppermute | solution.py:235
  31.3 34.4 %all-to-all-start = ((bf16[16,288,128]{2,1,0:T(8,128)(2,1)}), bf16[16,288,128]{2,1,0:T(8,128)(2,1)}, u32[]{:S(2)}, u32[]{:S(2)}) async-start(bf16[16,288,128]{2,1,0:T(8,128)(2,1)} %bitcast.47), calls=%async_computation | async-start | bytes 2359296 | tf_op jit(solution)/shard_map/all_to_all | solution.py:1160
  65.7 22.1 %copy-start = (bf16[2,1,64,256]{3,2,1,0:T(8,128)(2,1)S(1)}, bf16[2,1,64,256]{3,2,1,0:T(8,128)(2,1)}, u32[]{:S(2)}) copy-start(bf16[2,1,64,256]{3,2,1,0:T(8,128)(2,1)} %param.17) | copy-start | bytes 196612
  65.8 22.1 %copy-start.1 = (bf16[2,1,64,256]{3,2,1,0:T(8,128)(2,1)S(1)}, bf16[2,1,64,256]{3,2,1,0:T(8,128)(2,1)}, u32[]{:S(2)}) copy-start(bf16[2,1,64,256]{3,2,1,0:T(8,128)(2,1)} %param.19) | copy-start | bytes 196612
  65.8 22.1 %copy-start.2 = (s32[256]{0:T(256)S(1)}, s32[256]{0:T(256)}, u32[]{:S(2)}) copy-start(s32[256]{0:T(256)} %param.23) | copy-start | bytes 3076
  65.8 22.1 %copy-start.3 = (s32[2,1,64]{2,1,0:T(1,128)S(1)}, s32[2,1,64]{2,1,0:T(1,128)}, u32[]{:S(2)}) copy-start(s32[2,1,64]{2,1,0:T(1,128)} %param.21) | copy-start | bytes 1540
  65.8 22.1 %copy-start.4 = (bf16[2,1,128,256]{3,2,1,0:T(8,128)(2,1)S(1)}, bf16[2,1,128,256]{3,2,1,0:T(8,128)(2,1)}, u32[]{:S(2)}) copy-start(bf16[2,1,128,256]{3,2,1,0:T(8,128)(2,1)} %param.18) | copy-start | bytes 393220
  65.8 22.1 %copy-start.5 = (bf16[2,1,128,256]{3,2,1,0:T(8,128)(2,1)S(1)}, bf16[2,1,128,256]{3,2,1,0:T(8,128)(2,1)}, u32[]{:S(2)}) copy-start(bf16[2,1,128,256]{3,2,1,0:T(8,128)(2,1)} %param.20) | copy-start | bytes 393220
  65.8 22.1 %copy-start.6 = (s32[2,1,128]{2,1,0:T(1,128)S(1)}, s32[2,1,128]{2,1,0:T(1,128)}, u32[]{:S(2)}) copy-start(s32[2,1,128]{2,1,0:T(1,128)} %param.22) | copy-start | bytes 3076
  65.8 22.1 %copy-start.7 = (f32[528,256]{1,0:T(8,128)S(1)}, f32[528,256]{1,0:T(8,128)}, u32[]{:S(2)}) copy-start(f32[528,256]{1,0:T(8,128)} %get-tuple-element.111.refs_12_) | copy-start | bytes 1622020
  65.8 22.1 %copy-start.8 = (bf16[512,512]{1,0:T(8,128)(2,1)S(1)}, bf16[512,512]{1,0:T(8,128)(2,1)}, u32[]{:S(2)}) copy-start(bf16[512,512]{1,0:T(8,128)(2,1)} %get-tuple-element.110.refs_11_) | copy-start | bytes 1572868
  65.9 22.1 %copy-start.10 = (bf16[512,256]{1,0:T(8,128)(2,1)S(1)}, bf16[512,256]{1,0:T(8,128)(2,1)}, u32[]{:S(2)}) copy-start(bf16[512,256]{1,0:T(8,128)(2,1)} %get-tuple-element.81.refs_5_.refs_8_.refs_1_) | copy-start | bytes 786436
  65.9 22.1 %copy-start.12 = (f32[8,256]{1,0:T(8,128)S(1)}, f32[8,256]{1,0:T(8,128)}, u32[]{:S(2)}) copy-start(f32[8,256]{1,0:T(8,128)} %get-tuple-element.82.refs_7_.refs_6_.refs_2_) | copy-start | bytes 24580
  82.2 1.9 %collective-permute-start.9 = (bf16[1792,128]{1,0:T(8,128)(2,1)S(1)}, bf16[1792,128]{1,0:T(8,128)(2,1)S(1)}, u32[]{:S(2)}, u32[]{:S(2)}) collective-permute-start(bf16[1792,128]{1,0:T(8,128)(2,1)S(1)} %get-tuple-element.115), channel_id=1, source_target_pairs={{0,16},{16,0},{1,17},{17,1},{2,18},{18,2},{3,19},{19,3},{4,20},{20... | collective-permute-start | bytes 1376264 | tf_op jit(solution)/shard_map/ppermute | solution.py:937
  84.3 8.2 %collective-permute-start.10 = (bf16[576,128]{1,0:T(8,128)(2,1)S(1)}, bf16[576,128]{1,0:T(8,128)(2,1)S(1)}, u32[]{:S(2)}, u32[]{:S(2)}) collective-permute-start(bf16[576,128]{1,0:T(8,128)(2,1)S(1)} %get-tuple-element.119), channel_id=1, source_target_pairs={{0,1},{1,0},{2,3},{3,2},{4,5},{5,4},{6,7},{7,6},{8,9},{9,8},{10,11... | collective-permute-start | bytes 442376 | tf_op jit(solution)/shard_map/ppermute | solution.py:935
  86.3 8.8 %collective-permute-start.11 = (bf16[576,128]{1,0:T(8,128)(2,1)S(1)}, bf16[576,128]{1,0:T(8,128)(2,1)S(1)}, u32[]{:S(2)}, u32[]{:S(2)}) collective-permute-start(bf16[576,128]{1,0:T(8,128)(2,1)S(1)} %get-tuple-element.120), channel_id=1, source_target_pairs={{0,2},{1,3},{2,0},{3,1},{4,6},{5,7},{6,4},{7,5},{8,10},{9,11},{10,... | collective-permute-start | bytes 442376 | tf_op jit(solution)/shard_map/ppermute | solution.py:935
  87.7 7.3 %collective-permute-start.12 = (bf16[576,128]{1,0:T(8,128)(2,1)S(1)}, bf16[576,128]{1,0:T(8,128)(2,1)S(1)}, u32[]{:S(2)}, u32[]{:S(2)}) collective-permute-start(bf16[576,128]{1,0:T(8,128)(2,1)S(1)} %get-tuple-element.121), channel_id=1, source_target_pairs={{0,3},{1,2},{2,1},{3,0},{4,7},{5,6},{6,5},{7,4},{8,11},{9,10},{10,... | collective-permute-start | bytes 442376 | tf_op jit(solution)/shard_map/ppermute | solution.py:935
  88.0 1.0 copy-start.9
  88.9 0.9 copy-start.11
  95.1 5.6 %collective-permute-start.13 = (bf16[288,128]{1,0:T(8,128)(2,1)S(1)}, bf16[288,128]{1,0:T(8,128)(2,1)S(1)}, u32[]{:S(2)}, u32[]{:S(2)}) collective-permute-start(bf16[288,128]{1,0:T(8,128)(2,1)S(1)} %get-tuple-element.123), channel_id=1, source_target_pairs={{0,8},{1,9},{2,10},{3,11},{4,12},{5,13},{6,14},{7,15},{8,0},{9,1},... | collective-permute-start | bytes 221192 | tf_op jit(solution)/shard_map/ppermute | solution.py:935
  100.8 4.0 %collective-permute-start.14 = (bf16[144,128]{1,0:T(8,128)(2,1)S(1)}, bf16[144,128]{1,0:T(8,128)(2,1)S(1)}, u32[]{:S(2)}, u32[]{:S(2)}) collective-permute-start(bf16[144,128]{1,0:T(8,128)(2,1)S(1)} %get-tuple-element.125), channel_id=1, source_target_pairs={{0,4},{1,5},{2,6},{3,7},{4,0},{5,1},{6,2},{7,3},{8,12},{9,13},{10,... | collective-permute-start | bytes 110600 | tf_op jit(solution)/shard_map/ppermute | solution.py:935

commit v4 on v3

--- a/solution.py
+++ b/solution.py
@@ -66,7 +66,7 @@
     lax.fori_loop(0, count, lambda i, c: (body(i), c)[1], 0)
 
 
-def run(name, body, ins, outs, scratch=None, flops=0, far=(), early=(), placed=(), pin=None, vmem=60):
+def run(name, body, ins, outs, scratch=None, flops=0, far=(), early=(), placed=(), pin=None, hold=(), vmem=60):
     scratch = dict(scratch or {}, **{k: outs[k] for k in early})
     scratch.update({k: (ins[k].shape, ins[k].dtype) for k in far})
     if far:
@@ -85,6 +85,11 @@
 
     def spec(key):
         return pl.BlockSpec(memory_space=pltpu.HBM if key in far else pltpu.VMEM)
+
+    def at(key, value):
+        if key in hold or key in far:
+            return pltpu.with_memory_space_constraint(value, pltpu.HBM if key in far else pltpu.VMEM)
+        return value
 
     result = pl.pallas_call(
         kernel,
@@ -103,7 +108,7 @@
         compiler_params=pltpu.CompilerParams(vmem_limit_bytes=vmem << 20),
         cost_estimate=pl.CostEstimate(flops=flops, bytes_accessed=1 << 20, transcendentals=0),
         name=name,
-    )(*ins.values())
+    )(*(at(k, v) for k, v in ins.items()))
     return dict(zip(outs, result))
 
 
@@ -161,7 +166,7 @@
         low = 2 * IN_ROWS + half * OUT_ROWS
         r.buf[low : low + OUT_ROWS, :] = out_w[:, lanes]
     r.buf[PACK - CH_ROWS : PACK, :] = chan
-    for name in ("comp", "tok", "cot", "mask"):
+    for name in ("comp", "tok", "cot", "mask", "s_tok", "s_cot", "s_mask"):
         getattr(r, name + "_near")[...] = getattr(r, name)[...]
     T = r.tok.shape[0] // MB
     for which, first in enumerate((T - 16, 0)):
@@ -558,8 +563,8 @@
     )
 
 
-LATE = ("ip", "inner", "slope", "silu", "gslope", "sz", "V", "GR", "xwT", "rate")
-LATE_LONG = LATE + ("inT", "outw", "dtw2")
+LATE = ("ip", "inner", "slope", "silu", "gslope", "sz", "V", "GR")
+LATE_LONG = LATE
 
 
 def post(r, T, halo):
@@ -810,7 +815,6 @@
             unpack(r)
             r.gain[...] = gain_of(r)
         derive(r)
-        send(r, *(k for k in r.early if k not in PREP_OUTS))
 
     prep(r, T, True, ready)
     send(r, *PREP_OUTS)
@@ -833,7 +837,7 @@
 
 
 FROM_SHORT = ("s_inT", "s_out", "s_peT", "s_gain")
-LONG_FIRST = ("sel", "elements", "r2", "st", "si", "gm")
+LONG_FIRST = ("sel", "st", "si", "gm")
 LONG_FAR = LONG_FIRST + LATE_LONG + FROM_SHORT
 
 
@@ -841,13 +845,11 @@
     fetch(r, *LONG_FIRST)
     arrived(r, "sel")
     maps(r, T)
-    arrived(r, "elements", "r2")
     enter(r)
     arrived(r, "st", "si", "gm")
     fetch(r, *LATE_LONG, *FROM_SHORT)
     scan_forward(r, T, r.entering, True)
     scan_backward(r, T, r.entering)
-    arrived(r, "inT", "outw", "dtw2")
     post(r, T, True)
     param_grads(r)
     arrived(r, *FROM_SHORT)
@@ -906,8 +908,6 @@
 
 
 def add_core_body(r):
-    fetch(r, "keep")
-    arrived(r, "keep")
     for near in range(4):
         part = getattr(r, f"part{near}")
         for q in range(4):
@@ -941,7 +941,7 @@
         add_core_body,
         dict(got=got, keep=keep),
         {f"part{i}": four for i in range(4)},
-        far=("keep",),
+        hold=("keep", "got"),
         vmem=8,
     )
     near = {f"got{i}": swapped(parts[f"part{i}"], i) for i in range(1, 4)}
@@ -1061,7 +1061,7 @@
     long_in = tokens_of(long_tokens, long_cotangent, long_mask)
     short_in = tokens_of(short_tokens, short_cotangent, short_mask)
 
-    near = dict(comp=comp, **long_in)
+    near = dict(comp=comp, **long_in, **{"s_" + k: v for k, v in short_in.items()})
 
     if packed:
         packing = run(
@@ -1078,8 +1078,7 @@
                 a_log=a_log,
                 skip=d_skip.reshape(1, -1),
                 out_w=out_weight,
-                comp=comp,
-                **long_in,
+                **near,
             ),
             dict(
                 buf=((GATHER, LT), BF),
@@ -1130,7 +1129,7 @@
     started = run(
         "long_start",
         functools.partial(long_start_body, T=span, packed=packed),
-        dict(near, **weights_in),
+        dict({k: near[k] for k in ("comp", *long_in)}, **weights_in),
         dict(
             carry=((count * ELEMENT, LT), BF), **prep_outs(span), **derived, **(unpacked if packed else {})
         ),
@@ -1145,12 +1144,12 @@
             **(dict(edges=((count * 2 * EDGE, LT), BF)) if packed else {}),
         ),
         flops=1 << 33,
-        early=PREP_OUTS + tuple(derived) + (tuple(unpacked) if packed else ()),
+        early=PREP_OUTS,
         placed=("carry",),
-        pin={
-            k: pltpu.HBM
-            for k in PREP_OUTS + tuple(derived) + (tuple(unpacked) if packed else ()) + ("carry",)
-        },
+        pin=dict(
+            {k: pltpu.HBM for k in PREP_OUTS + ("carry",)},
+            **{k: pltpu.VMEM for k in (*derived, *(unpacked if packed else ()))},
+        ),
         vmem=40,
     )
     weights = {k: started[k] for k in derived}
@@ -1162,8 +1161,8 @@
         "short_windows",
         functools.partial(short_windows_body, T=short),
         dict(
-            comp=comp,
-            **short_in,
+            comp=near["comp"],
+            **{k: near["s_" + k] for k in short_in},
             **{
                 k: weights[k]
                 for k in ("inT", "outw", "pe", "gain", "dtw2", "xwT", "rowp", "r2", "rate")
@@ -1176,7 +1175,8 @@
             if k != "gated"
         },
         flops=1 << 36,
-        vmem=63,
+        hold=("inT", "outw", "pe", "dtw2", "xwT", "rowp", "r2", "rate", "gain", "comp", "tok", "cot", "mask"),
+        vmem=56,
     )
 
     ins = dict(
@@ -1205,8 +1205,9 @@
         outs,
         scratch,
         flops=1 << 35,
-        far=tuple(k for k in LONG_FAR),
-        pin=dict(give=pltpu.VMEM, keep=pltpu.VMEM) if packed else None,
+        far=LONG_FAR,
+        hold=(*(("elements",) if packed else ()), "edge", "r2", "rowp", "rate", "gain", "inT", "outw", "xwT", "dtw2"),
+        pin={k: pltpu.VMEM for k in ("rows", "gated", *(("give", "keep") if packed else ()))},
         vmem=56,
     )
 
@@ -1224,7 +1225,7 @@
         s_gated=shorts["gated"],
         s_rows=shorts["rows"],
     )
-    finished = run("outputs", outputs_body, ins, outs, flops=1 << 32, vmem=32)
+    finished = run("outputs", outputs_body, ins, outs, flops=1 << 32, hold=("l_rows", "l_gated"), vmem=32)
     ins = dict(ing=finished["l_ing"])
     outs = dict(grad=((MB * span, D), F32))
     if packed:

time: 106 us -> 104 us (0.981)
  Pallas kernels: 58.4 us -> 55.9 us
  local copies, waits for them, and re-layouts: 1.96 us -> 0.04 us
  waiting for transfers between devices: 21 us -> 22.8 us
  starting transfers between devices: 23.3 us -> 24.5 us
    pallas_call x11, Pallas kernels: 58.4 us -> 55.9 us  [run(): pl.pallas_call(kernel, out_shape=tuple((pin[k](*v) if pin and k in pin el...]
    unnamed x26 -> x18, local copies, waits for them, and re-layouts: 1.96 us -> 0.04 us
    ppermute x10, waiting for transfers between devices: 18.2 us -> 19.6 us  [swapped(): return lax.ppermute(x, 'seq', [(i, i ^ mask) for i in range(count)])]
    ppermute x10, starting transfers between devices: 16.6 us -> 17.9 us  [swapped(): return lax.ppermute(x, 'seq', [(i, i ^ mask) for i in range(count)])]
  transfers between devices with their start and end apart: 16 -> 16, of which waited for: 11 -> 14; matrix products, arithmetic and copies ran while one was open for 0% -> 0% of each run, Pallas kernels for 29% -> 28%
where the time goes in v4:
time: 104 us
  Pallas kernels  55.9 us (54%)
  starting transfers between devices  24.5 us (24%)
  waiting for transfers between devices  22.8 us (22%)
    pallas_call x11, Pallas kernels, run(): pl.pallas_call(kernel, out_shape=tuple((pin[k](*v) if pin and k in pin el...  55.9 us
    ppermute x10, waiting for transfers between devices, swapped(): return lax.ppermute(x, 'seq', [(i, i ^ mask) for i in range(count)])  19.6 us
    ppermute x10, starting transfers between devices, swapped(): return lax.ppermute(x, 'seq', [(i, i ^ mask) for i in range(count)])  17.9 us
    all_to_all x1, starting transfers between devices, local(): elements = lax.all_to_all(started['carry'], 'seq', 0, 0, tiled=True)  6.14 us
  transfers between devices with their start and end apart: 16, of which 14 were waited for; matrix products, arithmetic and copies ran while one was open for 0% of the time, Pallas kernels for 28%

profile of v4, /device:TPU:0, one launch (start us, length us, event | category | flops | bytes accessed | tf_op | source)
XLA Modules:
  0.0 104.0 jit_solution(7022474510068532552)
XLA Ops:
  0.6 1.4 %pack.1 = (bf16[144,128]{1,0:T(8,128)(2,1)S(1)}, s32[1,256]{1,0:T(1,128)S(1)}, bf16[128,256]{1,0:T(8,128)(2,1)S(1)}, bf16[128,256]{1,0:T(8,128)(2,1)S(1)}, s32[2...) custom-call(f32[1,8]{1,0:T(1,128)} %bitcast.49, ...), custom_call_target="tpu_custom_call" | custom-call | bytes 1048576 | tf_op jit(solution)/shard_map/pack/pallas_call | solution.py:94
  2.0 4.1 %collective-permute-start = (bf16[144,128]{1,0:T(8,128)(2,1)S(1)}, bf16[144,128]{1,0:T(8,128)(2,1)S(1)}, u32[]{:S(2)}, u32[]{:S(2)}) collective-permute-start(bf16[144,128]{1,0:T(8,128)(2,1)S(1)} %get-tuple-element.83.refs_0_), channel_id=1, source_target_pairs={{0,8},{1,9},{2,10},{3,11},{4,12},{5,13},{6,14},{7,15},{8,0},{9,1},... | collective-permute-start | bytes 110600 | tf_op jit(solution)/shard_map/ppermute | solution.py:229
  6.1 2.3 %collective-permute-done.refs_1_ = bf16[144,128]{1,0:T(8,128)(2,1)S(1)} collective-permute-done((bf16[144,128]{1,0:T(8,128)(2,1)S(1)}, bf16[144,128]{1,0:T(8,128)(2,1)S(1)}, u32[]{:S(2)}, u32[]{:S(2)}) %collective-permute-start) | collective-permute-done | bytes 36896 | tf_op jit(solution)/shard_map/ppermute | solution.py:229
  8.5 1.5 %collective-permute-start.1 = (bf16[288,128]{1,0:T(8,128)(2,1)S(1)}, bf16[288,128]{1,0:T(8,128)(2,1)S(1)}, u32[]{:S(2)}, u32[]{:S(2)}) collective-permute-start(bf16[288,128]{1,0:T(8,128)(2,1)S(1)} %join8.1.refs_0_), channel_id=1, source_target_pairs={{0,4},{1,5},{2,6},{3,7},{4,0},{5,1},{6,2},{7,3},{8,12},{9,13},{10,... | collective-permute-start | bytes 221192 | tf_op jit(solution)/shard_map/ppermute | solution.py:229
  10.0 2.8 %collective-permute-done.1.refs_1_ = bf16[288,128]{1,0:T(8,128)(2,1)S(1)} collective-permute-done((bf16[288,128]{1,0:T(8,128)(2,1)S(1)}, bf16[288,128]{1,0:T(8,128)(2,1)S(1)}, u32[]{:S(2)}, u32[]{:S(2)}) %collective-permute-start.1) | collective-permute-done | bytes 73760 | tf_op jit(solution)/shard_map/ppermute | solution.py:229
  12.8 2.7 %collective-permute-start.4 = (bf16[576,128]{1,0:T(8,128)(2,1)S(1)}, bf16[576,128]{1,0:T(8,128)(2,1)S(1)}, u32[]{:S(2)}, u32[]{:S(2)}) collective-permute-start(bf16[576,128]{1,0:T(8,128)(2,1)S(1)} %join4.1.refs_4_), channel_id=1, source_target_pairs={{0,3},{1,2},{2,1},{3,0},{4,7},{5,6},{6,5},{7,4},{8,11},{9,10},{10,... | collective-permute-start | bytes 442376 | tf_op jit(solution)/shard_map/ppermute | solution.py:229
  15.6 0.5 collective-permute-start.3
  16.1 0.3 collective-permute-start.2
  16.4 0.0 collective-permute-start.5
  16.4 3.1 %collective-permute-done.4.refs_7_ = bf16[576,128]{1,0:T(8,128)(2,1)S(1)} collective-permute-done((bf16[576,128]{1,0:T(8,128)(2,1)S(1)}, bf16[576,128]{1,0:T(8,128)(2,1)S(1)}, u32[]{:S(2)}, u32[]{:S(2)}) %collective-permute-start.4) | collective-permute-done | bytes 147488 | tf_op jit(solution)/shard_map/ppermute | solution.py:229
  19.5 0.0 collective-permute-start.8
  19.5 1.5 %collective-permute-done.3.refs_6_ = bf16[576,128]{1,0:T(8,128)(2,1)S(1)} collective-permute-done((bf16[576,128]{1,0:T(8,128)(2,1)S(1)}, bf16[576,128]{1,0:T(8,128)(2,1)S(1)}, u32[]{:S(2)}, u32[]{:S(2)}) %collective-permute-start.3) | collective-permute-done | bytes 147488 | tf_op jit(solution)/shard_map/ppermute | solution.py:229
  21.1 0.0 collective-permute-start.7
  21.1 0.1 collective-permute-done.2.refs_5_
  21.2 0.4 collective-permute-start.6
  21.6 0.0 collective-permute-done.5.refs_8_
  21.6 0.0 collective-permute-done.8.refs_11_
  21.6 0.9 collective-permute-done.7.refs_10_
  22.4 0.2 collective-permute-done.6.refs_9_
  22.6 8.7 %long_start.1 = (bf16[4608,128]{1,0:T(8,128)(2,1)}, bf16[272,256]{1,0:T(8,128)(2,1)}, bf16[256,256]{1,0:T(8,128)(2,1)}, f32[272,512]{1,0:T(8,128)}, f32[256,512]...) custom-call(s32[1,256]{1,0:T(1,128)S(1)} %get-tuple-element.79.refs_, ...), custom_call_target="tpu_custom_call" | custom-call | flops 8589934592 | bytes 1048576 | tf_op jit(solution)/shard_map/long_start/pallas_call | solution.py:94
  31.3 6.1 %all-to-all-start = ((bf16[16,288,128]{2,1,0:T(8,128)(2,1)}), bf16[16,288,128]{2,1,0:T(8,128)(2,1)S(1)}, u32[]{:S(2)}, u32[]{:S(2)}) async-start(bf16[16,288,128]{2,1,0:T(8,128)(2,1)} %bitcast.47), calls=%async_computation | async-start | bytes 2359296 | tf_op jit(solution)/shard_map/all_to_all | solution.py:1159
  37.5 26.8 %short_windows.1 = (f32[1024,256]{1,0:T(8,128)}, f32[512,256]{1,0:T(8,128)}, f32[128,512]{1,0:T(8,128)}, f32[8,256]{1,0:T(8,128)}, f32[528,256]{1,0:T(8,128)}, /*index=5*/bf16[512,512]{1,0:T(8,128)(2,1)}) custom-call(s32[1,256]{1,0:T(1,128)S(1)} %get-tuple-element.79.refs_0_, bf16[256,256]{1,0:T(8,128)(2,1)S(1)} %get-tuple-element.106.refs_1_, ...), custom_call_target="tpu_custom_call" | custom-call | flops 68719476736 | bytes 1048576 | tf_op jit(solution)/shard_map/short_windows/pallas_call | solution.py:94
  64.3 0.3 all-to-all-done
  64.6 0.0 copy-start
  64.6 0.0 copy-start.1
  64.6 0.0 copy-start.2
  64.6 0.0 copy-start.3
  64.6 0.0 copy-start.4
  64.6 0.0 copy-start.5
  64.6 0.0 copy-start.6
  64.7 0.0 copy-start.7
  64.7 0.0 copy-start.8
  64.7 15.4 %long_windows.1 = (f32[272,256]{1,0:T(8,128)S(1)}, bf16[256,512]{1,0:T(8,128)(2,1)S(1)}, bf16[1792,128]{1,0:T(8,128)(2,1)S(1)}, bf16[2304,128]{1,0:T(8,128)(2,1)S(1)}) custom-call(bf16[4608,128]{1,0:T(8,128)(2,1)S(1)} %bitcast.31, s32[1,256]{1,0:T(1,128)} %bitcast.41, bf16[16,256]{1,0:T(8,128)(2,1)S(1)} %get-tuple-element.87.refs_2_, ...), custom_call_target="tpu_custom_call" | custom-call | flops 34359738368 | bytes 1048576 | tf_op jit(solution)/shard_map/long_windows/pallas_call | solution.py:94
  80.1 0.1 collective-permute-start.9
  80.1 1.8 %collective-permute-done.9.refs_0_ = bf16[1792,128]{1,0:T(8,128)(2,1)S(1)} collective-permute-done((bf16[1792,128]{1,0:T(8,128)(2,1)S(1)}, bf16[1792,128]{1,0:T(8,128)(2,1)S(1)}, u32[]{:S(2)}, u32[]{:S(2)}) %collective-permute-start.9) | collective-permute-done | bytes 458784 | tf_op jit(solution)/shard_map/ppermute | solution.py:937
  81.9 0.1 add_core.1
  82.0 1.7 %collective-permute-start.10 = (bf16[576,128]{1,0:T(8,128)(2,1)S(1)}, bf16[576,128]{1,0:T(8,128)(2,1)S(1)}, u32[]{:S(2)}, u32[]{:S(2)}) collective-permute-start(bf16[576,128]{1,0:T(8,128)(2,1)S(1)} %get-tuple-element.125), channel_id=1, source_target_pairs={{0,1},{1,0},{2,3},{3,2},{4,5},{5,4},{6,7},{7,6},{8,9},{9,8},{10,11... | collective-permute-start | bytes 442376 | tf_op jit(solution)/shard_map/ppermute | solution.py:935
  83.7 1.5 %collective-permute-start.11 = (bf16[576,128]{1,0:T(8,128)(2,1)S(1)}, bf16[576,128]{1,0:T(8,128)(2,1)S(1)}, u32[]{:S(2)}, u32[]{:S(2)}) collective-permute-start(bf16[576,128]{1,0:T(8,128)(2,1)S(1)} %get-tuple-element.126), channel_id=1, source_target_pairs={{0,2},{1,3},{2,0},{3,1},{4,6},{5,7},{6,4},{7,5},{8,10},{9,11},{10,... | collective-permute-start | bytes 442376 | tf_op jit(solution)/shard_map/ppermute | solution.py:935
  85.2 0.5 collective-permute-start.12
  85.7 0.0 copy-done
  85.7 0.0 copy-done.1
  85.7 0.0 copy-done.2
  85.7 0.0 copy-done.3
  85.7 0.0 copy-done.4
  85.7 0.0 copy-done.5
  85.8 0.0 copy-done.6
  85.8 0.0 copy-done.7
  85.8 0.0 copy-done.8
  85.8 2.7 %outputs.1 = (bf16[128,256]{1,0:T(8,128)(2,1)}, f32[128,256]{1,0:T(8,128)S(1)}, bf16[256,256]{1,0:T(8,128)(2,1)}, f32[256,256]{1,0:T(8,128)}, f32[8,128]{1,0:T(8,128)S(1)}) custom-call(s32[1,256]{1,0:T(1,128)S(1)} %bitcast.42, bf16[512,256]{1,0:T(8,128)(2,1)S(1)} %get-tuple-element.84.refs_5_.refs_8_.refs_1_, ...), custom_call_target="tpu_custom_call" | custom-call | flops 4294967296 | bytes 1048576 | tf_op jit(solution)/shard_map/outputs/pallas_call | solution.py:94
  88.5 0.1 collective-permute-done.10.refs_2_
  88.6 2.9 %collective-permute-done.11.refs_3_ = bf16[576,128]{1,0:T(8,128)(2,1)S(1)} collective-permute-done((bf16[576,128]{1,0:T(8,128)(2,1)S(1)}, bf16[576,128]{1,0:T(8,128)(2,1)S(1)}, u32[]{:S(2)}, u32[]{:S(2)}) %collective-permute-start.11) | collective-permute-done | bytes 147488 | tf_op jit(solution)/shard_map/ppermute | solution.py:935
  91.5 1.3 %collective-permute-done.12.refs_4_ = bf16[576,128]{1,0:T(8,128)(2,1)S(1)} collective-permute-done((bf16[576,128]{1,0:T(8,128)(2,1)S(1)}, bf16[576,128]{1,0:T(8,128)(2,1)S(1)}, u32[]{:S(2)}, u32[]{:S(2)}) %collective-permute-start.12) | collective-permute-done | bytes 147488 | tf_op jit(solution)/shard_map/ppermute | solution.py:935
  92.7 0.1 add_near.1
  92.8 3.2 %collective-permute-start.13 = (bf16[288,128]{1,0:T(8,128)(2,1)S(1)}, bf16[288,128]{1,0:T(8,128)(2,1)S(1)}, u32[]{:S(2)}, u32[]{:S(2)}) collective-permute-start(bf16[288,128]{1,0:T(8,128)(2,1)S(1)} %get-tuple-element.129), channel_id=1, source_target_pairs={{0,8},{1,9},{2,10},{3,11},{4,12},{5,13},{6,14},{7,15},{8,0},{9,1},... | collective-permute-start | bytes 221192 | tf_op jit(solution)/shard_map/ppermute | solution.py:935
  96.1 3.1 %collective-permute-done.13.refs_1_ = bf16[288,128]{1,0:T(8,128)(2,1)S(1)} collective-permute-done((bf16[288,128]{1,0:T(8,128)(2,1)S(1)}, bf16[288,128]{1,0:T(8,128)(2,1)S(1)}, u32[]{:S(2)}, u32[]{:S(2)}) %collective-permute-start.13) | collective-permute-done | bytes 73760 | tf_op jit(solution)/shard_map/ppermute | solution.py:935
  99.2 1.8 %collective-permute-start.14 = (bf16[144,128]{1,0:T(8,128)(2,1)S(1)}, bf16[144,128]{1,0:T(8,128)(2,1)S(1)}, u32[]{:S(2)}, u32[]{:S(2)}) collective-permute-start(bf16[144,128]{1,0:T(8,128)(2,1)S(1)} %get-tuple-element.131), channel_id=1, source_target_pairs={{0,4},{1,5},{2,6},{3,7},{4,0},{5,1},{6,2},{7,3},{8,12},{9,13},{10,... | collective-permute-start | bytes 110600 | tf_op jit(solution)/shard_map/ppermute | solution.py:935
  101.1 2.2 %collective-permute-done.14.refs_2_ = bf16[144,128]{1,0:T(8,128)(2,1)S(1)} collective-permute-done((bf16[144,128]{1,0:T(8,128)(2,1)S(1)}, bf16[144,128]{1,0:T(8,128)(2,1)S(1)}, u32[]{:S(2)}, u32[]{:S(2)}) %collective-permute-start.14) | collective-permute-done | bytes 36896 | tf_op jit(solution)/shard_map/ppermute | solution.py:935
  103.2 0.8 final.1
  (3 shorter events, 0.0 us)
Async XLA Ops:
  2.0 6.4 %collective-permute-start = (bf16[144,128]{1,0:T(8,128)(2,1)S(1)}, bf16[144,128]{1,0:T(8,128)(2,1)S(1)}, u32[]{:S(2)}, u32[]{:S(2)}) collective-permute-start(bf16[144,128]{1,0:T(8,128)(2,1)S(1)} %get-tuple-element.83.refs_0_), channel_id=1, source_target_pairs={{0,8},{1,9},{2,10},{3,11},{4,12},{5,13},{6,14},{7,15},{8,0},{9,1},... | collective-permute-start | bytes 110600 | tf_op jit(solution)/shard_map/ppermute | solution.py:229
  8.5 4.4 %collective-permute-start.1 = (bf16[288,128]{1,0:T(8,128)(2,1)S(1)}, bf16[288,128]{1,0:T(8,128)(2,1)S(1)}, u32[]{:S(2)}, u32[]{:S(2)}) collective-permute-start(bf16[288,128]{1,0:T(8,128)(2,1)S(1)} %join8.1.refs_0_), channel_id=1, source_target_pairs={{0,4},{1,5},{2,6},{3,7},{4,0},{5,1},{6,2},{7,3},{8,12},{9,13},{10,... | collective-permute-start | bytes 221192 | tf_op jit(solution)/shard_map/ppermute | solution.py:229
  12.8 6.7 %collective-permute-start.4 = (bf16[576,128]{1,0:T(8,128)(2,1)S(1)}, bf16[576,128]{1,0:T(8,128)(2,1)S(1)}, u32[]{:S(2)}, u32[]{:S(2)}) collective-permute-start(bf16[576,128]{1,0:T(8,128)(2,1)S(1)} %join4.1.refs_4_), channel_id=1, source_target_pairs={{0,3},{1,2},{2,1},{3,0},{4,7},{5,6},{6,5},{7,4},{8,11},{9,10},{10,... | collective-permute-start | bytes 442376 | tf_op jit(solution)/shard_map/ppermute | solution.py:229
  15.6 5.5 %collective-permute-start.3 = (bf16[576,128]{1,0:T(8,128)(2,1)S(1)}, bf16[576,128]{1,0:T(8,128)(2,1)S(1)}, u32[]{:S(2)}, u32[]{:S(2)}) collective-permute-start(bf16[576,128]{1,0:T(8,128)(2,1)S(1)} %join4.1.refs_4_), channel_id=1, source_target_pairs={{0,2},{1,3},{2,0},{3,1},{4,6},{5,7},{6,4},{7,5},{8,10},{9,11},{10,... | collective-permute-start | bytes 442376 | tf_op jit(solution)/shard_map/ppermute | solution.py:229
  16.1 5.1 %collective-permute-start.2 = (bf16[576,128]{1,0:T(8,128)(2,1)S(1)}, bf16[576,128]{1,0:T(8,128)(2,1)S(1)}, u32[]{:S(2)}, u32[]{:S(2)}) collective-permute-start(bf16[576,128]{1,0:T(8,128)(2,1)S(1)} %join4.1.refs_4_), channel_id=1, source_target_pairs={{0,1},{1,0},{2,3},{3,2},{4,5},{5,4},{6,7},{7,6},{8,9},{9,8},{10,11... | collective-permute-start | bytes 442376 | tf_op jit(solution)/shard_map/ppermute | solution.py:229
  16.4 5.2 %collective-permute-start.5 = (bf16[576,128]{1,0:T(8,128)(2,1)S(1)}, bf16[576,128]{1,0:T(8,128)(2,1)S(1)}, u32[]{:S(2)}, u32[]{:S(2)}) collective-permute-start(bf16[576,128]{1,0:T(8,128)(2,1)S(1)} %join4.1.refs_4_), channel_id=1, source_target_pairs={{0,16},{16,0},{1,17},{17,1},{2,18},{18,2},{3,19},{19,3},{4,20},{20... | collective-permute-start | bytes 442376 | tf_op jit(solution)/shard_map/ppermute | solution.py:240
  19.5 2.1 %collective-permute-start.8 = (bf16[576,128]{1,0:T(8,128)(2,1)S(1)}, bf16[576,128]{1,0:T(8,128)(2,1)S(1)}, u32[]{:S(2)}, u32[]{:S(2)}) collective-permute-start(bf16[576,128]{1,0:T(8,128)(2,1)S(1)} %collective-permute-done.4.refs_7_), channel_id=1, source_target_pairs={{0,16},{16,0},{1,17},{17,1},{2,18},{18,2},{3,19},{19,3},{4,20},{20... | collective-permute-start | bytes 442376 | tf_op jit(solution)/shard_map/ppermute | solution.py:240
  21.1 1.4 %collective-permute-start.7 = (bf16[576,128]{1,0:T(8,128)(2,1)S(1)}, bf16[576,128]{1,0:T(8,128)(2,1)S(1)}, u32[]{:S(2)}, u32[]{:S(2)}) collective-permute-start(bf16[576,128]{1,0:T(8,128)(2,1)S(1)} %collective-permute-done.3.refs_6_), channel_id=1, source_target_pairs={{0,16},{16,0},{1,17},{17,1},{2,18},{18,2},{3,19},{19,3},{4,20},{20... | collective-permute-start | bytes 442376 | tf_op jit(solution)/shard_map/ppermute | solution.py:240
  21.2 1.4 %collective-permute-start.6 = (bf16[576,128]{1,0:T(8,128)(2,1)S(1)}, bf16[576,128]{1,0:T(8,128)(2,1)S(1)}, u32[]{:S(2)}, u32[]{:S(2)}) collective-permute-start(bf16[576,128]{1,0:T(8,128)(2,1)S(1)} %collective-permute-done.2.refs_5_), channel_id=1, source_target_pairs={{0,16},{16,0},{1,17},{17,1},{2,18},{18,2},{3,19},{19,3},{4,20},{20... | collective-permute-start | bytes 442376 | tf_op jit(solution)/shard_map/ppermute | solution.py:240
  31.3 33.3 %all-to-all-start = ((bf16[16,288,128]{2,1,0:T(8,128)(2,1)}), bf16[16,288,128]{2,1,0:T(8,128)(2,1)S(1)}, u32[]{:S(2)}, u32[]{:S(2)}) async-start(bf16[16,288,128]{2,1,0:T(8,128)(2,1)} %bitcast.47), calls=%async_computation | async-start | bytes 2359296 | tf_op jit(solution)/shard_map/all_to_all | solution.py:1159
  64.6 21.1 %copy-start = (bf16[2,1,128,256]{3,2,1,0:T(8,128)(2,1)S(1)}, bf16[2,1,128,256]{3,2,1,0:T(8,128)(2,1)}, u32[]{:S(2)}) copy-start(bf16[2,1,128,256]{3,2,1,0:T(8,128)(2,1)} %param.18) | copy-start | bytes 393220
  64.6 21.1 %copy-start.1 = (bf16[2,1,128,256]{3,2,1,0:T(8,128)(2,1)S(1)}, bf16[2,1,128,256]{3,2,1,0:T(8,128)(2,1)}, u32[]{:S(2)}) copy-start(bf16[2,1,128,256]{3,2,1,0:T(8,128)(2,1)} %param.20) | copy-start | bytes 393220
  64.6 21.1 %copy-start.2 = (bf16[2,1,64,256]{3,2,1,0:T(8,128)(2,1)S(1)}, bf16[2,1,64,256]{3,2,1,0:T(8,128)(2,1)}, u32[]{:S(2)}) copy-start(bf16[2,1,64,256]{3,2,1,0:T(8,128)(2,1)} %param.17) | copy-start | bytes 196612
  64.6 21.1 %copy-start.3 = (bf16[2,1,64,256]{3,2,1,0:T(8,128)(2,1)S(1)}, bf16[2,1,64,256]{3,2,1,0:T(8,128)(2,1)}, u32[]{:S(2)}) copy-start(bf16[2,1,64,256]{3,2,1,0:T(8,128)(2,1)} %param.19) | copy-start | bytes 196612
  64.6 21.1 %copy-start.4 = (s32[256]{0:T(256)S(1)}, s32[256]{0:T(256)}, u32[]{:S(2)}) copy-start(s32[256]{0:T(256)} %param.23) | copy-start | bytes 3076
  64.6 21.1 %copy-start.5 = (s32[2,1,64]{2,1,0:T(1,128)S(1)}, s32[2,1,64]{2,1,0:T(1,128)}, u32[]{:S(2)}) copy-start(s32[2,1,64]{2,1,0:T(1,128)} %param.21) | copy-start | bytes 1540
  64.6 21.1 %copy-start.6 = (s32[2,1,128]{2,1,0:T(1,128)S(1)}, s32[2,1,128]{2,1,0:T(1,128)}, u32[]{:S(2)}) copy-start(s32[2,1,128]{2,1,0:T(1,128)} %param.22) | copy-start | bytes 3076
  64.7 21.1 %copy-start.7 = (f32[528,256]{1,0:T(8,128)S(1)}, f32[528,256]{1,0:T(8,128)}, u32[]{:S(2)}) copy-start(f32[528,256]{1,0:T(8,128)} %get-tuple-element.117.refs_12_) | copy-start | bytes 1622020
  64.7 21.1 %copy-start.8 = (bf16[512,512]{1,0:T(8,128)(2,1)S(1)}, bf16[512,512]{1,0:T(8,128)(2,1)}, u32[]{:S(2)}) copy-start(bf16[512,512]{1,0:T(8,128)(2,1)} %get-tuple-element.116.refs_11_) | copy-start | bytes 1572868
  80.1 1.9 %collective-permute-start.9 = (bf16[1792,128]{1,0:T(8,128)(2,1)S(1)}, bf16[1792,128]{1,0:T(8,128)(2,1)S(1)}, u32[]{:S(2)}, u32[]{:S(2)}) collective-permute-start(bf16[1792,128]{1,0:T(8,128)(2,1)S(1)} %get-tuple-element.121), channel_id=1, source_target_pairs={{0,16},{16,0},{1,17},{17,1},{2,18},{18,2},{3,19},{19,3},{4,20},{20... | collective-permute-start | bytes 1376264 | tf_op jit(solution)/shard_map/ppermute | solution.py:937
  82.0 6.5 %collective-permute-start.10 = (bf16[576,128]{1,0:T(8,128)(2,1)S(1)}, bf16[576,128]{1,0:T(8,128)(2,1)S(1)}, u32[]{:S(2)}, u32[]{:S(2)}) collective-permute-start(bf16[576,128]{1,0:T(8,128)(2,1)S(1)} %get-tuple-element.125), channel_id=1, source_target_pairs={{0,1},{1,0},{2,3},{3,2},{4,5},{5,4},{6,7},{7,6},{8,9},{9,8},{10,11... | collective-permute-start | bytes 442376 | tf_op jit(solution)/shard_map/ppermute | solution.py:935
  83.7 7.8 %collective-permute-start.11 = (bf16[576,128]{1,0:T(8,128)(2,1)S(1)}, bf16[576,128]{1,0:T(8,128)(2,1)S(1)}, u32[]{:S(2)}, u32[]{:S(2)}) collective-permute-start(bf16[576,128]{1,0:T(8,128)(2,1)S(1)} %get-tuple-element.126), channel_id=1, source_target_pairs={{0,2},{1,3},{2,0},{3,1},{4,6},{5,7},{6,4},{7,5},{8,10},{9,11},{10,... | collective-permute-start | bytes 442376 | tf_op jit(solution)/shard_map/ppermute | solution.py:935
  85.2 7.6 %collective-permute-start.12 = (bf16[576,128]{1,0:T(8,128)(2,1)S(1)}, bf16[576,128]{1,0:T(8,128)(2,1)S(1)}, u32[]{:S(2)}, u32[]{:S(2)}) collective-permute-start(bf16[576,128]{1,0:T(8,128)(2,1)S(1)} %get-tuple-element.127), channel_id=1, source_target_pairs={{0,3},{1,2},{2,1},{3,0},{4,7},{5,6},{6,5},{7,4},{8,11},{9,10},{10,... | collective-permute-start | bytes 442376 | tf_op jit(solution)/shard_map/ppermute | solution.py:935
  92.8 6.4 %collective-permute-start.13 = (bf16[288,128]{1,0:T(8,128)(2,1)S(1)}, bf16[288,128]{1,0:T(8,128)(2,1)S(1)}, u32[]{:S(2)}, u32[]{:S(2)}) collective-permute-start(bf16[288,128]{1,0:T(8,128)(2,1)S(1)} %get-tuple-element.129), channel_id=1, source_target_pairs={{0,8},{1,9},{2,10},{3,11},{4,12},{5,13},{6,14},{7,15},{8,0},{9,1},... | collective-permute-start | bytes 221192 | tf_op jit(solution)/shard_map/ppermute | solution.py:935
  99.2 4.0 %collective-permute-start.14 = (bf16[144,128]{1,0:T(8,128)(2,1)S(1)}, bf16[144,128]{1,0:T(8,128)(2,1)S(1)}, u32[]{:S(2)}, u32[]{:S(2)}) collective-permute-start(bf16[144,128]{1,0:T(8,128)(2,1)S(1)} %get-tuple-element.131), channel_id=1, source_target_pairs={{0,4},{1,5},{2,6},{3,7},{4,0},{5,1},{6,2},{7,3},{8,12},{9,13},{10,... | collective-permute-start | bytes 110600 | tf_op jit(solution)/shard_map/ppermute | solution.py:935

commit v5 on v4

--- a/solution.py
+++ b/solution.py
@@ -24,7 +24,7 @@
 GATHER = PACK + 2 * EDGE
 FAR = (8, 4)
 SLOTS = (0, 8, 4, 12)
-SUM_SLOTS = (0, 4, 8, 12)
+SUM_SLOTS = (0, 8, 4, 12)
 AT_DT, AT_A, AT_SMALL = 48, 64, 96
 
 
@@ -409,7 +409,7 @@
     return slice(e * LT, (e + 1) * LT)
 
 
-def scan_forward(r, T, start, full, U=16, tiles=range(E // LT)):
+def scan_forward(r, T, start, full, U=32, tiles=range(E // LT)):
     low = iota((8, LT), 0) < 4
     for e in tiles:
         es = lanes_of(e)
@@ -452,7 +452,7 @@
                 r.ends[8 * k : 8 * k + 8, es] = last[k]
 
 
-def scan_adjoint_local(r, T, U=8, tiles=range(E // LT)):
+def scan_adjoint_local(r, T, U=16, tiles=range(E // LT)):
     low = iota((8, LT), 0) < 4
     for e in tiles:
         es = lanes_of(e)
@@ -957,11 +957,11 @@
     ends = run(
         "add_far",
         add_far_body,
-        dict(low=sums["low"], got=swapped(sums["high"], 8)),
+        dict(low=sums["low"], got=swapped(sums["high"], 4)),
         dict(own=one, last=one),
         vmem=8,
     )
-    return ends["own"], swapped(ends["last"], 4)
+    return ends["own"], swapped(ends["last"], 8)
 
 
 def final_body(r, packed):

time: 104 us -> 104 us (level)
  no operation moved by 1% of the time
where the time goes in v5:
time: 104 us; the launch traced here: 103 us
  Pallas kernels  55.4 us (53%)
  starting transfers between devices  24.7 us (24%)
  waiting for transfers between devices  22.5 us (22%)
    pallas_call x11, Pallas kernels, run(): pl.pallas_call(kernel, out_shape=tuple((pin[k](*v) if pin and k in pin el...  55.4 us
    ppermute x10, waiting for transfers between devices, swapped(): return lax.ppermute(x, 'seq', [(i, i ^ mask) for i in range(count)])  19.1 us
    ppermute x10, starting transfers between devices, swapped(): return lax.ppermute(x, 'seq', [(i, i ^ mask) for i in range(count)])  18.2 us
    all_to_all x1, starting transfers between devices, local(): elements = lax.all_to_all(started['carry'], 'seq', 0, 0, tiled=True)  6.14 us
  transfers between devices with their start and end apart: 16, of which 14 were waited for; matrix products, arithmetic and copies ran while one was open for 0% of the time, Pallas kernels for 28%

profile of v5, /device:TPU:0, one launch (start us, length us, event | category | flops | bytes accessed | tf_op | source)
XLA Modules:
  0.0 103.5 jit_solution(306135004531566433)
XLA Ops:
  0.6 1.4 %pack.1 = (bf16[144,128]{1,0:T(8,128)(2,1)S(1)}, s32[1,256]{1,0:T(1,128)S(1)}, bf16[128,256]{1,0:T(8,128)(2,1)S(1)}, bf16[128,256]{1,0:T(8,128)(2,1)S(1)}, s32[2...) custom-call(f32[1,8]{1,0:T(1,128)} %bitcast.49, ...), custom_call_target="tpu_custom_call" | custom-call | bytes 1048576 | tf_op jit(solution)/shard_map/pack/pallas_call | solution.py:94
  2.0 4.1 %collective-permute-start = (bf16[144,128]{1,0:T(8,128)(2,1)S(1)}, bf16[144,128]{1,0:T(8,128)(2,1)S(1)}, u32[]{:S(2)}, u32[]{:S(2)}) collective-permute-start(bf16[144,128]{1,0:T(8,128)(2,1)S(1)} %get-tuple-element.83.refs_0_), channel_id=1, source_target_pairs={{0,8},{1,9},{2,10},{3,11},{4,12},{5,13},{6,14},{7,15},{8,0},{9,1},... | collective-permute-start | bytes 110600 | tf_op jit(solution)/shard_map/ppermute | solution.py:229
  6.1 2.3 %collective-permute-done.refs_1_ = bf16[144,128]{1,0:T(8,128)(2,1)S(1)} collective-permute-done((bf16[144,128]{1,0:T(8,128)(2,1)S(1)}, bf16[144,128]{1,0:T(8,128)(2,1)S(1)}, u32[]{:S(2)}, u32[]{:S(2)}) %collective-permute-start) | collective-permute-done | bytes 36896 | tf_op jit(solution)/shard_map/ppermute | solution.py:229
  8.5 1.5 %collective-permute-start.1 = (bf16[288,128]{1,0:T(8,128)(2,1)S(1)}, bf16[288,128]{1,0:T(8,128)(2,1)S(1)}, u32[]{:S(2)}, u32[]{:S(2)}) collective-permute-start(bf16[288,128]{1,0:T(8,128)(2,1)S(1)} %join8.1.refs_0_), channel_id=1, source_target_pairs={{0,4},{1,5},{2,6},{3,7},{4,0},{5,1},{6,2},{7,3},{8,12},{9,13},{10,... | collective-permute-start | bytes 221192 | tf_op jit(solution)/shard_map/ppermute | solution.py:229
  10.0 2.8 %collective-permute-done.1.refs_1_ = bf16[288,128]{1,0:T(8,128)(2,1)S(1)} collective-permute-done((bf16[288,128]{1,0:T(8,128)(2,1)S(1)}, bf16[288,128]{1,0:T(8,128)(2,1)S(1)}, u32[]{:S(2)}, u32[]{:S(2)}) %collective-permute-start.1) | collective-permute-done | bytes 73760 | tf_op jit(solution)/shard_map/ppermute | solution.py:229
  12.8 2.7 %collective-permute-start.4 = (bf16[576,128]{1,0:T(8,128)(2,1)S(1)}, bf16[576,128]{1,0:T(8,128)(2,1)S(1)}, u32[]{:S(2)}, u32[]{:S(2)}) collective-permute-start(bf16[576,128]{1,0:T(8,128)(2,1)S(1)} %join4.1.refs_4_), channel_id=1, source_target_pairs={{0,3},{1,2},{2,1},{3,0},{4,7},{5,6},{6,5},{7,4},{8,11},{9,10},{10,... | collective-permute-start | bytes 442376 | tf_op jit(solution)/shard_map/ppermute | solution.py:229
  15.6 0.5 collective-permute-start.3
  16.1 0.3 collective-permute-start.2
  16.4 0.0 collective-permute-start.5
  16.4 3.1 %collective-permute-done.4.refs_7_ = bf16[576,128]{1,0:T(8,128)(2,1)S(1)} collective-permute-done((bf16[576,128]{1,0:T(8,128)(2,1)S(1)}, bf16[576,128]{1,0:T(8,128)(2,1)S(1)}, u32[]{:S(2)}, u32[]{:S(2)}) %collective-permute-start.4) | collective-permute-done | bytes 147488 | tf_op jit(solution)/shard_map/ppermute | solution.py:229
  19.5 0.0 collective-permute-start.8
  19.5 1.5 %collective-permute-done.3.refs_6_ = bf16[576,128]{1,0:T(8,128)(2,1)S(1)} collective-permute-done((bf16[576,128]{1,0:T(8,128)(2,1)S(1)}, bf16[576,128]{1,0:T(8,128)(2,1)S(1)}, u32[]{:S(2)}, u32[]{:S(2)}) %collective-permute-start.3) | collective-permute-done | bytes 147488 | tf_op jit(solution)/shard_map/ppermute | solution.py:229
  21.1 0.0 collective-permute-start.7
  21.1 0.1 collective-permute-done.2.refs_5_
  21.2 0.4 collective-permute-start.6
  21.6 0.0 collective-permute-done.5.refs_8_
  21.6 0.0 collective-permute-done.8.refs_11_
  21.6 0.9 collective-permute-done.7.refs_10_
  22.4 0.2 collective-permute-done.6.refs_9_
  22.6 8.5 %long_start.1 = (bf16[4608,128]{1,0:T(8,128)(2,1)}, bf16[272,256]{1,0:T(8,128)(2,1)}, bf16[256,256]{1,0:T(8,128)(2,1)}, f32[272,512]{1,0:T(8,128)}, f32[256,512]...) custom-call(s32[1,256]{1,0:T(1,128)S(1)} %get-tuple-element.79.refs_, ...), custom_call_target="tpu_custom_call" | custom-call | flops 8589934592 | bytes 1048576 | tf_op jit(solution)/shard_map/long_start/pallas_call | solution.py:94
  31.1 6.1 %all-to-all-start = ((bf16[16,288,128]{2,1,0:T(8,128)(2,1)}), bf16[16,288,128]{2,1,0:T(8,128)(2,1)S(1)}, u32[]{:S(2)}, u32[]{:S(2)}) async-start(bf16[16,288,128]{2,1,0:T(8,128)(2,1)} %bitcast.47), calls=%async_computation | async-start | bytes 2359296 | tf_op jit(solution)/shard_map/all_to_all | solution.py:1159
  37.3 26.6 %short_windows.1 = (f32[1024,256]{1,0:T(8,128)}, f32[512,256]{1,0:T(8,128)}, f32[128,512]{1,0:T(8,128)}, f32[8,256]{1,0:T(8,128)}, f32[528,256]{1,0:T(8,128)}, /*index=5*/bf16[512,512]{1,0:T(8,128)(2,1)}) custom-call(s32[1,256]{1,0:T(1,128)S(1)} %get-tuple-element.79.refs_0_, bf16[256,256]{1,0:T(8,128)(2,1)S(1)} %get-tuple-element.106.refs_1_, ...), custom_call_target="tpu_custom_call" | custom-call | flops 68719476736 | bytes 1048576 | tf_op jit(solution)/shard_map/short_windows/pallas_call | solution.py:94
  63.9 0.5 all-to-all-done
  64.4 0.0 copy-start
  64.4 0.0 copy-start.1
  64.4 0.0 copy-start.2
  64.4 0.0 copy-start.3
  64.4 0.0 copy-start.4
  64.4 0.0 copy-start.5
  64.4 0.0 copy-start.6
  64.4 0.0 copy-start.7
  64.5 0.0 copy-start.8
  64.5 15.3 %long_windows.1 = (f32[272,256]{1,0:T(8,128)S(1)}, bf16[256,512]{1,0:T(8,128)(2,1)S(1)}, bf16[1792,128]{1,0:T(8,128)(2,1)S(1)}, bf16[2304,128]{1,0:T(8,128)(2,1)S(1)}) custom-call(bf16[4608,128]{1,0:T(8,128)(2,1)S(1)} %bitcast.31, s32[1,256]{1,0:T(1,128)} %bitcast.41, bf16[16,256]{1,0:T(8,128)(2,1)S(1)} %get-tuple-element.87.refs_2_, ...), custom_call_target="tpu_custom_call" | custom-call | flops 34359738368 | bytes 1048576 | tf_op jit(solution)/shard_map/long_windows/pallas_call | solution.py:94
  79.7 0.1 collective-permute-start.9
  79.8 1.8 %collective-permute-done.9.refs_0_ = bf16[1792,128]{1,0:T(8,128)(2,1)S(1)} collective-permute-done((bf16[1792,128]{1,0:T(8,128)(2,1)S(1)}, bf16[1792,128]{1,0:T(8,128)(2,1)S(1)}, u32[]{:S(2)}, u32[]{:S(2)}) %collective-permute-start.9) | collective-permute-done | bytes 458784 | tf_op jit(solution)/shard_map/ppermute | solution.py:937
  81.6 0.1 add_core.1
  81.7 1.5 %collective-permute-start.10 = (bf16[576,128]{1,0:T(8,128)(2,1)S(1)}, bf16[576,128]{1,0:T(8,128)(2,1)S(1)}, u32[]{:S(2)}, u32[]{:S(2)}) collective-permute-start(bf16[576,128]{1,0:T(8,128)(2,1)S(1)} %get-tuple-element.125), channel_id=1, source_target_pairs={{0,1},{1,0},{2,3},{3,2},{4,5},{5,4},{6,7},{7,6},{8,9},{9,8},{10,11... | collective-permute-start | bytes 442376 | tf_op jit(solution)/shard_map/ppermute | solution.py:935
  83.2 1.6 %collective-permute-start.11 = (bf16[576,128]{1,0:T(8,128)(2,1)S(1)}, bf16[576,128]{1,0:T(8,128)(2,1)S(1)}, u32[]{:S(2)}, u32[]{:S(2)}) collective-permute-start(bf16[576,128]{1,0:T(8,128)(2,1)S(1)} %get-tuple-element.126), channel_id=1, source_target_pairs={{0,2},{1,3},{2,0},{3,1},{4,6},{5,7},{6,4},{7,5},{8,10},{9,11},{10,... | collective-permute-start | bytes 442376 | tf_op jit(solution)/shard_map/ppermute | solution.py:935
  84.8 0.6 collective-permute-start.12
  85.4 0.0 copy-done
  85.4 0.0 copy-done.1
  85.4 0.0 copy-done.2
  85.4 0.0 copy-done.3
  85.4 0.0 copy-done.4
  85.4 0.0 copy-done.5
  85.5 0.0 copy-done.6
  85.5 0.0 copy-done.7
  85.5 0.0 copy-done.8
  85.5 2.7 %outputs.1 = (bf16[128,256]{1,0:T(8,128)(2,1)}, f32[128,256]{1,0:T(8,128)S(1)}, bf16[256,256]{1,0:T(8,128)(2,1)}, f32[256,256]{1,0:T(8,128)}, f32[8,128]{1,0:T(8,128)S(1)}) custom-call(s32[1,256]{1,0:T(1,128)S(1)} %bitcast.42, bf16[512,256]{1,0:T(8,128)(2,1)S(1)} %get-tuple-element.84.refs_5_.refs_8_.refs_1_, ...), custom_call_target="tpu_custom_call" | custom-call | flops 4294967296 | bytes 1048576 | tf_op jit(solution)/shard_map/outputs/pallas_call | solution.py:94
  88.2 0.3 collective-permute-done.10.refs_2_
  88.5 2.6 %collective-permute-done.11.refs_3_ = bf16[576,128]{1,0:T(8,128)(2,1)S(1)} collective-permute-done((bf16[576,128]{1,0:T(8,128)(2,1)S(1)}, bf16[576,128]{1,0:T(8,128)(2,1)S(1)}, u32[]{:S(2)}, u32[]{:S(2)}) %collective-permute-start.11) | collective-permute-done | bytes 147488 | tf_op jit(solution)/shard_map/ppermute | solution.py:935
  91.1 1.3 %collective-permute-done.12.refs_4_ = bf16[576,128]{1,0:T(8,128)(2,1)S(1)} collective-permute-done((bf16[576,128]{1,0:T(8,128)(2,1)S(1)}, bf16[576,128]{1,0:T(8,128)(2,1)S(1)}, u32[]{:S(2)}, u32[]{:S(2)}) %collective-permute-start.12) | collective-permute-done | bytes 147488 | tf_op jit(solution)/shard_map/ppermute | solution.py:935
  92.4 0.1 add_near.1
  92.5 2.9 %collective-permute-start.13 = (bf16[288,128]{1,0:T(8,128)(2,1)S(1)}, bf16[288,128]{1,0:T(8,128)(2,1)S(1)}, u32[]{:S(2)}, u32[]{:S(2)}) collective-permute-start(bf16[288,128]{1,0:T(8,128)(2,1)S(1)} %get-tuple-element.129), channel_id=1, source_target_pairs={{0,4},{1,5},{2,6},{3,7},{4,0},{5,1},{6,2},{7,3},{8,12},{9,13},{10,... | collective-permute-start | bytes 221192 | tf_op jit(solution)/shard_map/ppermute | solution.py:935
  95.4 2.3 %collective-permute-done.13.refs_1_ = bf16[288,128]{1,0:T(8,128)(2,1)S(1)} collective-permute-done((bf16[288,128]{1,0:T(8,128)(2,1)S(1)}, bf16[288,128]{1,0:T(8,128)(2,1)S(1)}, u32[]{:S(2)}, u32[]{:S(2)}) %collective-permute-start.13) | collective-permute-done | bytes 73760 | tf_op jit(solution)/shard_map/ppermute | solution.py:935
  97.8 2.4 %collective-permute-start.14 = (bf16[144,128]{1,0:T(8,128)(2,1)S(1)}, bf16[144,128]{1,0:T(8,128)(2,1)S(1)}, u32[]{:S(2)}, u32[]{:S(2)}) collective-permute-start(bf16[144,128]{1,0:T(8,128)(2,1)S(1)} %get-tuple-element.131), channel_id=1, source_target_pairs={{0,8},{1,9},{2,10},{3,11},{4,12},{5,13},{6,14},{7,15},{8,0},{9,1},... | collective-permute-start | bytes 110600 | tf_op jit(solution)/shard_map/ppermute | solution.py:935
  100.2 2.5 %collective-permute-done.14.refs_2_ = bf16[144,128]{1,0:T(8,128)(2,1)S(1)} collective-permute-done((bf16[144,128]{1,0:T(8,128)(2,1)S(1)}, bf16[144,128]{1,0:T(8,128)(2,1)S(1)}, u32[]{:S(2)}, u32[]{:S(2)}) %collective-permute-start.14) | collective-permute-done | bytes 36896 | tf_op jit(solution)/shard_map/ppermute | solution.py:935
  102.7 0.8 final.1
  (3 shorter events, 0.0 us)
Async XLA Ops:
  2.0 6.4 %collective-permute-start = (bf16[144,128]{1,0:T(8,128)(2,1)S(1)}, bf16[144,128]{1,0:T(8,128)(2,1)S(1)}, u32[]{:S(2)}, u32[]{:S(2)}) collective-permute-start(bf16[144,128]{1,0:T(8,128)(2,1)S(1)} %get-tuple-element.83.refs_0_), channel_id=1, source_target_pairs={{0,8},{1,9},{2,10},{3,11},{4,12},{5,13},{6,14},{7,15},{8,0},{9,1},... | collective-permute-start | bytes 110600 | tf_op jit(solution)/shard_map/ppermute | solution.py:229
  8.5 4.4 %collective-permute-start.1 = (bf16[288,128]{1,0:T(8,128)(2,1)S(1)}, bf16[288,128]{1,0:T(8,128)(2,1)S(1)}, u32[]{:S(2)}, u32[]{:S(2)}) collective-permute-start(bf16[288,128]{1,0:T(8,128)(2,1)S(1)} %join8.1.refs_0_), channel_id=1, source_target_pairs={{0,4},{1,5},{2,6},{3,7},{4,0},{5,1},{6,2},{7,3},{8,12},{9,13},{10,... | collective-permute-start | bytes 221192 | tf_op jit(solution)/shard_map/ppermute | solution.py:229
  12.8 6.7 %collective-permute-start.4 = (bf16[576,128]{1,0:T(8,128)(2,1)S(1)}, bf16[576,128]{1,0:T(8,128)(2,1)S(1)}, u32[]{:S(2)}, u32[]{:S(2)}) collective-permute-start(bf16[576,128]{1,0:T(8,128)(2,1)S(1)} %join4.1.refs_4_), channel_id=1, source_target_pairs={{0,3},{1,2},{2,1},{3,0},{4,7},{5,6},{6,5},{7,4},{8,11},{9,10},{10,... | collective-permute-start | bytes 442376 | tf_op jit(solution)/shard_map/ppermute | solution.py:229
  15.6 5.5 %collective-permute-start.3 = (bf16[576,128]{1,0:T(8,128)(2,1)S(1)}, bf16[576,128]{1,0:T(8,128)(2,1)S(1)}, u32[]{:S(2)}, u32[]{:S(2)}) collective-permute-start(bf16[576,128]{1,0:T(8,128)(2,1)S(1)} %join4.1.refs_4_), channel_id=1, source_target_pairs={{0,2},{1,3},{2,0},{3,1},{4,6},{5,7},{6,4},{7,5},{8,10},{9,11},{10,... | collective-permute-start | bytes 442376 | tf_op jit(solution)/shard_map/ppermute | solution.py:229
  16.1 5.1 %collective-permute-start.2 = (bf16[576,128]{1,0:T(8,128)(2,1)S(1)}, bf16[576,128]{1,0:T(8,128)(2,1)S(1)}, u32[]{:S(2)}, u32[]{:S(2)}) collective-permute-start(bf16[576,128]{1,0:T(8,128)(2,1)S(1)} %join4.1.refs_4_), channel_id=1, source_target_pairs={{0,1},{1,0},{2,3},{3,2},{4,5},{5,4},{6,7},{7,6},{8,9},{9,8},{10,11... | collective-permute-start | bytes 442376 | tf_op jit(solution)/shard_map/ppermute | solution.py:229
  16.4 5.2 %collective-permute-start.5 = (bf16[576,128]{1,0:T(8,128)(2,1)S(1)}, bf16[576,128]{1,0:T(8,128)(2,1)S(1)}, u32[]{:S(2)}, u32[]{:S(2)}) collective-permute-start(bf16[576,128]{1,0:T(8,128)(2,1)S(1)} %join4.1.refs_4_), channel_id=1, source_target_pairs={{0,16},{16,0},{1,17},{17,1},{2,18},{18,2},{3,19},{19,3},{4,20},{20... | collective-permute-start | bytes 442376 | tf_op jit(solution)/shard_map/ppermute | solution.py:240
  19.5 2.1 %collective-permute-start.8 = (bf16[576,128]{1,0:T(8,128)(2,1)S(1)}, bf16[576,128]{1,0:T(8,128)(2,1)S(1)}, u32[]{:S(2)}, u32[]{:S(2)}) collective-permute-start(bf16[576,128]{1,0:T(8,128)(2,1)S(1)} %collective-permute-done.4.refs_7_), channel_id=1, source_target_pairs={{0,16},{16,0},{1,17},{17,1},{2,18},{18,2},{3,19},{19,3},{4,20},{20... | collective-permute-start | bytes 442376 | tf_op jit(solution)/shard_map/ppermute | solution.py:240
  21.1 1.4 %collective-permute-start.7 = (bf16[576,128]{1,0:T(8,128)(2,1)S(1)}, bf16[576,128]{1,0:T(8,128)(2,1)S(1)}, u32[]{:S(2)}, u32[]{:S(2)}) collective-permute-start(bf16[576,128]{1,0:T(8,128)(2,1)S(1)} %collective-permute-done.3.refs_6_), channel_id=1, source_target_pairs={{0,16},{16,0},{1,17},{17,1},{2,18},{18,2},{3,19},{19,3},{4,20},{20... | collective-permute-start | bytes 442376 | tf_op jit(solution)/shard_map/ppermute | solution.py:240
  21.2 1.4 %collective-permute-start.6 = (bf16[576,128]{1,0:T(8,128)(2,1)S(1)}, bf16[576,128]{1,0:T(8,128)(2,1)S(1)}, u32[]{:S(2)}, u32[]{:S(2)}) collective-permute-start(bf16[576,128]{1,0:T(8,128)(2,1)S(1)} %collective-permute-done.2.refs_5_), channel_id=1, source_target_pairs={{0,16},{16,0},{1,17},{17,1},{2,18},{18,2},{3,19},{19,3},{4,20},{20... | collective-permute-start | bytes 442376 | tf_op jit(solution)/shard_map/ppermute | solution.py:240
  31.1 33.3 %all-to-all-start = ((bf16[16,288,128]{2,1,0:T(8,128)(2,1)}), bf16[16,288,128]{2,1,0:T(8,128)(2,1)S(1)}, u32[]{:S(2)}, u32[]{:S(2)}) async-start(bf16[16,288,128]{2,1,0:T(8,128)(2,1)} %bitcast.47), calls=%async_computation | async-start | bytes 2359296 | tf_op jit(solution)/shard_map/all_to_all | solution.py:1159
  64.4 21.0 %copy-start = (bf16[2,1,128,256]{3,2,1,0:T(8,128)(2,1)S(1)}, bf16[2,1,128,256]{3,2,1,0:T(8,128)(2,1)}, u32[]{:S(2)}) copy-start(bf16[2,1,128,256]{3,2,1,0:T(8,128)(2,1)} %param.18) | copy-start | bytes 393220
  64.4 21.0 %copy-start.1 = (bf16[2,1,128,256]{3,2,1,0:T(8,128)(2,1)S(1)}, bf16[2,1,128,256]{3,2,1,0:T(8,128)(2,1)}, u32[]{:S(2)}) copy-start(bf16[2,1,128,256]{3,2,1,0:T(8,128)(2,1)} %param.20) | copy-start | bytes 393220
  64.4 21.0 %copy-start.2 = (bf16[2,1,64,256]{3,2,1,0:T(8,128)(2,1)S(1)}, bf16[2,1,64,256]{3,2,1,0:T(8,128)(2,1)}, u32[]{:S(2)}) copy-start(bf16[2,1,64,256]{3,2,1,0:T(8,128)(2,1)} %param.17) | copy-start | bytes 196612
  64.4 21.0 %copy-start.3 = (bf16[2,1,64,256]{3,2,1,0:T(8,128)(2,1)S(1)}, bf16[2,1,64,256]{3,2,1,0:T(8,128)(2,1)}, u32[]{:S(2)}) copy-start(bf16[2,1,64,256]{3,2,1,0:T(8,128)(2,1)} %param.19) | copy-start | bytes 196612
  64.4 21.0 %copy-start.4 = (s32[256]{0:T(256)S(1)}, s32[256]{0:T(256)}, u32[]{:S(2)}) copy-start(s32[256]{0:T(256)} %param.23) | copy-start | bytes 3076
  64.4 21.0 %copy-start.5 = (s32[2,1,64]{2,1,0:T(1,128)S(1)}, s32[2,1,64]{2,1,0:T(1,128)}, u32[]{:S(2)}) copy-start(s32[2,1,64]{2,1,0:T(1,128)} %param.21) | copy-start | bytes 1540
  64.4 21.0 %copy-start.6 = (s32[2,1,128]{2,1,0:T(1,128)S(1)}, s32[2,1,128]{2,1,0:T(1,128)}, u32[]{:S(2)}) copy-start(s32[2,1,128]{2,1,0:T(1,128)} %param.22) | copy-start | bytes 3076
  64.4 21.0 %copy-start.7 = (f32[528,256]{1,0:T(8,128)S(1)}, f32[528,256]{1,0:T(8,128)}, u32[]{:S(2)}) copy-start(f32[528,256]{1,0:T(8,128)} %get-tuple-element.117.refs_12_) | copy-start | bytes 1622020
  64.5 21.0 %copy-start.8 = (bf16[512,512]{1,0:T(8,128)(2,1)S(1)}, bf16[512,512]{1,0:T(8,128)(2,1)}, u32[]{:S(2)}) copy-start(bf16[512,512]{1,0:T(8,128)(2,1)} %get-tuple-element.116.refs_11_) | copy-start | bytes 1572868
  79.7 1.9 %collective-permute-start.9 = (bf16[1792,128]{1,0:T(8,128)(2,1)S(1)}, bf16[1792,128]{1,0:T(8,128)(2,1)S(1)}, u32[]{:S(2)}, u32[]{:S(2)}) collective-permute-start(bf16[1792,128]{1,0:T(8,128)(2,1)S(1)} %get-tuple-element.121), channel_id=1, source_target_pairs={{0,16},{16,0},{1,17},{17,1},{2,18},{18,2},{3,19},{19,3},{4,20},{20... | collective-permute-start | bytes 1376264 | tf_op jit(solution)/shard_map/ppermute | solution.py:937
  81.7 6.8 %collective-permute-start.10 = (bf16[576,128]{1,0:T(8,128)(2,1)S(1)}, bf16[576,128]{1,0:T(8,128)(2,1)S(1)}, u32[]{:S(2)}, u32[]{:S(2)}) collective-permute-start(bf16[576,128]{1,0:T(8,128)(2,1)S(1)} %get-tuple-element.125), channel_id=1, source_target_pairs={{0,1},{1,0},{2,3},{3,2},{4,5},{5,4},{6,7},{7,6},{8,9},{9,8},{10,11... | collective-permute-start | bytes 442376 | tf_op jit(solution)/shard_map/ppermute | solution.py:935
  83.2 7.9 %collective-permute-start.11 = (bf16[576,128]{1,0:T(8,128)(2,1)S(1)}, bf16[576,128]{1,0:T(8,128)(2,1)S(1)}, u32[]{:S(2)}, u32[]{:S(2)}) collective-permute-start(bf16[576,128]{1,0:T(8,128)(2,1)S(1)} %get-tuple-element.126), channel_id=1, source_target_pairs={{0,2},{1,3},{2,0},{3,1},{4,6},{5,7},{6,4},{7,5},{8,10},{9,11},{10,... | collective-permute-start | bytes 442376 | tf_op jit(solution)/shard_map/ppermute | solution.py:935
  84.8 7.6 %collective-permute-start.12 = (bf16[576,128]{1,0:T(8,128)(2,1)S(1)}, bf16[576,128]{1,0:T(8,128)(2,1)S(1)}, u32[]{:S(2)}, u32[]{:S(2)}) collective-permute-start(bf16[576,128]{1,0:T(8,128)(2,1)S(1)} %get-tuple-element.127), channel_id=1, source_target_pairs={{0,3},{1,2},{2,1},{3,0},{4,7},{5,6},{6,5},{7,4},{8,11},{9,10},{10,... | collective-permute-start | bytes 442376 | tf_op jit(solution)/shard_map/ppermute | solution.py:935
  92.5 5.2 %collective-permute-start.13 = (bf16[288,128]{1,0:T(8,128)(2,1)S(1)}, bf16[288,128]{1,0:T(8,128)(2,1)S(1)}, u32[]{:S(2)}, u32[]{:S(2)}) collective-permute-start(bf16[288,128]{1,0:T(8,128)(2,1)S(1)} %get-tuple-element.129), channel_id=1, source_target_pairs={{0,4},{1,5},{2,6},{3,7},{4,0},{5,1},{6,2},{7,3},{8,12},{9,13},{10,... | collective-permute-start | bytes 221192 | tf_op jit(solution)/shard_map/ppermute | solution.py:935
  97.8 4.9 %collective-permute-start.14 = (bf16[144,128]{1,0:T(8,128)(2,1)S(1)}, bf16[144,128]{1,0:T(8,128)(2,1)S(1)}, u32[]{:S(2)}, u32[]{:S(2)}) collective-permute-start(bf16[144,128]{1,0:T(8,128)(2,1)S(1)} %get-tuple-element.131), channel_id=1, source_target_pairs={{0,8},{1,9},{2,10},{3,11},{4,12},{5,13},{6,14},{7,15},{8,0},{9,1},... | collective-permute-start | bytes 110600 | tf_op jit(solution)/shard_map/ppermute | solution.py:935
